TPU v7x, 32 devices: a whole 2x2x4 slice. The times are simulated.
32 devices in a mesh: req: 8 (over z, y), tp: 4 (over x, core).
Axes of the slice: x: 2, y: 2, z: 4, core: 2. Of those that a mesh axis runs over, the one named last changes fastest.
Arguments:
- hidden: bfloat16 [64, 4096], P('req'), may hold values from -512 to 512
- norm_gain: bfloat16 [4096], replicated, may hold values from 1 to 3
- lm_head: bfloat16 [4096, 8192], P(None, ('req', 'tp'))
- targets: int32 [64], P('req'), may hold values from 0 to 8191
- segments: int32 [64], P('req'), may hold values from 0 to 3, never falling along the last dimension, each value on 1 to 32 neighbouring positions
- scored: int32 [64], P('req'), may hold values from 0 to 1, as said below
Outputs:
- token_logprob: float32 [64], P('req')
- token_entropy: float32 [64], P('req')
- seq_logprob: float32 [4], replicated
Inputs may be any that keep to these rules, and one draw needn't show every extreme that they name: At most 4 of the 8 rows of one index of req are scored, and exactly 4 on some index in every draw.
All inputs are finite; a program needn't handle non-finite values.
Results may differ from a plain program's by a relative error of at most 0.0061.
Values may be sent and summed in bfloat16 or wider, within the bound.
No kernel may reach another device: no remote copies, remote signals or barrier semaphores. Data moves between devices by JAX's collectives and lax.ppermute only.
A program may use at most 64 MiB of HBM per device.

v0:
```python
import jax
import jax.numpy as jnp
from jax import lax
from jax.sharding import PartitionSpec as P

SEQS = 4


def combined_all(value, axis, join):
    pieces = jax.tree.map(lambda part: lax.all_gather(part, axis), value)
    head = jax.tree.map(lambda part: part[0], pieces)
    tail = jax.tree.map(lambda part: part[1:], pieces)
    so_far, _ = lax.scan(lambda so_far, piece: (join(so_far, piece), None), head, tail)
    return so_far


def combine_stats(earlier, latter):
    row_top = jnp.maximum(earlier[0], latter[0])
    early_scale = jnp.exp(earlier[0] - row_top)
    late_scale = jnp.exp(latter[0] - row_top)
    return (
        row_top,
        earlier[1] * early_scale + latter[1] * late_scale,
        earlier[2] * early_scale + latter[2] * late_scale,
        earlier[3] + latter[3],
    )


def local(hidden, norm_gain, lm_head, targets, segments, scored):
    col_width = lm_head.shape[1]
    tp_count = lax.axis_size("tp")
    own_index = lax.axis_index("req")
    first_col = (own_index * tp_count + lax.axis_index("tp")) * col_width
    values = hidden.astype(jnp.float32)
    row_scale = lax.rsqrt(jnp.mean(values * values, axis=1, keepdims=True) + 1e-05)
    normed = (values * row_scale * norm_gain.astype(jnp.float32)[None, :]).astype(jnp.bfloat16)
    row_flags = scored.astype(jnp.float32)
    slot_count = normed.shape[0]
    columns = first_col + jnp.arange(col_width, dtype=jnp.int32)
    piece_rows, piece_ids = lax.all_gather((normed, targets), "req", axis=0, tiled=True)
    logits = jnp.dot(piece_rows, lm_head, preferred_element_type=jnp.float32)
    row_top = jnp.max(logits, axis=1)
    scaled = jnp.exp(logits - row_top[:, None])
    row_total = jnp.sum(scaled, axis=1)
    row_weighted = jnp.sum(scaled * logits, axis=1)
    picked = jnp.sum(jnp.where(columns[None, :] == piece_ids[:, None], logits, 0.0), axis=1)
    stacked = jnp.stack([row_top, row_total, row_weighted, picked], axis=0)
    row_stats = (stacked[0], stacked[1], stacked[2], stacked[3])
    full_stats = combined_all(row_stats, ("req", "tp"), combine_stats)
    merged = tuple(
        (
            lax.dynamic_slice_in_dim(member, own_index * slot_count, slot_count, 0)
            for member in full_stats
        )
    )
    log_norm = merged[0] + jnp.log(merged[1])
    slot_logprob = merged[3] - log_norm
    slot_entropy = log_norm - merged[2] / merged[1]
    token_logprob = row_flags * slot_logprob
    token_entropy = row_flags * slot_entropy
    seq_ids = jnp.arange(SEQS, dtype=jnp.int32)
    partial_sums = jnp.sum(
        jnp.where(segments[None, :] == seq_ids[:, None], token_logprob[None, :], 0.0), axis=1
    )
    seq_logprob = lax.psum(partial_sums, "req")
    return (token_logprob, token_entropy, seq_logprob)


def solution(mesh):
    return jax.shard_map(
        local,
        mesh=mesh,
        in_specs=(P("req", None), P(), P(None, ("req", "tp")), P("req"), P("req"), P("req")),
        out_specs=(P("req"), P("req"), P()),
        check_vma=False,
    )
```

profile of v0, /device:TPU:0, one launch (start us, length us, event | category | flops | bytes accessed | tf_op | source)
XLA Modules:
  0.0 115.5 jit_solution(9952803254516292559)
XLA Ops:
  0.7 1.4 %dynamic-slice = u32[1]{0:T(128)} dynamic-slice(u32[32]{0:T(128)} %constant.52, u32[]{:T(128)S(6)} %add.50), dynamic_slice_sizes={1} | dynamic-slice | bytes 12
  2.7 0.9 dynamic-update-slice.3
  3.6 13.1 %all-reduce.3 = s32[64]{0:T(128)S(1)} all-reduce(s32[64]{0:T(128)S(1)} %dynamic-update-slice.3), channel_id=1, replica_groups=mesh['req'=8,'tp'=4] {'req'}, use_global_device_ids=true, to_apply=%add.3 | all-reduce | flops 64 | bytes 512
  16.6 0.7 convert_element_type.14
  17.3 1.0 fusion.10
  18.3 0.9 fusion.12
  19.3 31.6 %all_gather.18 = bf16[64,4096]{1,0:T(8,128)(2,1)S(1)} all-gather(bf16[8,4096]{1,0:T(8,128)(2,1)S(1)} %fusion.12), channel_id=1, replica_groups=mesh['req'=8,'tp'=4] {'req'}, dimensions={0}, use_global_device_ids=true | all-gather | bytes 589824 | tf_op jit(solution)/shard_map/all_gather | solution.py:40
  50.9 0.6 fusion.15
  51.4 0.2 multiply_reduce_fusion
  51.7 0.3 dynamic-update-slice.2
  51.9 0.3 dynamic-update-slice.4
  52.2 0.3 dynamic-update-slice.1
  52.5 0.3 dynamic-update-slice
  52.7 37.3 %all-reduce.5 = (f32[2048]{0:T(1024)S(1)}, f32[2048]{0:T(1024)S(1)}, f32[2048]{0:T(1024)S(1)}, f32[2048]{0:T(1024)S(1)}) all-reduce(f32[2048]{0:T(1024)S(1)} %dynamic-update-slice, f32[2048]{0:T(1024)S(1)} %dynamic-update-slice.1, f32[2048]{0:T(1024)S(1)} %dynamic-update-slice.2, ...), channel_id=2, replica_groups=mesh['req'=8,'tp'=4] {'req','tp'}, use_global_device_ids=true, to_apply=%add | all-reduce | flops 8192 | bytes 65536
  90.0 0.1 slice.44
  90.1 0.1 reshape.35
  90.2 0.1 reshape.36
  90.3 0.1 slice.46
  90.4 0.1 reshape.37
  90.5 0.1 reshape.38
  90.6 2.5 %while.16 = (s32[]{:T(128)}, f32[64]{0:T(128)S(1)}, f32[64]{0:T(128)S(1)}, f32[64]{0:T(128)S(1)}, f32[64]{0:T(128)S(1)}, /*index=5*/f32[31,64]{1,0:T(8,128)S(1)}...) while((s32[]{:T(128)}, f32[64]{0:T(128)S(1)}, f32[64]{0:T(128)S(1)}, ...), condition=%wide.region_6.7_spmd, body=%wide.region_5.6_spmd.sunk | while | flops 770 | bytes 4461 | solution.py:13
  93.1 0.6 subtract_multiply_fusion
  93.7 0.1 select_reduce_fusion.1
  93.8 21.6 %psum.7 = f32[4]{0:T(128)} all-reduce(f32[4]{0:T(128)S(1)} %select_reduce_fusion.1), channel_id=1, replica_groups=mesh['req'=8,'tp'=4] {'req'}, use_global_device_ids=true, to_apply=%region_8.9 | all-reduce | flops 4 | bytes 32 | tf_op jit(solution)/shard_map/psum | solution.py:65
  (114 shorter events, 2.0 us)
Async XLA Ops:
  0.6 50.2 %copy-start = (bf16[4096,256]{1,0:T(8,128)(2,1)S(1)}, bf16[4096,256]{1,0:T(8,128)(2,1)}, u32[]{:S(2)}) copy-start(bf16[4096,256]{1,0:T(8,128)(2,1)} %param.10) | copy-start | bytes 6291460
  0.6 92.5 %copy-start.1 = (s32[8]{0:T(128)S(1)}, s32[8]{0:T(128)}, u32[]{:S(2)}) copy-start(s32[8]{0:T(128)} %param.13) | copy-start | bytes 100
  0.7 93.1 %copy-start.3 = (s32[8]{0:T(128)S(1)}, s32[8]{0:T(128)}, u32[]{:S(2)}) copy-start(s32[8]{0:T(128)} %param.12) | copy-start | bytes 100
  93.7 21.7 %copy-start.2 = (f32[8]{0:T(128)}, f32[8]{0:T(128)S(1)}, u32[]{:S(2)}) copy-start(f32[8]{0:T(128)S(1)} %get-tuple-element.87) | copy-start | bytes 100
where the time goes:
time: 116 us; the launch traced here: 115 us
  blocking collectives  104 us (90%)
  other arithmetic  5.32 us (5%)
  local copies, waits for them, and re-layouts  3.96 us (3%)
  between operations  1.4 us (1%)
    unnamed x2, blocking collectives  50.3 us
    all_gather x1, blocking collectives, local(): lax.all_gather((normed, targets), 'req', axis=0, tiled=True)  31.6 us
    psum x1, blocking collectives, local(): seq_logprob = lax.psum(partial_sums, 'req')  21.6 us
    unnamed x19, local copies, waits for them, and re-layouts  3.32 us

commit v1 on v0

v1 whole, which is shorter than its diff:
```python
import functools

import jax
import jax.numpy as jnp
from jax import lax
from jax.experimental import pallas as pl
from jax.experimental.pallas import tpu as pltpu
from jax.sharding import PartitionSpec as P

SEQS = 4
PICK = 4
LANES = 128
STATS = 4

VMEM = pltpu.VMEM
SMEM = pltpu.SMEM


def ranks_of(scored_ref, row_count):
    ranks, so_far = [], jnp.int32(0)
    for row in range(row_count):
        ranks.append(so_far)
        so_far = so_far + scored_ref[row]
    return ranks, so_far


def pack_kernel(hidden_ref, gain_ref, targets_ref, segments_ref, scored_ref, out_ref, wide_ref, halves_ref):
    row_count, width = hidden_ref.shape
    half = width // 2
    wide_ref[...] = hidden_ref[...].astype(jnp.float32)
    ranks, count = ranks_of(scored_ref, row_count)
    source = [jnp.int32(0)] * PICK
    for row in range(row_count):
        for r in range(PICK):
            hit = jnp.logical_and(scored_ref[row] == 1, ranks[row] == r)
            source[r] = jnp.where(hit, row, source[r])
    for r in range(PICK):
        halves_ref[r : r + 1, :] = wide_ref[pl.ds(source[r], 1), :half]
        halves_ref[PICK + r : PICK + r + 1, :] = wide_ref[pl.ds(source[r], 1), half:]
    values = halves_ref[...]
    part = jnp.sum(values * values, axis=1, keepdims=True)
    part = jnp.broadcast_to(part, (2 * PICK, LANES))
    total = (part + pltpu.roll(part, PICK, 0))[:, :1]
    row_scale = lax.rsqrt(total / width + 1e-05)
    upper = lax.broadcasted_iota(jnp.int32, (2 * PICK, 1), 0) < PICK
    gain = jnp.where(upper, gain_ref[:, :half].astype(jnp.float32), gain_ref[:, half:].astype(jnp.float32))
    out_ref[:, :half] = (values * row_scale * gain).astype(jnp.bfloat16)
    sub = lax.broadcasted_iota(jnp.int32, (2 * PICK, LANES), 0)
    sub = jnp.where(sub >= PICK, sub - PICK, sub)
    lane = lax.broadcasted_iota(jnp.int32, (2 * PICK, LANES), 1)
    side = jnp.zeros((2 * PICK, LANES), jnp.int32)
    for r in range(PICK):
        target = targets_ref[source[r]]
        fields = (target % 256, (target // 256) % 256, target // 65536, segments_ref[source[r]], (count > r).astype(jnp.int32))
        line = jnp.zeros((2 * PICK, LANES), jnp.int32)
        for at, field in enumerate(fields):
            line = jnp.where(lane == at, field, line)
        side = jnp.where(sub == r, line, side)
    out_ref[:, half:] = side.astype(jnp.float32).astype(jnp.bfloat16)


def score_kernel(place_ref, rows_ref, head_ref, stats_ref, meta_ref):
    width, cols = head_ref.shape
    half = width // 2
    groups = rows_ref.shape[0] // (2 * PICK)
    used = groups * PICK
    rows = rows_ref[:, :half]
    early = jnp.dot(rows, head_ref[:half, :], preferred_element_type=jnp.float32)
    late = jnp.dot(rows, head_ref[half:, :], preferred_element_type=jnp.float32)
    early = early.reshape(groups // 2, 2, 2 * PICK, cols)
    late = late.reshape(groups // 2, 2, 2 * PICK, cols)
    upper = lax.broadcasted_iota(jnp.int32, (1, 2 * PICK, 1), 1) < PICK

    def swap(block):
        flat = block.reshape(groups // 2 * 2 * PICK, block.shape[-1])
        return jnp.concatenate(
            [pltpu.roll(flat[i * 2 * PICK : (i + 1) * 2 * PICK], PICK, 0) for i in range(groups // 2)], axis=0
        ).reshape(block.shape)

    logits = jnp.where(upper, early[:, 0] + swap(late[:, 0]), swap(early[:, 1]) + late[:, 1])
    logits = logits.reshape(used, cols)
    side = rows_ref[:, half:].astype(jnp.float32).reshape(groups // 2, 2, 2 * PICK, LANES)
    side = jnp.where(upper, side[:, 0], side[:, 1]).reshape(used, LANES)
    copies = max(1, LANES // used)
    if copies > 1:
        logits = jnp.concatenate([logits] * copies, axis=0)
        side = jnp.concatenate([side] * copies, axis=0)
    logits = logits.T
    side = side.T
    ids = (side[0:1] + 256.0 * side[1:2] + 65536.0 * side[2:3]).astype(jnp.int32)
    row_top = jnp.max(logits, axis=0, keepdims=True)
    scaled = jnp.exp(logits - row_top)
    row_total = jnp.sum(scaled, axis=0, keepdims=True)
    row_weighted = jnp.sum(scaled * logits, axis=0, keepdims=True)
    columns = place_ref[0] * cols + lax.broadcasted_iota(jnp.int32, logits.shape, 0)
    picked = jnp.sum(jnp.where(columns == ids, logits, 0.0), axis=0, keepdims=True)
    stats = (row_top, row_total, row_weighted, picked)
    if copies > 1:
        lane = lax.broadcasted_iota(jnp.int32, (1, LANES), 1)
        joined = picked
        for at in range(STATS - 1):
            joined = jnp.where(lane // used == at, stats[at], joined)
        stats_ref[...] = joined
    else:
        for at in range(STATS):
            stats_ref[:, at * used : (at + 1) * used] = stats[at]
    meta_ref[...] = side[0:8, :]


def finish_kernel(used, place_ref, scored_ref, stats_ref, meta_ref, logprob_ref, entropy_ref, seq_ref):
    row_count = scored_ref.shape[0]
    lanes = max(used, LANES)

    def stat(at):
        if used >= LANES:
            return stats_ref[:, at * used : (at + 1) * used]
        return stats_ref[...] if at == 0 else pltpu.roll(stats_ref[...], LANES - at * used, 1)

    tops = stat(0)
    row_top = jnp.max(tops, axis=0, keepdims=True)
    weight = jnp.exp(tops - row_top)
    row_total = jnp.sum(stat(1) * weight, axis=0, keepdims=True)
    row_weighted = jnp.sum(stat(2) * weight, axis=0, keepdims=True)
    picked = jnp.sum(stat(3), axis=0, keepdims=True)
    log_norm = row_top + jnp.log(row_total)
    lane = lax.broadcasted_iota(jnp.int32, (1, lanes), 1)
    in_use = jnp.logical_and(meta_ref[4:5, :] > 0.5, lane < used)
    logprob = jnp.where(in_use, picked - log_norm, 0.0)
    entropy = jnp.where(in_use, log_norm - row_weighted / row_total, 0.0)
    segment = meta_ref[3:4, :].astype(jnp.int32)
    for s in range(SEQS):
        seq_ref[s] = jnp.sum(jnp.where(segment == s, logprob, 0.0))
    ranks, _ = ranks_of(scored_ref, row_count)
    first = place_ref[1] * PICK
    for row in range(row_count):
        own = jnp.logical_and(lane == first + ranks[row], scored_ref[row] == 1)
        logprob_ref[row] = jnp.sum(jnp.where(own, logprob, 0.0))
        entropy_ref[row] = jnp.sum(jnp.where(own, entropy, 0.0))


def local(hidden, norm_gain, lm_head, targets, segments, scored):
    row_count, width = hidden.shape
    groups, tp_count = lax.axis_size("req"), lax.axis_size("tp")
    own = lax.axis_index("req")
    place = jnp.stack([own * tp_count + lax.axis_index("tp"), own]).astype(jnp.int32)
    half = width // 2
    used = groups * PICK
    lanes = max(used, LANES)

    def spec(space):
        return pl.BlockSpec(memory_space=space)

    packed = pl.pallas_call(
        pack_kernel,
        out_shape=jax.ShapeDtypeStruct((2 * PICK, half + LANES), jnp.bfloat16),
        in_specs=[spec(VMEM)] * 2 + [spec(SMEM)] * 3,
        out_specs=spec(VMEM),
        scratch_shapes=[VMEM((row_count, width), jnp.float32), VMEM((2 * PICK, half), jnp.float32)],
    )(hidden, norm_gain.reshape(1, width), targets, segments, scored)
    rows = lax.all_gather(packed, "req", axis=0, tiled=True)
    stats, meta = pl.pallas_call(
        score_kernel,
        out_shape=(
            jax.ShapeDtypeStruct((1, STATS * used), jnp.float32),
            jax.ShapeDtypeStruct((8, lanes), jnp.float32),
        ),
        in_specs=[spec(SMEM), spec(VMEM), spec(VMEM)],
        out_specs=(spec(VMEM), spec(VMEM)),
        compiler_params=pltpu.CompilerParams(vmem_limit_bytes=40 * 1024 * 1024),
    )(place, rows, lm_head)
    gathered = lax.all_gather(stats, ("req", "tp"), axis=0, tiled=True)
    return pl.pallas_call(
        functools.partial(finish_kernel, used),
        out_shape=(
            jax.ShapeDtypeStruct((row_count,), jnp.float32),
            jax.ShapeDtypeStruct((row_count,), jnp.float32),
            jax.ShapeDtypeStruct((SEQS,), jnp.float32),
        ),
        in_specs=[spec(SMEM), spec(SMEM), spec(VMEM), spec(VMEM)],
        out_specs=(spec(SMEM), spec(SMEM), spec(SMEM)),
    )(place, scored, gathered, meta)


def solution(mesh):
    return jax.shard_map(
        local,
        mesh=mesh,
        in_specs=(P("req", None), P(), P(None, ("req", "tp")), P("req"), P("req"), P("req")),
        out_specs=(P("req"), P("req"), P()),
        check_vma=False,
    )
```

time: 116 us -> 84.5 us (0.73)
  blocking collectives: 104 us -> 75.6 us
  other arithmetic: 5.32 us -> 0.08 us
  Pallas kernels: 0 us -> 4.36 us
    unnamed x2 -> x0, blocking collectives: 50.3 us -> none
    all_gather x1 -> x2, blocking collectives: 31.6 us -> 75.6 us  [the longest x1 42.9 us: local(): gathered = lax.all_gather(stats, ('req', 'tp'), axis=0, tiled=True)]
    psum x1 -> x0, blocking collectives: 21.6 us -> none  [local(): seq_logprob = lax.psum(partial_sums, 'req')]
    pallas_call x0 -> x3, Pallas kernels: none -> 4.36 us  [the longest x1 1.7 us: local(): pl.pallas_call(pack_kernel, out_shape=jax.ShapeDtypeStruct((2 * PICK, hal...]
    add x63 -> x0, other arithmetic: 1.75 us -> none  [the longest x31 0.93 us: combine_stats(): earlier[1] * early_scale + latter[1] * late_scale]
    convert_element_type x2 -> x0, other arithmetic: 1.63 us -> none  [the longest x1 0.93 us: local(): (values * row_scale * norm_gain.astype(jnp.float32)[None, :]).astype(jnp....]
    reduce_sum x3 -> x0, other arithmetic: 1.33 us -> none  [the longest x1 0.99 us: local(): jnp.mean(values * values, axis=1, keepdims=True) + 1e-05]
    reshape x0 -> x1, local copies, waits for them, and re-layouts: none -> 1.31 us  [local(): norm_gain.reshape(1, width)]
where the time goes in v1:
time: 84.5 us; the launch traced here: 84.2 us
  blocking collectives  75.6 us (89%)
  Pallas kernels  4.36 us (5%)
  local copies, waits for them, and re-layouts  3.49 us (4%)
    all_gather x1, blocking collectives, local(): gathered = lax.all_gather(stats, ('req', 'tp'), axis=0, tiled=True)  42.9 us
    all_gather x1, blocking collectives, local(): rows = lax.all_gather(packed, 'req', axis=0, tiled=True)  32.8 us
    unnamed x6, local copies, waits for them, and re-layouts  2.18 us
    pallas_call x1, Pallas kernels, local(): pl.pallas_call(pack_kernel, out_shape=jax.ShapeDtypeStruct((2 * PICK, hal...  1.7 us

profile of v1, /device:TPU:0, one launch (start us, length us, event | category | flops | bytes accessed | tf_op | source)
XLA Modules:
  0.0 84.2 jit_solution(17349516715490886052)
XLA Ops:
  0.6 0.1 pad_add_fusion.place_ref
  0.7 0.0 copy-start.2
  0.7 1.3 %reshape.9.gain_ref = bf16[1,4096]{1,0:T(2,128)(2,1)} reshape(bf16[4096]{0:T(1024)(128)(2,1)} %param.7) | data formatting | bytes 16384 | tf_op jit(solution)/shard_map/reshape | solution.py:159
  2.0 1.7 %shard_map.85 = bf16[8,2176]{1,0:T(8,128)(2,1)} custom-call(bf16[8,4096]{1,0:T(8,128)(2,1)} %hidden_ref.1, bf16[1,4096]{1,0:T(2,128)(2,1)} %reshape.9.gain_ref, s32[8]{0:T(128)} %targets_ref.1, s32[8]{0:T(128)} %segments_ref.1, s32[8]{0:T(128)} %scored_ref.3), custom_call_target="tpu_custom_call" | custom-call | tf_op jit(solution)/shard_map/pallas_call | solution.py:153
  3.7 32.8 %all_gather.6.rows_ref = bf16[64,2176]{1,0:T(8,128)(2,1)S(1)} all-gather(bf16[8,2176]{1,0:T(8,128)(2,1)} %shard_map.85), channel_id=1, replica_groups=mesh['req'=8,'tp'=4] {'req'}, dimensions={0}, use_global_device_ids=true | all-gather | bytes 313344 | tf_op jit(solution)/shard_map/all_gather | solution.py:160
  36.5 0.0 copy-start
  36.5 1.6 %copy-done = bf16[4096,256]{1,0:T(8,128)(2,1)S(1)} copy-done((bf16[4096,256]{1,0:T(8,128)(2,1)S(1)}, bf16[4096,256]{1,0:T(8,128)(2,1)}, u32[]{:S(2)}) %copy-start) | copy-done | bytes 2097176
  38.1 1.2 %shard_map.86 = (f32[1,128]{1,0:T(1,128)S(1)}, f32[8,128]{1,0:T(8,128)S(1)}) custom-call(s32[2]{0:T(128)S(1)} %pad_add_fusion.place_ref, bf16[64,2176]{1,0:T(8,128)(2,1)S(1)} %all_gather.6.rows_ref, bf16[4096,256]{1,0:T(8,128)(2,1)S(1)} %copy-done), custom_call_target="tpu_custom_call" | custom-call | tf_op jit(solution)/shard_map/pallas_call | solution.py:161
  39.3 0.0 copy-start.1
  39.3 0.6 copy-done.1
  39.9 42.9 %all-gather = f32[32,1,128]{2,1,0:T(1,128)} all-gather(f32[1,1,128]{2,1,0:T(1,128)S(1)} %bitcast.4), channel_id=1, replica_groups=mesh['req'=8,'tp'=4] {'req','tp'}, dimensions={0}, use_global_device_ids=true | all-gather | bytes 16896 | tf_op jit(solution)/shard_map/all_gather | solution.py:171
  82.7 0.0 copy-done.2
  82.7 1.5 %shard_map.87 = (f32[8]{0:T(128)}, f32[8]{0:T(128)}, f32[4]{0:T(128)}) custom-call(s32[2]{0:T(128)} %copy-done.2, s32[8]{0:T(128)} %scored_ref.3, f32[32,128]{1,0:T(8,128)} %bitcast.5, f32[8,128]{1,0:T(8,128)} %copy-done.1), custom_call_target="tpu_custom_call" | custom-call | tf_op jit(solution)/shard_map/pallas_call | solution.py:172
Async XLA Ops:
  0.7 82.0 %copy-start.2 = (s32[2]{0:T(128)}, s32[2]{0:T(128)S(1)}, u32[]{:S(2)}) copy-start(s32[2]{0:T(128)S(1)} %pad_add_fusion.place_ref) | copy-start | bytes 28
  36.5 1.6 %copy-start = (bf16[4096,256]{1,0:T(8,128)(2,1)S(1)}, bf16[4096,256]{1,0:T(8,128)(2,1)}, u32[]{:S(2)}) copy-start(bf16[4096,256]{1,0:T(8,128)(2,1)} %head_ref.1) | copy-start | bytes 6291460
  39.3 0.6 copy-start.1

commit v2 on v1

--- a/solution.py
+++ b/solution.py
@@ -138,6 +138,11 @@
         entropy_ref[row] = jnp.sum(jnp.where(own, entropy, 0.0))
 
 
+def sent_to_all(block, axis):
+    copies = jnp.broadcast_to(block[None], (lax.axis_size(axis),) + block.shape)
+    return lax.all_to_all(copies, axis, 0, 0).reshape((-1,) + block.shape[1:])
+
+
 def local(hidden, norm_gain, lm_head, targets, segments, scored):
     row_count, width = hidden.shape
     groups, tp_count = lax.axis_size("req"), lax.axis_size("tp")
@@ -157,7 +162,7 @@
         out_specs=spec(VMEM),
         scratch_shapes=[VMEM((row_count, width), jnp.float32), VMEM((2 * PICK, half), jnp.float32)],
     )(hidden, norm_gain.reshape(1, width), targets, segments, scored)
-    rows = lax.all_gather(packed, "req", axis=0, tiled=True)
+    rows = sent_to_all(packed, "req")
     stats, meta = pl.pallas_call(
         score_kernel,
         out_shape=(
@@ -168,7 +173,7 @@
         out_specs=(spec(VMEM), spec(VMEM)),
         compiler_params=pltpu.CompilerParams(vmem_limit_bytes=40 * 1024 * 1024),
     )(place, rows, lm_head)
-    gathered = lax.all_gather(stats, ("req", "tp"), axis=0, tiled=True)
+    gathered = sent_to_all(stats, ("req", "tp"))
     return pl.pallas_call(
         functools.partial(finish_kernel, used),
         out_shape=(

time: 84.5 us -> 37.7 us (0.45)
  blocking collectives: 75.6 us -> 10.7 us
  waiting for transfers between devices: 0 us -> 9.19 us
  starting transfers between devices: 0 us -> 7.28 us
  local copies, waits for them, and re-layouts: 3.49 us -> 4.98 us
    all_gather x2 -> x0, blocking collectives: 75.6 us -> none  [the longest x1 42.9 us: local(): gathered = lax.all_gather(stats, ('req', 'tp'), axis=0, tiled=True)]
    all_to_all x0 -> x1, blocking collectives: none -> 10.7 us  [sent_to_all(): return lax.all_to_all(copies, axis, 0, 0).reshape((-1,) + block.shape[1:])]
    all_to_all x0 -> x1, waiting for transfers between devices: none -> 9.19 us  [sent_to_all(): return lax.all_to_all(copies, axis, 0, 0).reshape((-1,) + block.shape[1:])]
    all_to_all x0 -> x1, starting transfers between devices: none -> 7.28 us  [sent_to_all(): return lax.all_to_all(copies, axis, 0, 0).reshape((-1,) + block.shape[1:])]
    broadcast_in_dim x0 -> x2, local copies, waits for them, and re-layouts: none -> 1.5 us  [sent_to_all(): copies = jnp.broadcast_to(block[None], (lax.axis_size(axis),) + block.shape)]
  transfers between devices with their start and end apart: 0 -> 1, of which waited for: 0 -> 1; matrix products, arithmetic and copies ran while one was open for 0% -> 0% of each run, Pallas kernels for 0% -> 0%
where the time goes in v2:
time: 37.7 us; the launch traced here: 37.2 us
  blocking collectives  10.7 us (28%)
  waiting for transfers between devices  9.19 us (24%)
  starting transfers between devices  7.28 us (19%)
  local copies, waits for them, and re-layouts  4.98 us (13%)
  Pallas kernels  4.37 us (12%)
  between operations  0.65 us (2%)
    all_to_all x1, blocking collectives, sent_to_all(): return lax.all_to_all(copies, axis, 0, 0).reshape((-1,) + block.shape[1:])  10.7 us
    all_to_all x1, waiting for transfers between devices, sent_to_all(): return lax.all_to_all(copies, axis, 0, 0).reshape((-1,) + block.shape[1:])  9.19 us
    all_to_all x1, starting transfers between devices, sent_to_all(): return lax.all_to_all(copies, axis, 0, 0).reshape((-1,) + block.shape[1:])  7.28 us
    unnamed x6, local copies, waits for them, and re-layouts  2.18 us
    pallas_call x1, Pallas kernels, local(): pl.pallas_call(pack_kernel, out_shape=jax.ShapeDtypeStruct((2 * PICK, hal...  1.69 us
    broadcast_in_dim x2, local copies, waits for them, and re-layouts, sent_to_all(): copies = jnp.broadcast_to(block[None], (lax.axis_size(axis),) + block.shape)  1.5 us
    pallas_call x1, Pallas kernels, local(): pl.pallas_call(functools.partial(finish_kernel, used), out_shape=(jax.Sha...  1.49 us
    reshape x1, local copies, waits for them, and re-layouts, local(): norm_gain.reshape(1, width)  1.31 us
  transfers between devices with their start and end apart: 1, of which 1 were waited for; matrix products, arithmetic and copies ran while one was open for 0% of the time, Pallas kernels for 0%

profile of v2, /device:TPU:0, one launch (start us, length us, event | category | flops | bytes accessed | tf_op | source)
XLA Modules:
  0.0 37.2 jit_solution(16281497102851710213)
XLA Ops:
  0.6 1.3 %reshape.19.gain_ref = bf16[1,4096]{1,0:T(2,128)(2,1)} reshape(bf16[4096]{0:T(1024)(128)(2,1)} %param.7) | data formatting | bytes 16384 | tf_op jit(solution)/shard_map/reshape | solution.py:164
  1.9 1.7 %shard_map.85 = bf16[8,2176]{1,0:T(8,128)(2,1)} custom-call(bf16[8,4096]{1,0:T(8,128)(2,1)} %hidden_ref.1, bf16[1,4096]{1,0:T(2,128)(2,1)} %reshape.19.gain_ref, s32[8]{0:T(128)} %targets_ref.1, s32[8]{0:T(128)} %segments_ref.1, s32[8]{0:T(128)} %scored_ref.3), custom_call_target="tpu_custom_call" | custom-call | tf_op jit(solution)/shard_map/pallas_call | solution.py:158
  3.6 1.5 %broadcast_in_dim.6 = bf16[8,8,2176]{2,1,0:T(8,128)(2,1)} broadcast(bf16[8,2176]{1,0:T(8,128)(2,1)} %shard_map.85), dimensions={1,2} | broadcast | bytes 313344 | tf_op jit(solution)/shard_map/broadcast_in_dim | solution.py:142
  5.1 7.3 %all-to-all-start = ((bf16[8,8,2176]{2,1,0:T(8,128)(2,1)}), bf16[8,8,2176]{2,1,0:T(8,128)(2,1)S(1)}, u32[]{:S(2)}, u32[]{:S(2)}) async-start(bf16[8,8,2176]{2,1,0:T(8,128)(2,1)} %broadcast_in_dim.6), calls=%async_computation | async-start | bytes 557056 | tf_op jit(solution)/shard_map/all_to_all | solution.py:143
  12.4 0.1 pad_add_fusion.place_ref
  12.5 0.0 copy-start.2
  12.5 9.2 %all-to-all-done = bf16[8,8,2176]{2,1,0:T(8,128)(2,1)S(1)} async-done(((bf16[8,8,2176]{2,1,0:T(8,128)(2,1)}), bf16[8,8,2176]{2,1,0:T(8,128)(2,1)S(1)}, u32[]{:S(2)}, u32[]{:S(2)}) %all-to-all-start) | async-done | bytes 278560 | tf_op jit(solution)/shard_map/all_to_all | solution.py:143
  21.7 0.0 copy-start
  21.7 1.6 %copy-done = bf16[4096,256]{1,0:T(8,128)(2,1)S(1)} copy-done((bf16[4096,256]{1,0:T(8,128)(2,1)S(1)}, bf16[4096,256]{1,0:T(8,128)(2,1)}, u32[]{:S(2)}) %copy-start) | copy-done | bytes 2097176
  23.3 1.2 %shard_map.86 = (f32[1,128]{1,0:T(1,128)S(1)}, f32[8,128]{1,0:T(8,128)S(1)}) custom-call(s32[2]{0:T(128)S(1)} %pad_add_fusion.place_ref, bf16[64,2176]{1,0:T(8,128)(2,1)S(1)} %bitcast.5, bf16[4096,256]{1,0:T(8,128)(2,1)S(1)} %copy-done), custom_call_target="tpu_custom_call" | custom-call | tf_op jit(solution)/shard_map/pallas_call | solution.py:166
  24.5 0.0 copy-start.1
  24.5 0.6 %copy-done.1 = f32[8,128]{1,0:T(8,128)} copy-done((f32[8,128]{1,0:T(8,128)}, f32[8,128]{1,0:T(8,128)S(1)}, u32[]{:S(2)}) %copy-start.1) | copy-done | bytes 4120
  25.1 10.7 %all_to_all.10 = f32[32,1,128]{2,1,0:T(1,128)} all-to-all(f32[32,1,128]{2,1,0:T(1,128)S(1)} %broadcast_in_dim.16), channel_id=1, replica_groups=mesh['req'=8,'tp'=4] {'req','tp'}, dimensions={0} | all-to-all | bytes 32768 | tf_op jit(solution)/shard_map/all_to_all | solution.py:143
  35.7 0.0 copy-done.2
  35.7 1.5 %shard_map.87 = (f32[8]{0:T(128)}, f32[8]{0:T(128)}, f32[4]{0:T(128)}) custom-call(s32[2]{0:T(128)} %copy-done.2, s32[8]{0:T(128)} %scored_ref.3, f32[32,128]{1,0:T(8,128)} %bitcast.7, f32[8,128]{1,0:T(8,128)} %copy-done.1), custom_call_target="tpu_custom_call" | custom-call | tf_op jit(solution)/shard_map/pallas_call | solution.py:177
  (1 shorter events, 0.0 us)
Async XLA Ops:
  5.1 16.5 %all-to-all-start = ((bf16[8,8,2176]{2,1,0:T(8,128)(2,1)}), bf16[8,8,2176]{2,1,0:T(8,128)(2,1)S(1)}, u32[]{:S(2)}, u32[]{:S(2)}) async-start(bf16[8,8,2176]{2,1,0:T(8,128)(2,1)} %broadcast_in_dim.6), calls=%async_computation | async-start | bytes 557056 | tf_op jit(solution)/shard_map/all_to_all | solution.py:143
  12.5 23.3 %copy-start.2 = (s32[2]{0:T(128)}, s32[2]{0:T(128)S(1)}, u32[]{:S(2)}) copy-start(s32[2]{0:T(128)S(1)} %pad_add_fusion.place_ref) | copy-start | bytes 28
  21.7 1.6 %copy-start = (bf16[4096,256]{1,0:T(8,128)(2,1)S(1)}, bf16[4096,256]{1,0:T(8,128)(2,1)}, u32[]{:S(2)}) copy-start(bf16[4096,256]{1,0:T(8,128)(2,1)} %head_ref.1) | copy-start | bytes 6291460
  24.5 0.6 %copy-start.1 = (f32[8,128]{1,0:T(8,128)}, f32[8,128]{1,0:T(8,128)S(1)}, u32[]{:S(2)}) copy-start(f32[8,128]{1,0:T(8,128)S(1)} %get-tuple-element.6.meta_ref) | copy-start | bytes 12292

commit v3 on v2

--- a/solution.py
+++ b/solution.py
@@ -24,10 +24,11 @@
     return ranks, so_far
 
 
-def pack_kernel(hidden_ref, gain_ref, targets_ref, segments_ref, scored_ref, out_ref, wide_ref, halves_ref):
+def pack_kernel(hidden_ref, gain_ref, targets_ref, segments_ref, scored_ref, out_ref, wide_ref, halves_ref, gains_ref):
     row_count, width = hidden_ref.shape
     half = width // 2
     wide_ref[...] = hidden_ref[...].astype(jnp.float32)
+    gains_ref[...] = gain_ref[...].astype(jnp.float32)
     ranks, count = ranks_of(scored_ref, row_count)
     source = [jnp.int32(0)] * PICK
     for row in range(row_count):
@@ -40,23 +41,40 @@
     values = halves_ref[...]
     part = jnp.sum(values * values, axis=1, keepdims=True)
     part = jnp.broadcast_to(part, (2 * PICK, LANES))
-    total = (part + pltpu.roll(part, PICK, 0))[:, :1]
-    row_scale = lax.rsqrt(total / width + 1e-05)
-    upper = lax.broadcasted_iota(jnp.int32, (2 * PICK, 1), 0) < PICK
-    gain = jnp.where(upper, gain_ref[:, :half].astype(jnp.float32), gain_ref[:, half:].astype(jnp.float32))
-    out_ref[:, :half] = (values * row_scale * gain).astype(jnp.bfloat16)
+    row_scale = lax.rsqrt((part + pltpu.roll(part, PICK, 0)) / width + 1e-05)
     sub = lax.broadcasted_iota(jnp.int32, (2 * PICK, LANES), 0)
-    sub = jnp.where(sub >= PICK, sub - PICK, sub)
     lane = lax.broadcasted_iota(jnp.int32, (2 * PICK, LANES), 1)
+    upper = sub < PICK
+    chunks = half // LANES
+    for at in range(chunks):
+        gain = jnp.where(upper, gains_ref[at : at + 1, :], gains_ref[chunks + at : chunks + at + 1, :])
+        piece = halves_ref[:, at * LANES : (at + 1) * LANES]
+        piece = (piece * row_scale * gain).astype(jnp.bfloat16)
+        for to in range(out_ref.shape[0]):
+            out_ref[to, :, at * LANES : (at + 1) * LANES] = piece
+    row_of = jnp.where(upper, sub, sub - PICK)
     side = jnp.zeros((2 * PICK, LANES), jnp.int32)
     for r in range(PICK):
         target = targets_ref[source[r]]
-        fields = (target % 256, (target // 256) % 256, target // 65536, segments_ref[source[r]], (count > r).astype(jnp.int32))
-        line = jnp.zeros((2 * PICK, LANES), jnp.int32)
-        for at, field in enumerate(fields):
-            line = jnp.where(lane == at, field, line)
-        side = jnp.where(sub == r, line, side)
-    out_ref[:, half:] = side.astype(jnp.float32).astype(jnp.bfloat16)
+        digits = jnp.where(lane == 0, target & 255, jnp.where(lane == 1, (target >> 8) & 255, target >> 16))
+        line = jnp.where(lane < 3, digits, jnp.where(lane == 3, segments_ref[source[r]], (count > r).astype(jnp.int32)))
+        side = jnp.where(row_of == r, line, side)
+    side = side.astype(jnp.float32).astype(jnp.bfloat16)
+    for to in range(out_ref.shape[0]):
+        out_ref[to, :, half:] = side
+
+
+def stage_kernel(head_ref, out_ref, sems):
+    parts = sems.shape[0]
+    depth = head_ref.shape[0] // parts
+    copies = [
+        pltpu.make_async_copy(head_ref.at[pl.ds(i * depth, depth)], out_ref.at[pl.ds(i * depth, depth)], sems.at[i])
+        for i in range(parts)
+    ]
+    for copy in copies:
+        copy.start()
+    for copy in copies:
+        copy.wait()
 
 
 def score_kernel(place_ref, rows_ref, head_ref, stats_ref, meta_ref):
@@ -127,15 +145,32 @@
     in_use = jnp.logical_and(meta_ref[4:5, :] > 0.5, lane < used)
     logprob = jnp.where(in_use, picked - log_norm, 0.0)
     entropy = jnp.where(in_use, log_norm - row_weighted / row_total, 0.0)
+    sub = lax.broadcasted_iota(jnp.int32, (8, LANES), 0)
+    own_lane = lax.broadcasted_iota(jnp.int32, (8, LANES), 1)
+    rows_of = lax.broadcasted_iota(jnp.int32, (8, lanes), 0)
     segment = meta_ref[3:4, :].astype(jnp.int32)
-    for s in range(SEQS):
-        seq_ref[s] = jnp.sum(jnp.where(segment == s, logprob, 0.0))
+    sums = jnp.sum(jnp.where(segment == rows_of, logprob, 0.0), axis=1, keepdims=True)
+    seqs = jnp.sum(jnp.where(sub == own_lane, sums, 0.0), axis=0, keepdims=True)
+    seq_ref[...] = seqs[0, :SEQS]
+    first = place_ref[1] * PICK
+    block = first // LANES
+    own_logprob, own_entropy = logprob[:, :LANES], entropy[:, :LANES]
+    for at in range(1, lanes // LANES):
+        piece = slice(at * LANES, (at + 1) * LANES)
+        own_logprob = jnp.where(block == at, logprob[:, piece], own_logprob)
+        own_entropy = jnp.where(block == at, entropy[:, piece], own_entropy)
     ranks, _ = ranks_of(scored_ref, row_count)
-    first = place_ref[1] * PICK
+    at = jnp.zeros((8, LANES), jnp.int32)
+    keep = jnp.zeros((8, LANES), jnp.int32)
     for row in range(row_count):
-        own = jnp.logical_and(lane == first + ranks[row], scored_ref[row] == 1)
-        logprob_ref[row] = jnp.sum(jnp.where(own, logprob, 0.0))
-        entropy_ref[row] = jnp.sum(jnp.where(own, entropy, 0.0))
+        at = jnp.where(own_lane == row, first - block * LANES + ranks[row], at)
+        keep = jnp.where(own_lane == row, scored_ref[row], keep)
+    at = jnp.minimum(at, LANES - 1)
+    both = jnp.where(sub == 0, own_logprob, own_entropy)
+    both = jnp.take_along_axis(both, at, axis=1)
+    both = jnp.where(keep == 1, both, 0.0)
+    logprob_ref[...] = both[0, :row_count]
+    entropy_ref[...] = both[1, :row_count]
 
 
 def sent_to_all(block, axis):
@@ -157,22 +192,34 @@
 
     packed = pl.pallas_call(
         pack_kernel,
-        out_shape=jax.ShapeDtypeStruct((2 * PICK, half + LANES), jnp.bfloat16),
+        out_shape=jax.ShapeDtypeStruct((groups, 2 * PICK, half + LANES), jnp.bfloat16),
         in_specs=[spec(VMEM)] * 2 + [spec(SMEM)] * 3,
         out_specs=spec(VMEM),
-        scratch_shapes=[VMEM((row_count, width), jnp.float32), VMEM((2 * PICK, half), jnp.float32)],
-    )(hidden, norm_gain.reshape(1, width), targets, segments, scored)
-    rows = sent_to_all(packed, "req")
+        scratch_shapes=[
+            VMEM((row_count, width), jnp.float32),
+            VMEM((2 * PICK, half), jnp.float32),
+            VMEM((width // LANES, LANES), jnp.float32),
+        ],
+    )(hidden, norm_gain.reshape(width // LANES, LANES), targets, segments, scored)
+    rows = lax.all_to_all(packed, "req", 0, 0).reshape(groups * 2 * PICK, half + LANES)
+    head = pl.pallas_call(
+        stage_kernel,
+        out_shape=VMEM(lm_head.shape, lm_head.dtype),
+        in_specs=[spec(pltpu.HBM)],
+        out_specs=spec(VMEM),
+        scratch_shapes=[pltpu.SemaphoreType.DMA((4,))],
+        cost_estimate=pl.CostEstimate(flops=0, bytes_accessed=2 * lm_head.size * 2, transcendentals=0),
+    )(pltpu.with_memory_space_constraint(lm_head, pltpu.HBM))
     stats, meta = pl.pallas_call(
         score_kernel,
         out_shape=(
             jax.ShapeDtypeStruct((1, STATS * used), jnp.float32),
-            jax.ShapeDtypeStruct((8, lanes), jnp.float32),
+            VMEM((8, lanes), jnp.float32),
         ),
         in_specs=[spec(SMEM), spec(VMEM), spec(VMEM)],
         out_specs=(spec(VMEM), spec(VMEM)),
         compiler_params=pltpu.CompilerParams(vmem_limit_bytes=40 * 1024 * 1024),
-    )(place, rows, lm_head)
+    )(place, rows, pltpu.with_memory_space_constraint(head, VMEM))
     gathered = sent_to_all(stats, ("req", "tp"))
     return pl.pallas_call(
         functools.partial(finish_kernel, used),
@@ -182,8 +229,8 @@
             jax.ShapeDtypeStruct((SEQS,), jnp.float32),
         ),
         in_specs=[spec(SMEM), spec(SMEM), spec(VMEM), spec(VMEM)],
-        out_specs=(spec(SMEM), spec(SMEM), spec(SMEM)),
-    )(place, scored, gathered, meta)
+        out_specs=(spec(VMEM), spec(VMEM), spec(VMEM)),
+    )(place, scored, gathered, pltpu.with_memory_space_constraint(meta, VMEM))
 
 
 def solution(mesh):

time: 37.7 us -> 32.4 us (0.86)
  local copies, waits for them, and re-layouts: 4.98 us -> 0.01 us
  waiting for transfers between devices: 9.19 us -> 7.63 us
  Pallas kernels: 4.37 us -> 5.9 us
    unnamed x6 -> x2, local copies, waits for them, and re-layouts: 2.18 us -> 0.01 us
    pallas_call x1 -> x2, Pallas kernels: 1.69 us -> 3.3 us  [the longest x1 1.75 us: local(): pl.pallas_call(pack_kernel, out_shape=jax.ShapeDtypeStruct((groups, 2 * P...]
    all_to_all x1, waiting for transfers between devices: 9.19 us -> 7.63 us  [local(): lax.all_to_all(packed, 'req', 0, 0).reshape(groups * 2 * PICK, half + LANES)]
    broadcast_in_dim x2 -> x1, local copies, waits for them, and re-layouts: 1.5 us -> 0.01 us  [sent_to_all(): copies = jnp.broadcast_to(block[None], (lax.axis_size(axis),) + block.shape)]
    reshape x1 -> x0, local copies, waits for them, and re-layouts: 1.31 us -> none  [local(): norm_gain.reshape(1, width)]
  transfers between devices with their start and end apart: 1 -> 1, of which waited for: 1 -> 1; matrix products, arithmetic and copies ran while one was open for 0% -> 0% of each run, Pallas kernels for 0% -> 5%
where the time goes in v3:
time: 32.4 us; the launch traced here: 32.1 us
  blocking collectives  10.5 us (32%)
  waiting for transfers between devices  7.63 us (24%)
  starting transfers between devices  7.28 us (22%)
  Pallas kernels  5.9 us (18%)
  between operations  0.67 us (2%)
    all_to_all x1, blocking collectives, sent_to_all(): return lax.all_to_all(copies, axis, 0, 0).reshape((-1,) + block.shape[1:])  10.5 us
    all_to_all x1, waiting for transfers between devices, local(): lax.all_to_all(packed, 'req', 0, 0).reshape(groups * 2 * PICK, half + LANES)  7.63 us
    all_to_all x1, starting transfers between devices, local(): lax.all_to_all(packed, 'req', 0, 0).reshape(groups * 2 * PICK, half + LANES)  7.28 us
    pallas_call x1, Pallas kernels, local(): pl.pallas_call(pack_kernel, out_shape=jax.ShapeDtypeStruct((groups, 2 * P...  1.75 us
    pallas_call x1, Pallas kernels, local(): pl.pallas_call(stage_kernel, out_shape=VMEM(lm_head.shape, lm_head.dtype)...  1.55 us
    pallas_call x1, Pallas kernels, local(): pl.pallas_call(functools.partial(finish_kernel, used), out_shape=(jax.Sha...  1.41 us
    pallas_call x1, Pallas kernels, local(): pl.pallas_call(score_kernel, out_shape=(jax.ShapeDtypeStruct((1, STATS *...  1.18 us
  transfers between devices with their start and end apart: 1, of which 1 were waited for; matrix products, arithmetic and copies ran while one was open for 0% of the time, Pallas kernels for 5%

profile of v3, /device:TPU:0, one launch (start us, length us, event | category | flops | bytes accessed | tf_op | source)
XLA Modules:
  0.0 32.1 jit_solution(8793289215304857716)
XLA Ops:
  0.6 1.8 %shard_map.85 = bf16[8,8,2176]{2,1,0:T(8,128)(2,1)} custom-call(bf16[8,4096]{1,0:T(8,128)(2,1)} %hidden_ref.1, bf16[32,128]{1,0:T(8,128)(2,1)} %bitcast.9, s32[8]{0:T(128)} %targets_ref.1, s32[8]{0:T(128)} %segments_ref.1, s32[8]{0:T(128)} %scored_ref.3), custom_call_target="tpu_custom_call" | custom-call | tf_op jit(solution)/shard_map/pallas_call | solution.py:193
  2.4 7.3 %all-to-all-start = ((bf16[8,8,2176]{2,1,0:T(8,128)(2,1)}), bf16[8,8,2176]{2,1,0:T(8,128)(2,1)S(1)}, u32[]{:S(2)}, u32[]{:S(2)}) async-start(bf16[8,8,2176]{2,1,0:T(8,128)(2,1)} %shard_map.85), calls=%async_computation | async-start | bytes 557056 | tf_op jit(solution)/shard_map/all_to_all | solution.py:204
  9.7 1.5 %shard_map.86.head_ref = bf16[4096,256]{1,0:T(8,128)(2,1)S(1)} custom-call(bf16[4096,256]{1,0:T(8,128)(2,1)} %head_ref.1), custom_call_target="tpu_custom_call" | custom-call | bytes 4194304 | tf_op jit(solution)/shard_map/pallas_call | solution.py:205
  11.2 0.1 pad_add_fusion.place_ref
  11.3 0.0 copy-start
  11.3 7.6 %all-to-all-done = bf16[8,8,2176]{2,1,0:T(8,128)(2,1)S(1)} async-done(((bf16[8,8,2176]{2,1,0:T(8,128)(2,1)}), bf16[8,8,2176]{2,1,0:T(8,128)(2,1)S(1)}, u32[]{:S(2)}, u32[]{:S(2)}) %all-to-all-start) | async-done | bytes 278560 | tf_op jit(solution)/shard_map/all_to_all | solution.py:204
  18.9 1.2 %shard_map.87 = (f32[1,128]{1,0:T(1,128)S(1)}, f32[8,128]{1,0:T(8,128)S(1)}) custom-call(s32[2]{0:T(128)S(1)} %pad_add_fusion.place_ref, bf16[64,2176]{1,0:T(8,128)(2,1)S(1)} %bitcast.6, bf16[4096,256]{1,0:T(8,128)(2,1)S(1)} %shard_map.86.head_ref), custom_call_target="tpu_custom_call" | custom-call | tf_op jit(solution)/shard_map/pallas_call | solution.py:213
  20.1 10.5 %all_to_all.10 = f32[32,1,128]{2,1,0:T(1,128)} all-to-all(f32[32,1,128]{2,1,0:T(1,128)S(1)} %broadcast_in_dim.9), channel_id=1, replica_groups=mesh['req'=8,'tp'=4] {'req','tp'}, dimensions={0} | all-to-all | bytes 32768 | tf_op jit(solution)/shard_map/all_to_all | solution.py:178
  30.7 0.0 copy-done
  30.7 1.4 %shard_map.88 = (f32[8]{0:T(128)}, f32[8]{0:T(128)}, f32[4]{0:T(128)}) custom-call(s32[2]{0:T(128)} %copy-done, s32[8]{0:T(128)} %scored_ref.3, f32[32,128]{1,0:T(8,128)} %bitcast.8, f32[8,128]{1,0:T(8,128)S(1)} %get-tuple-element.6.meta_ref), custom_call_target="tpu_custom_call" | custom-call | tf_op jit(solution)/shard_map/pallas_call | solution.py:224
  (1 shorter events, 0.0 us)
Async XLA Ops:
  2.4 16.5 %all-to-all-start = ((bf16[8,8,2176]{2,1,0:T(8,128)(2,1)}), bf16[8,8,2176]{2,1,0:T(8,128)(2,1)S(1)}, u32[]{:S(2)}, u32[]{:S(2)}) async-start(bf16[8,8,2176]{2,1,0:T(8,128)(2,1)} %shard_map.85), calls=%async_computation | async-start | bytes 557056 | tf_op jit(solution)/shard_map/all_to_all | solution.py:204
  11.3 19.4 %copy-start = (s32[2]{0:T(128)}, s32[2]{0:T(128)S(1)}, u32[]{:S(2)}) copy-start(s32[2]{0:T(128)S(1)} %pad_add_fusion.place_ref) | copy-start | bytes 28

commit v4 on v3

--- a/solution.py
+++ b/solution.py
@@ -50,8 +50,7 @@
         gain = jnp.where(upper, gains_ref[at : at + 1, :], gains_ref[chunks + at : chunks + at + 1, :])
         piece = halves_ref[:, at * LANES : (at + 1) * LANES]
         piece = (piece * row_scale * gain).astype(jnp.bfloat16)
-        for to in range(out_ref.shape[0]):
-            out_ref[to, :, at * LANES : (at + 1) * LANES] = piece
+        out_ref[:, at * LANES : (at + 1) * LANES] = piece
     row_of = jnp.where(upper, sub, sub - PICK)
     side = jnp.zeros((2 * PICK, LANES), jnp.int32)
     for r in range(PICK):
@@ -60,8 +59,7 @@
         line = jnp.where(lane < 3, digits, jnp.where(lane == 3, segments_ref[source[r]], (count > r).astype(jnp.int32)))
         side = jnp.where(row_of == r, line, side)
     side = side.astype(jnp.float32).astype(jnp.bfloat16)
-    for to in range(out_ref.shape[0]):
-        out_ref[to, :, half:] = side
+    out_ref[:, half:] = side
 
 
 def stage_kernel(head_ref, out_ref, sems):
@@ -77,12 +75,15 @@
         copy.wait()
 
 
-def score_kernel(place_ref, rows_ref, head_ref, stats_ref, meta_ref):
+def score_kernel(groups, place_ref, head_ref, *refs):
+    blocks, (stats_ref, meta_ref, rows_ref) = refs[:groups], refs[groups:]
     width, cols = head_ref.shape
     half = width // 2
-    groups = rows_ref.shape[0] // (2 * PICK)
     used = groups * PICK
-    rows = rows_ref[:, :half]
+    for step, block in enumerate(blocks):
+        sender = place_ref[1] - step
+        rows_ref[jnp.where(sender < 0, sender + groups, sender)] = block[...]
+    rows = rows_ref[:, :, :half].reshape(groups * 2 * PICK, half)
     early = jnp.dot(rows, head_ref[:half, :], preferred_element_type=jnp.float32)
     late = jnp.dot(rows, head_ref[half:, :], preferred_element_type=jnp.float32)
     early = early.reshape(groups // 2, 2, 2 * PICK, cols)
@@ -97,7 +98,7 @@
 
     logits = jnp.where(upper, early[:, 0] + swap(late[:, 0]), swap(early[:, 1]) + late[:, 1])
     logits = logits.reshape(used, cols)
-    side = rows_ref[:, half:].astype(jnp.float32).reshape(groups // 2, 2, 2 * PICK, LANES)
+    side = rows_ref[:, :, half:].astype(jnp.float32).reshape(groups // 2, 2, 2 * PICK, LANES)
     side = jnp.where(upper, side[:, 0], side[:, 1]).reshape(used, LANES)
     copies = max(1, LANES // used)
     if copies > 1:
@@ -192,7 +193,7 @@
 
     packed = pl.pallas_call(
         pack_kernel,
-        out_shape=jax.ShapeDtypeStruct((groups, 2 * PICK, half + LANES), jnp.bfloat16),
+        out_shape=jax.ShapeDtypeStruct((2 * PICK, half + LANES), jnp.bfloat16),
         in_specs=[spec(VMEM)] * 2 + [spec(SMEM)] * 3,
         out_specs=spec(VMEM),
         scratch_shapes=[
@@ -201,7 +202,9 @@
             VMEM((width // LANES, LANES), jnp.float32),
         ],
     )(hidden, norm_gain.reshape(width // LANES, LANES), targets, segments, scored)
-    rows = lax.all_to_all(packed, "req", 0, 0).reshape(groups * 2 * PICK, half + LANES)
+    blocks = [packed] + [
+        lax.ppermute(packed, "req", [(i, (i + step) % groups) for i in range(groups)]) for step in range(1, groups)
+    ]
     head = pl.pallas_call(
         stage_kernel,
         out_shape=VMEM(lm_head.shape, lm_head.dtype),
@@ -211,15 +214,16 @@
         cost_estimate=pl.CostEstimate(flops=0, bytes_accessed=2 * lm_head.size * 2, transcendentals=0),
     )(pltpu.with_memory_space_constraint(lm_head, pltpu.HBM))
     stats, meta = pl.pallas_call(
-        score_kernel,
+        functools.partial(score_kernel, groups),
         out_shape=(
             jax.ShapeDtypeStruct((1, STATS * used), jnp.float32),
             VMEM((8, lanes), jnp.float32),
         ),
-        in_specs=[spec(SMEM), spec(VMEM), spec(VMEM)],
+        in_specs=[spec(SMEM)] + [spec(VMEM)] * (1 + groups),
         out_specs=(spec(VMEM), spec(VMEM)),
+        scratch_shapes=[VMEM((groups, 2 * PICK, half + LANES), jnp.bfloat16)],
         compiler_params=pltpu.CompilerParams(vmem_limit_bytes=40 * 1024 * 1024),
-    )(place, rows, pltpu.with_memory_space_constraint(head, VMEM))
+    )(place, pltpu.with_memory_space_constraint(head, VMEM), *blocks)
     gathered = sent_to_all(stats, ("req", "tp"))
     return pl.pallas_call(
         functools.partial(finish_kernel, used),

time: 32.4 us -> 33.2 us (1.025)
  starting transfers between devices: 7.28 us -> 12.4 us
  waiting for transfers between devices: 7.63 us -> 4.06 us
  blocking collectives: 10.5 us -> 9.89 us
    ppermute x0 -> x7, starting transfers between devices: none -> 12.4 us  [local(): lax.ppermute(packed, 'req', [(i, (i + step) % groups) for i in range(grou...]
    all_to_all x1 -> x0, waiting for transfers between devices: 7.63 us -> none  [local(): lax.all_to_all(packed, 'req', 0, 0).reshape(groups * 2 * PICK, half + LANES)]
    all_to_all x1 -> x0, starting transfers between devices: 7.28 us -> none  [local(): lax.all_to_all(packed, 'req', 0, 0).reshape(groups * 2 * PICK, half + LANES)]
    ppermute x0 -> x7, waiting for transfers between devices: none -> 4.06 us  [local(): lax.ppermute(packed, 'req', [(i, (i + step) % groups) for i in range(grou...]
    all_to_all x1, blocking collectives: 10.5 us -> 9.89 us  [sent_to_all(): return lax.all_to_all(copies, axis, 0, 0).reshape((-1,) + block.shape[1:])]
  transfers between devices with their start and end apart: 1 -> 7, of which waited for: 1 -> 3; matrix products, arithmetic and copies ran while one was open for 0% -> 0% of each run, Pallas kernels for 5% -> 5%
where the time goes in v4:
time: 33.2 us; the launch traced here: 32.9 us
  starting transfers between devices  12.4 us (37%)
  blocking collectives  9.89 us (30%)
  Pallas kernels  5.79 us (17%)
  waiting for transfers between devices  4.06 us (12%)
  between operations  0.68 us (2%)
    ppermute x7, starting transfers between devices, local(): lax.ppermute(packed, 'req', [(i, (i + step) % groups) for i in range(grou...  12.4 us
    all_to_all x1, blocking collectives, sent_to_all(): return lax.all_to_all(copies, axis, 0, 0).reshape((-1,) + block.shape[1:])  9.89 us
    ppermute x7, waiting for transfers between devices, local(): lax.ppermute(packed, 'req', [(i, (i + step) % groups) for i in range(grou...  4.06 us
    pallas_call x1, Pallas kernels, local(): pl.pallas_call(pack_kernel, out_shape=jax.ShapeDtypeStruct((2 * PICK, hal...  1.63 us
    pallas_call x1, Pallas kernels, local(): pl.pallas_call(stage_kernel, out_shape=VMEM(lm_head.shape, lm_head.dtype)...  1.56 us
    pallas_call x1, Pallas kernels, local(): pl.pallas_call(functools.partial(finish_kernel, used), out_shape=(jax.Sha...  1.41 us
    pallas_call x1, Pallas kernels, local(): pl.pallas_call(functools.partial(score_kernel, groups), out_shape=(jax.Sh...  1.19 us
  transfers between devices with their start and end apart: 7, of which 3 were waited for; matrix products, arithmetic and copies ran while one was open for 0% of the time, Pallas kernels for 5%

profile of v4, /device:TPU:0, one launch (start us, length us, event | category | flops | bytes accessed | tf_op | source)
XLA Modules:
  0.0 32.9 jit_solution(3328997240186684288)
XLA Ops:
  0.6 1.6 %shard_map.86.refs_0_ = bf16[8,2176]{1,0:T(8,128)(2,1)} custom-call(bf16[8,4096]{1,0:T(8,128)(2,1)} %hidden_ref.1, bf16[32,128]{1,0:T(8,128)(2,1)} %bitcast.7, s32[8]{0:T(128)} %targets_ref.1, s32[8]{0:T(128)} %segments_ref.1, s32[8]{0:T(128)} %scored_ref.3), custom_call_target="tpu_custom_call" | custom-call | tf_op jit(solution)/shard_map/pallas_call | solution.py:194
  2.3 6.0 %collective-permute-start.6 = (bf16[8,2176]{1,0:T(8,128)(2,1)}, bf16[8,2176]{1,0:T(8,128)(2,1)S(1)}, u32[]{:S(2)}, u32[]{:S(2)}) collective-permute-start(bf16[8,2176]{1,0:T(8,128)(2,1)} %shard_map.86.refs_0_), channel_id=1, source_target_pairs={{0,28},{4,0},{8,4},{12,8},{16,12},{20,16},{24,20},{28,24},{1,29},{... | collective-permute-start | bytes 104456 | tf_op jit(solution)/shard_map/ppermute | solution.py:206
  8.3 0.4 %collective-permute-start.5 = (bf16[8,2176]{1,0:T(8,128)(2,1)}, bf16[8,2176]{1,0:T(8,128)(2,1)S(1)}, u32[]{:S(2)}, u32[]{:S(2)}) collective-permute-start(bf16[8,2176]{1,0:T(8,128)(2,1)} %shard_map.86.refs_0_), channel_id=1, source_target_pairs={{0,24},{4,28},{8,0},{12,4},{16,8},{20,12},{24,16},{28,20},{1,25},{... | collective-permute-start | bytes 104456 | tf_op jit(solution)/shard_map/ppermute | solution.py:206
  8.7 0.0 collective-permute-start.4
  8.7 3.0 %collective-permute-start.3 = (bf16[8,2176]{1,0:T(8,128)(2,1)}, bf16[8,2176]{1,0:T(8,128)(2,1)S(1)}, u32[]{:S(2)}, u32[]{:S(2)}) collective-permute-start(bf16[8,2176]{1,0:T(8,128)(2,1)} %shard_map.86.refs_0_), channel_id=1, source_target_pairs={{0,16},{4,20},{8,24},{12,28},{16,0},{20,4},{24,8},{28,12},{1,17},{... | collective-permute-start | bytes 104456 | tf_op jit(solution)/shard_map/ppermute | solution.py:206
  11.7 0.0 collective-permute-start.2
  11.7 0.0 collective-permute-done.6.refs_7_
  11.7 1.9 %collective-permute-start.1 = (bf16[8,2176]{1,0:T(8,128)(2,1)}, bf16[8,2176]{1,0:T(8,128)(2,1)S(1)}, u32[]{:S(2)}, u32[]{:S(2)}) collective-permute-start(bf16[8,2176]{1,0:T(8,128)(2,1)} %shard_map.86.refs_0_), channel_id=1, source_target_pairs={{0,8},{4,12},{8,16},{12,20},{16,24},{20,28},{24,0},{28,4},{1,9},{5... | collective-permute-start | bytes 104456 | tf_op jit(solution)/shard_map/ppermute | solution.py:206
  13.6 0.0 collective-permute-done.5.refs_6_
  13.6 1.1 %collective-permute-start = (bf16[8,2176]{1,0:T(8,128)(2,1)}, bf16[8,2176]{1,0:T(8,128)(2,1)S(1)}, u32[]{:S(2)}, u32[]{:S(2)}) collective-permute-start(bf16[8,2176]{1,0:T(8,128)(2,1)} %shard_map.86.refs_0_), channel_id=1, source_target_pairs={{0,4},{4,8},{8,12},{12,16},{16,20},{20,24},{24,28},{28,0},{1,5},{5... | collective-permute-start | bytes 104456 | tf_op jit(solution)/shard_map/ppermute | solution.py:206
  14.7 0.1 pad_add_fusion.place_ref
  14.8 0.0 copy-start.1
  14.8 0.0 copy-start
  14.8 1.6 %shard_map.85.head_ref = bf16[4096,256]{1,0:T(8,128)(2,1)S(1)} custom-call(bf16[4096,256]{1,0:T(8,128)(2,1)} %head_ref.1), custom_call_target="tpu_custom_call" | custom-call | bytes 4194304 | tf_op jit(solution)/shard_map/pallas_call | solution.py:208
  16.3 0.0 collective-permute-done.4.refs_5_
  16.4 0.0 collective-permute-done.3.refs_4_
  16.4 1.6 %collective-permute-done.2.refs_3_ = bf16[8,2176]{1,0:T(8,128)(2,1)S(1)} collective-permute-done((bf16[8,2176]{1,0:T(8,128)(2,1)}, bf16[8,2176]{1,0:T(8,128)(2,1)S(1)}, u32[]{:S(2)}, u32[]{:S(2)}) %collective-permute-start.2) | collective-permute-done | bytes 34848 | tf_op jit(solution)/shard_map/ppermute | solution.py:206
  18.0 1.0 %collective-permute-done.1.refs_2_ = bf16[8,2176]{1,0:T(8,128)(2,1)S(1)} collective-permute-done((bf16[8,2176]{1,0:T(8,128)(2,1)}, bf16[8,2176]{1,0:T(8,128)(2,1)S(1)}, u32[]{:S(2)}, u32[]{:S(2)}) %collective-permute-start.1) | collective-permute-done | bytes 34848 | tf_op jit(solution)/shard_map/ppermute | solution.py:206
  19.0 1.4 %collective-permute-done.refs_1_ = bf16[8,2176]{1,0:T(8,128)(2,1)S(1)} collective-permute-done((bf16[8,2176]{1,0:T(8,128)(2,1)}, bf16[8,2176]{1,0:T(8,128)(2,1)S(1)}, u32[]{:S(2)}, u32[]{:S(2)}) %collective-permute-start) | collective-permute-done | bytes 34848 | tf_op jit(solution)/shard_map/ppermute | solution.py:206
  20.4 0.0 copy-done.1
  20.4 0.0 copy-done
  20.4 1.2 %shard_map.87 = (f32[1,128]{1,0:T(1,128)S(1)}, f32[8,128]{1,0:T(8,128)S(1)}) custom-call(s32[2]{0:T(128)S(1)} %pad_add_fusion.place_ref, bf16[4096,256]{1,0:T(8,128)(2,1)S(1)} %shard_map.85.head_ref, bf16[8,2176]{1,0:T(8,128)(2,1)S(1)} %copy-done, bf16[8,2176]{1,0:T(8,128)(2,1)S(1)} %collective-permute-done.refs_1_, ...), custom_call_target="tpu_custom_call" | custom-call | tf_op jit(solution)/shard_map/pallas_call | solution.py:216
  21.6 9.9 %all_to_all.5 = f32[32,1,128]{2,1,0:T(1,128)} all-to-all(f32[32,1,128]{2,1,0:T(1,128)S(1)} %broadcast_in_dim.9), channel_id=1, replica_groups=mesh['req'=8,'tp'=4] {'req','tp'}, dimensions={0} | all-to-all | bytes 32768 | tf_op jit(solution)/shard_map/all_to_all | solution.py:179
  31.5 1.4 %shard_map.88 = (f32[8]{0:T(128)}, f32[8]{0:T(128)}, f32[4]{0:T(128)}) custom-call(s32[2]{0:T(128)} %copy-done.1, s32[8]{0:T(128)} %scored_ref.3, f32[32,128]{1,0:T(8,128)} %bitcast.6, f32[8,128]{1,0:T(8,128)S(1)} %get-tuple-element.6.meta_ref), custom_call_target="tpu_custom_call" | custom-call | tf_op jit(solution)/shard_map/pallas_call | solution.py:228
  (1 shorter events, 0.0 us)
Async XLA Ops:
  2.3 9.4 %collective-permute-start.6 = (bf16[8,2176]{1,0:T(8,128)(2,1)}, bf16[8,2176]{1,0:T(8,128)(2,1)S(1)}, u32[]{:S(2)}, u32[]{:S(2)}) collective-permute-start(bf16[8,2176]{1,0:T(8,128)(2,1)} %shard_map.86.refs_0_), channel_id=1, source_target_pairs={{0,28},{4,0},{8,4},{12,8},{16,12},{20,16},{24,20},{28,24},{1,29},{... | collective-permute-start | bytes 104456 | tf_op jit(solution)/shard_map/ppermute | solution.py:206
  8.3 5.3 %collective-permute-start.5 = (bf16[8,2176]{1,0:T(8,128)(2,1)}, bf16[8,2176]{1,0:T(8,128)(2,1)S(1)}, u32[]{:S(2)}, u32[]{:S(2)}) collective-permute-start(bf16[8,2176]{1,0:T(8,128)(2,1)} %shard_map.86.refs_0_), channel_id=1, source_target_pairs={{0,24},{4,28},{8,0},{12,4},{16,8},{20,12},{24,16},{28,20},{1,25},{... | collective-permute-start | bytes 104456 | tf_op jit(solution)/shard_map/ppermute | solution.py:206
  8.7 7.6 %collective-permute-start.4 = (bf16[8,2176]{1,0:T(8,128)(2,1)}, bf16[8,2176]{1,0:T(8,128)(2,1)S(1)}, u32[]{:S(2)}, u32[]{:S(2)}) collective-permute-start(bf16[8,2176]{1,0:T(8,128)(2,1)} %shard_map.86.refs_0_), channel_id=1, source_target_pairs={{0,20},{4,24},{8,28},{12,0},{16,4},{20,8},{24,12},{28,16},{1,21},{... | collective-permute-start | bytes 104456 | tf_op jit(solution)/shard_map/ppermute | solution.py:206
  8.7 7.6 %collective-permute-start.3 = (bf16[8,2176]{1,0:T(8,128)(2,1)}, bf16[8,2176]{1,0:T(8,128)(2,1)S(1)}, u32[]{:S(2)}, u32[]{:S(2)}) collective-permute-start(bf16[8,2176]{1,0:T(8,128)(2,1)} %shard_map.86.refs_0_), channel_id=1, source_target_pairs={{0,16},{4,20},{8,24},{12,28},{16,0},{20,4},{24,8},{28,12},{1,17},{... | collective-permute-start | bytes 104456 | tf_op jit(solution)/shard_map/ppermute | solution.py:206
  11.7 6.3 %collective-permute-start.2 = (bf16[8,2176]{1,0:T(8,128)(2,1)}, bf16[8,2176]{1,0:T(8,128)(2,1)S(1)}, u32[]{:S(2)}, u32[]{:S(2)}) collective-permute-start(bf16[8,2176]{1,0:T(8,128)(2,1)} %shard_map.86.refs_0_), channel_id=1, source_target_pairs={{0,12},{4,16},{8,20},{12,24},{16,28},{20,0},{24,4},{28,8},{1,13},{... | collective-permute-start | bytes 104456 | tf_op jit(solution)/shard_map/ppermute | solution.py:206
  11.7 7.3 %collective-permute-start.1 = (bf16[8,2176]{1,0:T(8,128)(2,1)}, bf16[8,2176]{1,0:T(8,128)(2,1)S(1)}, u32[]{:S(2)}, u32[]{:S(2)}) collective-permute-start(bf16[8,2176]{1,0:T(8,128)(2,1)} %shard_map.86.refs_0_), channel_id=1, source_target_pairs={{0,8},{4,12},{8,16},{12,20},{16,24},{20,28},{24,0},{28,4},{1,9},{5... | collective-permute-start | bytes 104456 | tf_op jit(solution)/shard_map/ppermute | solution.py:206
  13.6 6.8 %collective-permute-start = (bf16[8,2176]{1,0:T(8,128)(2,1)}, bf16[8,2176]{1,0:T(8,128)(2,1)S(1)}, u32[]{:S(2)}, u32[]{:S(2)}) collective-permute-start(bf16[8,2176]{1,0:T(8,128)(2,1)} %shard_map.86.refs_0_), channel_id=1, source_target_pairs={{0,4},{4,8},{8,12},{12,16},{16,20},{20,24},{24,28},{28,0},{1,5},{5... | collective-permute-start | bytes 104456 | tf_op jit(solution)/shard_map/ppermute | solution.py:206
  14.8 5.6 %copy-start.1 = (s32[2]{0:T(128)}, s32[2]{0:T(128)S(1)}, u32[]{:S(2)}) copy-start(s32[2]{0:T(128)S(1)} %pad_add_fusion.place_ref) | copy-start | bytes 28
  14.8 5.6 %copy-start = (bf16[8,2176]{1,0:T(8,128)(2,1)S(1)}, bf16[8,2176]{1,0:T(8,128)(2,1)}, u32[]{:S(2)}) copy-start(bf16[8,2176]{1,0:T(8,128)(2,1)} %shard_map.86.refs_0_) | copy-start | bytes 104452

commit v5 on v3

v5 whole, which is shorter than its diff:
```python
import functools

import jax
import jax.numpy as jnp
from jax import lax
from jax.experimental import pallas as pl
from jax.experimental.pallas import tpu as pltpu
from jax.sharding import PartitionSpec as P

SEQS = 4
PICK = 4
PAIR = 2
MINE = PICK // PAIR
SUBS = 8
LANES = 128
STATS = 4

VMEM = pltpu.VMEM
SMEM = pltpu.SMEM


def ranks_of(scored_ref, row_count):
    ranks, so_far = [], jnp.int32(0)
    for row in range(row_count):
        ranks.append(so_far)
        so_far = so_far + scored_ref[row]
    return ranks, so_far


def iota(shape, axis):
    return lax.broadcasted_iota(jnp.int32, shape, axis)


def pack_kernel(share, hidden_ref, gain_ref, targets_ref, segments_ref, scored_ref, out_ref, wide_ref, parts_ref, gains_ref):
    row_count, width = hidden_ref.shape
    parts = SUBS // MINE
    span = width // parts
    own, half = lax.axis_index("req"), lax.axis_index("tp") % PAIR
    wide_ref[...] = hidden_ref[...].astype(jnp.float32)
    gains_ref[...] = gain_ref[...].astype(jnp.float32)
    ranks, count = ranks_of(scored_ref, row_count)
    source = [jnp.int32(0)] * PICK
    for row in range(row_count):
        for r in range(PICK):
            hit = jnp.logical_and(scored_ref[row] == 1, ranks[row] == r)
            source[r] = jnp.where(hit, row, source[r])
    mine = [source[i] for i in range(MINE)]
    for h in range(1, PAIR):
        mine = [jnp.where(half == h, source[h * MINE + i], mine[i]) for i in range(MINE)]
    for i in range(MINE):
        for k in range(parts):
            parts_ref[k * MINE + i : k * MINE + i + 1, :] = wide_ref[pl.ds(mine[i], 1), k * span : (k + 1) * span]
    values = parts_ref[...]
    part = jnp.broadcast_to(jnp.sum(values * values, axis=1, keepdims=True), (SUBS, LANES))
    total = part
    for k in range(1, parts):
        total = total + pltpu.roll(part, k * MINE, 0)
    row_scale = lax.rsqrt(total / width + 1e-05)
    sub, lane = iota((SUBS, LANES), 0), iota((SUBS, LANES), 1)
    chunks = span // LANES
    for at in range(chunks):
        gain = gains_ref[at : at + 1, :]
        for k in range(1, parts):
            gain = jnp.where(sub >= k * MINE, gains_ref[k * chunks + at : k * chunks + at + 1, :], gain)
        piece = parts_ref[:, at * LANES : (at + 1) * LANES]
        piece = (piece * row_scale * gain).astype(jnp.bfloat16)
        for to in range(out_ref.shape[0]):
            out_ref[to, :, at * LANES : (at + 1) * LANES] = piece
    width_side = out_ref.shape[2] - span
    sub, lane = iota((SUBS, width_side), 0), iota((SUBS, width_side), 1)
    at_row, at_half = lane % share - own * MINE, lane // share
    side = jnp.zeros((SUBS, width_side), jnp.int32)
    for i in range(MINE):
        target = targets_ref[mine[i]]
        digits = jnp.where(sub == 0, target & 255, jnp.where(sub == 1, (target >> 8) & 255, target >> 16))
        fields = jnp.zeros((SUBS, width_side), jnp.int32)
        for h in range(PAIR):
            r = h * MINE + i
            field = jnp.where(sub == 3, segments_ref[source[r]], (count > r).astype(jnp.int32))
            fields = jnp.where(at_half == h, field, fields)
        side = jnp.where(at_row == i, jnp.where(sub < 3, digits, jnp.where(sub < 5, fields, 0)), side)
    side = side.astype(jnp.float32).astype(jnp.bfloat16)
    for to in range(out_ref.shape[0]):
        out_ref[to, :, span:] = side


def stage_kernel(head_ref, out_ref, sems):
    parts = sems.shape[0]
    depth = head_ref.shape[0] // parts
    copies = [
        pltpu.make_async_copy(head_ref.at[pl.ds(i * depth, depth)], out_ref.at[pl.ds(i * depth, depth)], sems.at[i])
        for i in range(parts)
    ]
    for copy in copies:
        copy.start()
    for copy in copies:
        copy.wait()


def score_kernel(rows_ref, own_ref, other_ref, stats_ref, meta_ref):
    width, cols = own_ref.shape
    groups = rows_ref.shape[0]
    parts = SUBS // MINE
    span = width // parts
    share = groups * MINE
    tp, tp_count = lax.axis_index("tp"), lax.axis_size("tp")
    half = tp % PAIR
    place = lax.axis_index("req") * tp_count + tp
    meta = rows_ref[0, :, span:].astype(jnp.float32)
    for q in range(1, groups):
        meta = meta + rows_ref[q, :, span:].astype(jnp.float32)
    meta_ref[...] = meta
    rows = rows_ref[:, :, :span].reshape(groups * SUBS, span)
    bundle = iota((1, SUBS, 1), 1) // MINE

    def logits_of(head_ref):
        pieces = [
            jnp.dot(rows, head_ref[k * span : (k + 1) * span, :], preferred_element_type=jnp.float32).reshape(
                groups // parts, parts, SUBS, cols
            )
            for k in range(parts)
        ]
        total = None
        for shift in range(parts):
            picked = None
            for k in range(parts):
                piece = pieces[k][:, (k + shift) % parts]
                picked = piece if picked is None else jnp.where(bundle == k, piece, picked)
            if shift:
                picked = jnp.concatenate(
                    [pltpu.roll(picked[a], shift * MINE, 0)[None] for a in range(groups // parts)], axis=0
                )
            total = picked if total is None else total + picked
        return total.reshape(share, cols)

    logits = jnp.concatenate([logits_of(own_ref), logits_of(other_ref)], axis=1)
    copies = max(1, LANES // share)
    if copies > 1:
        logits = jnp.concatenate([logits] * copies, axis=0)
    logits = logits.T
    lanes = logits.shape[1]
    ids = (meta[0:1, :lanes] + 256.0 * meta[1:2, :lanes] + 65536.0 * meta[2:3, :lanes]).astype(jnp.int32)
    row_top = jnp.max(logits, axis=0, keepdims=True)
    scaled = jnp.exp(logits - row_top)
    row_total = jnp.sum(scaled, axis=0, keepdims=True)
    row_weighted = jnp.sum(scaled * logits, axis=0, keepdims=True)
    column = iota(logits.shape, 0)
    other = place - half + (half + 1) % PAIR
    columns = jnp.where(column < cols, place * cols, (other - 1) * cols) + column
    picked = jnp.sum(jnp.where(columns == ids, logits, 0.0), axis=0, keepdims=True)
    stats = (row_top, row_total, row_weighted, picked)
    if copies > 1:
        lane = iota((1, LANES), 1)
        joined = picked
        for at in range(STATS - 1):
            joined = jnp.where(lane // (PAIR * share) == at, stats[at], joined)
        neutral = jnp.where(lane < PAIR * share, -jnp.inf, 0.0)
        stats_ref[...] = jnp.where(lane // share % PAIR == half, joined, neutral)
    else:
        for at in range(STATS):
            for h in range(PAIR):
                first = (at * PAIR + h) * share
                stats_ref[:, first : first + share] = jnp.where(half == h, stats[at], 0.0 if at else -jnp.inf)


def finish_kernel(share, scored_ref, stats_ref, meta_ref, logprob_ref, entropy_ref, seq_ref):
    row_count = scored_ref.shape[0]
    used = PAIR * share
    lanes = max(used, LANES)

    def stat(at):
        if used >= LANES:
            return stats_ref[:, at * used : (at + 1) * used]
        return stats_ref[...] if at == 0 else pltpu.roll(stats_ref[...], LANES - at * used, 1)

    tops = stat(0)
    row_top = jnp.max(tops, axis=0, keepdims=True)
    weight = jnp.exp(tops - row_top)
    row_total = jnp.sum(stat(1) * weight, axis=0, keepdims=True)
    row_weighted = jnp.sum(stat(2) * weight, axis=0, keepdims=True)
    picked = jnp.sum(stat(3), axis=0, keepdims=True)
    log_norm = row_top + jnp.log(row_total)
    in_use = jnp.logical_and(meta_ref[4:5, :] > 0.5, iota((1, lanes), 1) < used)
    logprob = jnp.where(in_use, picked - log_norm, 0.0)
    entropy = jnp.where(in_use, log_norm - row_weighted / row_total, 0.0)
    sub, lane = iota((SUBS, LANES), 0), iota((SUBS, LANES), 1)
    segment = meta_ref[3:4, :].astype(jnp.int32)
    sums = jnp.sum(jnp.where(segment == iota((SUBS, lanes), 0), logprob, 0.0), axis=1, keepdims=True)
    seqs = jnp.sum(jnp.where(sub == lane, sums, 0.0), axis=0, keepdims=True)
    seq_ref[...] = seqs[0, :SEQS]
    ranks, _ = ranks_of(scored_ref, row_count)
    rank = jnp.zeros((SUBS, LANES), jnp.int32)
    keep = jnp.zeros((SUBS, LANES), jnp.int32)
    for row in range(row_count):
        rank = jnp.where(lane == row, ranks[row], rank)
        keep = jnp.where(lane == row, scored_ref[row], keep)
    mine = jnp.zeros((SUBS, LANES), jnp.float32)
    for h in range(PAIR):
        first = h * share + lax.axis_index("req") * MINE
        block = first // LANES
        own_logprob, own_entropy = logprob[:, :LANES], entropy[:, :LANES]
        for at in range(1, lanes // LANES):
            piece = slice(at * LANES, (at + 1) * LANES)
            own_logprob = jnp.where(block == at, logprob[:, piece], own_logprob)
            own_entropy = jnp.where(block == at, entropy[:, piece], own_entropy)
        both = jnp.where(sub == 0, own_logprob, own_entropy)
        both = jnp.take_along_axis(both, first - block * LANES + rank % MINE, axis=1)
        mine = jnp.where(jnp.logical_and(rank // MINE == h, keep == 1), both, mine)
    logprob_ref[...] = mine[0, :row_count]
    entropy_ref[...] = mine[1, :row_count]


def local(hidden, norm_gain, lm_head, targets, segments, scored):
    row_count, width = hidden.shape
    groups, tp_count = lax.axis_size("req"), lax.axis_size("tp")
    span = width * MINE // SUBS
    share = groups * MINE
    lanes = max(PAIR * share, LANES)

    def spec(space):
        return pl.BlockSpec(memory_space=space)

    other = lax.ppermute(lm_head, "tp", [(i, i + 1 - 2 * (i % PAIR)) for i in range(tp_count)])
    packed = pl.pallas_call(
        functools.partial(pack_kernel, share),
        out_shape=jax.ShapeDtypeStruct((groups, SUBS, span + lanes), jnp.bfloat16),
        in_specs=[spec(VMEM)] * 2 + [spec(SMEM)] * 3,
        out_specs=spec(VMEM),
        scratch_shapes=[
            VMEM((row_count, width), jnp.float32),
            VMEM((SUBS, span), jnp.float32),
            VMEM((width // LANES, LANES), jnp.float32),
        ],
    )(hidden, norm_gain.reshape(width // LANES, LANES), targets, segments, scored)
    rows = lax.all_to_all(packed, "req", 0, 0)
    head = pl.pallas_call(
        stage_kernel,
        out_shape=VMEM(lm_head.shape, lm_head.dtype),
        in_specs=[spec(pltpu.HBM)],
        out_specs=spec(VMEM),
        scratch_shapes=[pltpu.SemaphoreType.DMA((4,))],
        cost_estimate=pl.CostEstimate(flops=0, bytes_accessed=2 * lm_head.size * 2, transcendentals=0),
    )(pltpu.with_memory_space_constraint(lm_head, pltpu.HBM))
    stats, meta = pl.pallas_call(
        score_kernel,
        out_shape=(
            jax.ShapeDtypeStruct((1, STATS * PAIR * share), jnp.float32),
            VMEM((SUBS, lanes), jnp.float32),
        ),
        in_specs=[spec(VMEM)] * 3,
        out_specs=(spec(VMEM), spec(VMEM)),
        compiler_params=pltpu.CompilerParams(vmem_limit_bytes=40 * 1024 * 1024),
    )(rows, pltpu.with_memory_space_constraint(head, VMEM), other)
    gathered = sent_to_all(stats, ("req", "tp"))
    return pl.pallas_call(
        functools.partial(finish_kernel, share),
        out_shape=(
            jax.ShapeDtypeStruct((row_count,), jnp.float32),
            jax.ShapeDtypeStruct((row_count,), jnp.float32),
            jax.ShapeDtypeStruct((SEQS,), jnp.float32),
        ),
        in_specs=[spec(SMEM), spec(VMEM), spec(VMEM)],
        out_specs=(spec(VMEM), spec(VMEM), spec(VMEM)),
    )(scored, gathered, pltpu.with_memory_space_constraint(meta, VMEM))


def sent_to_all(block, axis):
    copies = jnp.broadcast_to(block[None], (lax.axis_size(axis),) + block.shape)
    return lax.all_to_all(copies, axis, 0, 0).reshape((-1,) + block.shape[1:])


def solution(mesh):
    return jax.shard_map(
        local,
        mesh=mesh,
        in_specs=(P("req", None), P(), P(None, ("req", "tp")), P("req"), P("req"), P("req")),
        out_specs=(P("req"), P("req"), P()),
        check_vma=False,
    )
```

time: 32.4 us -> 31.8 us (0.981)
  Pallas kernels: 5.9 us -> 7.28 us
  waiting for transfers between devices: 7.63 us -> 6.33 us
  blocking collectives: 10.5 us -> 9.75 us
    pallas_call x1, Pallas kernels: 1.18 us -> 2.63 us  [local(): pl.pallas_call(score_kernel, out_shape=(jax.ShapeDtypeStruct((1, STATS *...]
    all_to_all x1, waiting for transfers between devices: 7.63 us -> 6.32 us  [local(): rows = lax.all_to_all(packed, 'req', 0, 0)]
    all_to_all x1, blocking collectives: 10.5 us -> 9.75 us  [sent_to_all(): return lax.all_to_all(copies, axis, 0, 0).reshape((-1,) + block.shape[1:])]
    ppermute x0 -> x1, starting transfers between devices: none -> 0.52 us  [local(): lax.ppermute(lm_head, 'tp', [(i, i + 1 - 2 * (i % PAIR)) for i in range(t...]
    all_to_all x1, starting transfers between devices: 7.28 us -> 6.85 us  [local(): rows = lax.all_to_all(packed, 'req', 0, 0)]
  transfers between devices with their start and end apart: 1 -> 2, of which waited for: 1 -> 1; matrix products, arithmetic and copies ran while one was open for 0% -> 0% of each run, Pallas kernels for 5% -> 10%
where the time goes in v5:
time: 31.8 us; the launch traced here: 31.4 us
  blocking collectives  9.75 us (31%)
  starting transfers between devices  7.36 us (23%)
  Pallas kernels  7.28 us (23%)
  waiting for transfers between devices  6.33 us (20%)
  between operations  0.65 us (2%)
    all_to_all x1, blocking collectives, sent_to_all(): return lax.all_to_all(copies, axis, 0, 0).reshape((-1,) + block.shape[1:])  9.75 us
    all_to_all x1, starting transfers between devices, local(): rows = lax.all_to_all(packed, 'req', 0, 0)  6.85 us
    all_to_all x1, waiting for transfers between devices, local(): rows = lax.all_to_all(packed, 'req', 0, 0)  6.32 us
    pallas_call x1, Pallas kernels, local(): pl.pallas_call(score_kernel, out_shape=(jax.ShapeDtypeStruct((1, STATS *...  2.63 us
    pallas_call x1, Pallas kernels, local(): pl.pallas_call(functools.partial(pack_kernel, share), out_shape=jax.Shape...  1.69 us
    pallas_call x1, Pallas kernels, local(): pl.pallas_call(stage_kernel, out_shape=VMEM(lm_head.shape, lm_head.dtype)...  1.55 us
    pallas_call x1, Pallas kernels, local(): pl.pallas_call(functools.partial(finish_kernel, share), out_shape=(jax.Sh...  1.41 us
  transfers between devices with their start and end apart: 2, of which 1 were waited for; matrix products, arithmetic and copies ran while one was open for 0% of the time, Pallas kernels for 10%

profile of v5, /device:TPU:0, one launch (start us, length us, event | category | flops | bytes accessed | tf_op | source)
XLA Modules:
  0.0 31.4 jit_solution(17091755164857245550)
XLA Ops:
  0.6 0.5 %collective-permute-start = (bf16[4096,256]{1,0:T(8,128)(2,1)}, bf16[4096,256]{1,0:T(8,128)(2,1)}, u32[]{:S(2)}, u32[]{:S(2)}) collective-permute-start(bf16[4096,256]{1,0:T(8,128)(2,1)} %head_ref.1), channel_id=1, source_target_pairs={{0,1},{1,0},{2,3},{3,2},{4,5},{5,4},{6,7},{7,6},{8,9},{9,8},{10,11... | collective-permute-start | bytes 6291464 | tf_op jit(solution)/shard_map/ppermute | solution.py:223
  1.1 1.7 %shard_map.85 = bf16[8,8,1152]{2,1,0:T(8,128)(2,1)} custom-call(bf16[8,4096]{1,0:T(8,128)(2,1)} %hidden_ref.1, bf16[32,128]{1,0:T(8,128)(2,1)} %bitcast.5, s32[8]{0:T(128)} %targets_ref.1, s32[8]{0:T(128)} %segments_ref.1, s32[8]{0:T(128)} %scored_ref.3), custom_call_target="tpu_custom_call" | custom-call | tf_op jit(solution)/shard_map/pallas_call | solution.py:224
  2.8 6.8 %all-to-all-start = ((bf16[8,8,1152]{2,1,0:T(8,128)(2,1)}), bf16[8,8,1152]{2,1,0:T(8,128)(2,1)S(1)}, u32[]{:S(2)}, u32[]{:S(2)}) async-start(bf16[8,8,1152]{2,1,0:T(8,128)(2,1)} %shard_map.85), calls=%async_computation | async-start | bytes 294912 | tf_op jit(solution)/shard_map/all_to_all | solution.py:235
  9.7 1.5 %shard_map.86.own_ref = bf16[4096,256]{1,0:T(8,128)(2,1)S(1)} custom-call(bf16[4096,256]{1,0:T(8,128)(2,1)} %head_ref.1), custom_call_target="tpu_custom_call" | custom-call | bytes 4194304 | tf_op jit(solution)/shard_map/pallas_call | solution.py:236
  11.2 6.3 %all-to-all-done.rows_ref = bf16[8,8,1152]{2,1,0:T(8,128)(2,1)S(1)} async-done(((bf16[8,8,1152]{2,1,0:T(8,128)(2,1)}), bf16[8,8,1152]{2,1,0:T(8,128)(2,1)S(1)}, u32[]{:S(2)}, u32[]{:S(2)}) %all-to-all-start) | async-done | bytes 147488 | tf_op jit(solution)/shard_map/all_to_all | solution.py:235
  17.6 0.0 collective-permute-done.other_ref
  17.6 2.6 %shard_map.87 = (f32[1,128]{1,0:T(1,128)S(1)}, f32[8,128]{1,0:T(8,128)S(1)}) custom-call(bf16[8,8,1152]{2,1,0:T(8,128)(2,1)S(1)} %all-to-all-done.rows_ref, bf16[4096,256]{1,0:T(8,128)(2,1)S(1)} %shard_map.86.own_ref, bf16[4096,256]{1,0:T(8,128)(2,1)} %collective-permute-done.other_ref), custom_call_target="tpu_custom_call" | custom-call | tf_op jit(solution)/shard_map/pallas_call | solution.py:244
  20.2 9.8 %all_to_all.10 = f32[32,1,128]{2,1,0:T(1,128)} all-to-all(f32[32,1,128]{2,1,0:T(1,128)S(1)} %broadcast_in_dim.9), channel_id=1, replica_groups=mesh['req'=8,'tp'=4] {'req','tp'}, dimensions={0} | all-to-all | bytes 32768 | tf_op jit(solution)/shard_map/all_to_all | solution.py:269
  30.0 1.4 %shard_map.88 = (f32[8]{0:T(128)}, f32[8]{0:T(128)}, f32[4]{0:T(128)}) custom-call(s32[8]{0:T(128)} %scored_ref.3, f32[32,128]{1,0:T(8,128)} %bitcast.4, f32[8,128]{1,0:T(8,128)S(1)} %get-tuple-element.6.meta_ref), custom_call_target="tpu_custom_call" | custom-call | tf_op jit(solution)/shard_map/pallas_call | solution.py:255
  (1 shorter events, 0.0 us)
Async XLA Ops:
  0.6 16.9 %collective-permute-start = (bf16[4096,256]{1,0:T(8,128)(2,1)}, bf16[4096,256]{1,0:T(8,128)(2,1)}, u32[]{:S(2)}, u32[]{:S(2)}) collective-permute-start(bf16[4096,256]{1,0:T(8,128)(2,1)} %head_ref.1), channel_id=1, source_target_pairs={{0,1},{1,0},{2,3},{3,2},{4,5},{5,4},{6,7},{7,6},{8,9},{9,8},{10,11... | collective-permute-start | bytes 6291464 | tf_op jit(solution)/shard_map/ppermute | solution.py:223
  2.8 14.7 %all-to-all-start = ((bf16[8,8,1152]{2,1,0:T(8,128)(2,1)}), bf16[8,8,1152]{2,1,0:T(8,128)(2,1)S(1)}, u32[]{:S(2)}, u32[]{:S(2)}) async-start(bf16[8,8,1152]{2,1,0:T(8,128)(2,1)} %shard_map.85), calls=%async_computation | async-start | bytes 294912 | tf_op jit(solution)/shard_map/all_to_all | solution.py:235

commit v6 on v5

--- a/solution.py
+++ b/solution.py
@@ -97,7 +97,7 @@
         copy.wait()
 
 
-def score_kernel(rows_ref, own_ref, other_ref, stats_ref, meta_ref):
+def score_kernel(rows_ref, own_ref, other_ref, stats_ref, meta_ref, ordered_ref):
     width, cols = own_ref.shape
     groups = rows_ref.shape[0]
     parts = SUBS // MINE
@@ -106,61 +106,49 @@
     tp, tp_count = lax.axis_index("tp"), lax.axis_size("tp")
     half = tp % PAIR
     place = lax.axis_index("req") * tp_count + tp
+    count = groups * SUBS
+    into, out_of = iota((count, count), 0), iota((count, count), 1)
+    wanted = into % share // MINE * SUBS + into // share * MINE + into % MINE
+    order = jnp.where(out_of == wanted, 1.0, 0.0).astype(jnp.bfloat16)
+    rows = rows_ref[:, :, :span].reshape(count, span)
+    ordered = jnp.dot(order, rows, preferred_element_type=jnp.float32).astype(jnp.bfloat16)
+    for k in range(parts):
+        ordered_ref[:, k * span : (k + 1) * span] = ordered[k * share : (k + 1) * share]
     meta = rows_ref[0, :, span:].astype(jnp.float32)
     for q in range(1, groups):
         meta = meta + rows_ref[q, :, span:].astype(jnp.float32)
     meta_ref[...] = meta
-    rows = rows_ref[:, :, :span].reshape(groups * SUBS, span)
-    bundle = iota((1, SUBS, 1), 1) // MINE
-
-    def logits_of(head_ref):
-        pieces = [
-            jnp.dot(rows, head_ref[k * span : (k + 1) * span, :], preferred_element_type=jnp.float32).reshape(
-                groups // parts, parts, SUBS, cols
-            )
-            for k in range(parts)
-        ]
-        total = None
-        for shift in range(parts):
-            picked = None
-            for k in range(parts):
-                piece = pieces[k][:, (k + shift) % parts]
-                picked = piece if picked is None else jnp.where(bundle == k, piece, picked)
-            if shift:
-                picked = jnp.concatenate(
-                    [pltpu.roll(picked[a], shift * MINE, 0)[None] for a in range(groups // parts)], axis=0
-                )
-            total = picked if total is None else total + picked
-        return total.reshape(share, cols)
-
-    logits = jnp.concatenate([logits_of(own_ref), logits_of(other_ref)], axis=1)
-    copies = max(1, LANES // share)
-    if copies > 1:
-        logits = jnp.concatenate([logits] * copies, axis=0)
-    logits = logits.T
-    lanes = logits.shape[1]
-    ids = (meta[0:1, :lanes] + 256.0 * meta[1:2, :lanes] + 65536.0 * meta[2:3, :lanes]).astype(jnp.int32)
-    row_top = jnp.max(logits, axis=0, keepdims=True)
+    logits = jnp.concatenate(
+        [jnp.dot(ordered_ref[...], head[...], preferred_element_type=jnp.float32) for head in (own_ref, other_ref)],
+        axis=1,
+    )
+    lanes = max(share, LANES)
+    sub, lane = iota((share, lanes), 0), iota((share, lanes), 1)
+    ids = meta[0:1, :lanes] + 256.0 * meta[1:2, :lanes] + 65536.0 * meta[2:3, :lanes]
+    ids = jnp.sum(jnp.where(lane == sub, ids, 0.0), axis=1, keepdims=True).astype(jnp.int32)
+    row_top = jnp.max(logits, axis=1, keepdims=True)
     scaled = jnp.exp(logits - row_top)
-    row_total = jnp.sum(scaled, axis=0, keepdims=True)
-    row_weighted = jnp.sum(scaled * logits, axis=0, keepdims=True)
-    column = iota(logits.shape, 0)
-    other = place - half + (half + 1) % PAIR
+    row_total = jnp.sum(scaled, axis=1, keepdims=True)
+    row_weighted = jnp.sum(scaled * logits, axis=1, keepdims=True)
+    column = iota(logits.shape, 1)
+    other = place + 1 - 2 * half
     columns = jnp.where(column < cols, place * cols, (other - 1) * cols) + column
-    picked = jnp.sum(jnp.where(columns == ids, logits, 0.0), axis=0, keepdims=True)
+    picked = jnp.sum(jnp.where(columns == ids, logits, 0.0), axis=1, keepdims=True)
     stats = (row_top, row_total, row_weighted, picked)
-    if copies > 1:
-        lane = iota((1, LANES), 1)
+    if PAIR * share * STATS == LANES:
         joined = picked
         for at in range(STATS - 1):
             joined = jnp.where(lane // (PAIR * share) == at, stats[at], joined)
+        joined = jnp.sum(jnp.where(lane % share == sub, joined, 0.0), axis=0, keepdims=True)
+        lane = iota((1, LANES), 1)
         neutral = jnp.where(lane < PAIR * share, -jnp.inf, 0.0)
         stats_ref[...] = jnp.where(lane // share % PAIR == half, joined, neutral)
     else:
         for at in range(STATS):
+            line = jnp.sum(jnp.where(lane == sub, stats[at], 0.0), axis=0, keepdims=True)
             for h in range(PAIR):
                 first = (at * PAIR + h) * share
-                stats_ref[:, first : first + share] = jnp.where(half == h, stats[at], 0.0 if at else -jnp.inf)
+                stats_ref[:, first : first + share] = jnp.where(half == h, line, 0.0 if at else -jnp.inf)
 
 
 def finish_kernel(share, scored_ref, stats_ref, meta_ref, logprob_ref, entropy_ref, seq_ref):
@@ -223,7 +211,7 @@
     other = lax.ppermute(lm_head, "tp", [(i, i + 1 - 2 * (i % PAIR)) for i in range(tp_count)])
     packed = pl.pallas_call(
         functools.partial(pack_kernel, share),
-        out_shape=jax.ShapeDtypeStruct((groups, SUBS, span + lanes), jnp.bfloat16),
+        out_shape=VMEM((groups, SUBS, span + lanes), jnp.bfloat16),
         in_specs=[spec(VMEM)] * 2 + [spec(SMEM)] * 3,
         out_specs=spec(VMEM),
         scratch_shapes=[
@@ -249,6 +237,7 @@
         ),
         in_specs=[spec(VMEM)] * 3,
         out_specs=(spec(VMEM), spec(VMEM)),
+        scratch_shapes=[VMEM((share, width), jnp.bfloat16)],
         compiler_params=pltpu.CompilerParams(vmem_limit_bytes=40 * 1024 * 1024),
     )(rows, pltpu.with_memory_space_constraint(head, VMEM), other)
     gathered = sent_to_all(stats, ("req", "tp"))
@@ -261,7 +250,7 @@
         ),
         in_specs=[spec(SMEM), spec(VMEM), spec(VMEM)],
         out_specs=(spec(VMEM), spec(VMEM), spec(VMEM)),
-    )(scored, gathered, pltpu.with_memory_space_constraint(meta, VMEM))
+    )(scored, pltpu.with_memory_space_constraint(gathered, VMEM), pltpu.with_memory_space_constraint(meta, VMEM))
 
 
 def sent_to_all(block, axis):

time: 31.8 us -> 31.6 us (level)
  no operation moved by 1% of the time
where the time goes in v6:
time: 31.6 us; the launch traced here: 31.3 us
  blocking collectives  9.8 us (31%)
  starting transfers between devices  7.36 us (23%)
  Pallas kernels  7.11 us (22%)
  waiting for transfers between devices  6.33 us (20%)
  between operations  0.65 us (2%)
    all_to_all x1, blocking collectives, sent_to_all(): return lax.all_to_all(copies, axis, 0, 0).reshape((-1,) + block.shape[1:])  9.8 us
    all_to_all x1, starting transfers between devices, local(): rows = lax.all_to_all(packed, 'req', 0, 0)  6.85 us
    all_to_all x1, waiting for transfers between devices, local(): rows = lax.all_to_all(packed, 'req', 0, 0)  6.32 us
    pallas_call x1, Pallas kernels, local(): pl.pallas_call(score_kernel, out_shape=(jax.ShapeDtypeStruct((1, STATS *...  2.52 us
    pallas_call x1, Pallas kernels, local(): pl.pallas_call(functools.partial(pack_kernel, share), out_shape=VMEM((gro...  1.69 us
    pallas_call x1, Pallas kernels, local(): pl.pallas_call(stage_kernel, out_shape=VMEM(lm_head.shape, lm_head.dtype)...  1.55 us
    pallas_call x1, Pallas kernels, local(): pl.pallas_call(functools.partial(finish_kernel, share), out_shape=(jax.Sh...  1.35 us
  transfers between devices with their start and end apart: 2, of which 1 were waited for; matrix products, arithmetic and copies ran while one was open for 0% of the time, Pallas kernels for 10%

profile of v6, /device:TPU:0, one launch (start us, length us, event | category | flops | bytes accessed | tf_op | source)
XLA Modules:
  0.0 31.3 jit_solution(16530147718434508716)
XLA Ops:
  0.6 0.5 %collective-permute-start = (bf16[4096,256]{1,0:T(8,128)(2,1)}, bf16[4096,256]{1,0:T(8,128)(2,1)}, u32[]{:S(2)}, u32[]{:S(2)}) collective-permute-start(bf16[4096,256]{1,0:T(8,128)(2,1)} %head_ref.1), channel_id=1, source_target_pairs={{0,1},{1,0},{2,3},{3,2},{4,5},{5,4},{6,7},{7,6},{8,9},{9,8},{10,11... | collective-permute-start | bytes 6291464 | tf_op jit(solution)/shard_map/ppermute | solution.py:211
  1.1 1.7 %shard_map.85 = bf16[8,8,1152]{2,1,0:T(8,128)(2,1)} custom-call(bf16[8,4096]{1,0:T(8,128)(2,1)} %hidden_ref.1, bf16[32,128]{1,0:T(8,128)(2,1)} %bitcast.5, s32[8]{0:T(128)} %targets_ref.1, s32[8]{0:T(128)} %segments_ref.1, s32[8]{0:T(128)} %scored_ref.3), custom_call_target="tpu_custom_call" | custom-call | tf_op jit(solution)/shard_map/pallas_call | solution.py:212
  2.8 6.8 %all-to-all-start = ((bf16[8,8,1152]{2,1,0:T(8,128)(2,1)}), bf16[8,8,1152]{2,1,0:T(8,128)(2,1)S(1)}, u32[]{:S(2)}, u32[]{:S(2)}) async-start(bf16[8,8,1152]{2,1,0:T(8,128)(2,1)} %shard_map.85), calls=%async_computation | async-start | bytes 294912 | tf_op jit(solution)/shard_map/all_to_all | solution.py:223
  9.7 1.5 %shard_map.86.own_ref = bf16[4096,256]{1,0:T(8,128)(2,1)S(1)} custom-call(bf16[4096,256]{1,0:T(8,128)(2,1)} %head_ref.1), custom_call_target="tpu_custom_call" | custom-call | bytes 4194304 | tf_op jit(solution)/shard_map/pallas_call | solution.py:224
  11.2 6.3 %all-to-all-done.rows_ref = bf16[8,8,1152]{2,1,0:T(8,128)(2,1)S(1)} async-done(((bf16[8,8,1152]{2,1,0:T(8,128)(2,1)}), bf16[8,8,1152]{2,1,0:T(8,128)(2,1)S(1)}, u32[]{:S(2)}, u32[]{:S(2)}) %all-to-all-start) | async-done | bytes 147488 | tf_op jit(solution)/shard_map/all_to_all | solution.py:223
  17.6 0.0 collective-permute-done.other_ref
  17.6 2.5 %shard_map.87 = (f32[1,128]{1,0:T(1,128)S(1)}, f32[8,128]{1,0:T(8,128)S(1)}) custom-call(bf16[8,8,1152]{2,1,0:T(8,128)(2,1)S(1)} %all-to-all-done.rows_ref, bf16[4096,256]{1,0:T(8,128)(2,1)S(1)} %shard_map.86.own_ref, bf16[4096,256]{1,0:T(8,128)(2,1)} %collective-permute-done.other_ref), custom_call_target="tpu_custom_call" | custom-call | tf_op jit(solution)/shard_map/pallas_call | solution.py:232
  20.1 9.8 %all_to_all.10 = f32[32,1,128]{2,1,0:T(1,128)S(1)} all-to-all(f32[32,1,128]{2,1,0:T(1,128)S(1)} %broadcast_in_dim.9), channel_id=1, replica_groups=mesh['req'=8,'tp'=4] {'req','tp'}, dimensions={0} | all-to-all | bytes 32768 | tf_op jit(solution)/shard_map/all_to_all | solution.py:258
  29.9 1.3 %shard_map.88 = (f32[8]{0:T(128)}, f32[8]{0:T(128)}, f32[4]{0:T(128)}) custom-call(s32[8]{0:T(128)} %scored_ref.3, f32[32,128]{1,0:T(8,128)S(1)} %bitcast.3, f32[8,128]{1,0:T(8,128)S(1)} %get-tuple-element.6.meta_ref), custom_call_target="tpu_custom_call" | custom-call | tf_op jit(solution)/shard_map/pallas_call | solution.py:244
  (1 shorter events, 0.0 us)
Async XLA Ops:
  0.6 16.9 %collective-permute-start = (bf16[4096,256]{1,0:T(8,128)(2,1)}, bf16[4096,256]{1,0:T(8,128)(2,1)}, u32[]{:S(2)}, u32[]{:S(2)}) collective-permute-start(bf16[4096,256]{1,0:T(8,128)(2,1)} %head_ref.1), channel_id=1, source_target_pairs={{0,1},{1,0},{2,3},{3,2},{4,5},{5,4},{6,7},{7,6},{8,9},{9,8},{10,11... | collective-permute-start | bytes 6291464 | tf_op jit(solution)/shard_map/ppermute | solution.py:211
  2.8 14.7 %all-to-all-start = ((bf16[8,8,1152]{2,1,0:T(8,128)(2,1)}), bf16[8,8,1152]{2,1,0:T(8,128)(2,1)S(1)}, u32[]{:S(2)}, u32[]{:S(2)}) async-start(bf16[8,8,1152]{2,1,0:T(8,128)(2,1)} %shard_map.85), calls=%async_computation | async-start | bytes 294912 | tf_op jit(solution)/shard_map/all_to_all | solution.py:223

commit v7 on v6

--- a/solution.py
+++ b/solution.py
@@ -84,21 +84,31 @@
         out_ref[to, :, span:] = side
 
 
-def stage_kernel(head_ref, out_ref, sems):
-    parts = sems.shape[0]
-    depth = head_ref.shape[0] // parts
+def stage_kernel(own_ref, other_ref, own_out, other_out, sems):
+    copies = []
+    for at, (source, out) in enumerate(((own_ref, own_out), (other_ref, other_out))):
+        depth = out.shape[0] // sems.shape[1]
+        for i in range(sems.shape[1]):
+            piece = pl.ds(i * depth, depth)
+            copies.append(pltpu.make_async_copy(source.at[piece], out.at[piece], sems.at[at, i]))
+    for copy in copies:
+        copy.start()
+    for copy in copies:
+        copy.wait()
+
+
+def score_kernel(rows_ref, own_ref, upper_ref, other_ref, stats_ref, meta_ref, ordered_ref, lower_ref, sems):
+    width, cols = own_ref.shape
+    staged = upper_ref.shape[0]
+    depth = lower_ref.shape[0] // sems.shape[0]
     copies = [
-        pltpu.make_async_copy(head_ref.at[pl.ds(i * depth, depth)], out_ref.at[pl.ds(i * depth, depth)], sems.at[i])
-        for i in range(parts)
+        pltpu.make_async_copy(
+            other_ref.at[pl.ds(staged + i * depth, depth)], lower_ref.at[pl.ds(i * depth, depth)], sems.at[i]
+        )
+        for i in range(sems.shape[0])
     ]
     for copy in copies:
         copy.start()
-    for copy in copies:
-        copy.wait()
-
-
-def score_kernel(rows_ref, own_ref, other_ref, stats_ref, meta_ref, ordered_ref):
-    width, cols = own_ref.shape
     groups = rows_ref.shape[0]
     parts = SUBS // MINE
     span = width // parts
@@ -118,10 +128,12 @@
     for q in range(1, groups):
         meta = meta + rows_ref[q, :, span:].astype(jnp.float32)
     meta_ref[...] = meta
-    logits = jnp.concatenate(
-        [jnp.dot(ordered_ref[...], head[...], preferred_element_type=jnp.float32) for head in (own_ref, other_ref)],
-        axis=1,
-    )
+    own_logits = jnp.dot(ordered_ref[...], own_ref[...], preferred_element_type=jnp.float32)
+    other_logits = jnp.dot(ordered_ref[:, :staged], upper_ref[...], preferred_element_type=jnp.float32)
+    for copy in copies:
+        copy.wait()
+    other_logits += jnp.dot(ordered_ref[:, staged:], lower_ref[...], preferred_element_type=jnp.float32)
+    logits = jnp.concatenate([own_logits, other_logits], axis=1)
     lanes = max(share, LANES)
     sub, lane = iota((share, lanes), 0), iota((share, lanes), 1)
     ids = meta[0:1, :lanes] + 256.0 * meta[1:2, :lanes] + 65536.0 * meta[2:3, :lanes]
@@ -198,6 +210,10 @@
     entropy_ref[...] = mine[1, :row_count]
 
 
+def grant(mebibytes):
+    return pltpu.CompilerParams(vmem_limit_bytes=mebibytes * 1024 * 1024)
+
+
 def local(hidden, norm_gain, lm_head, targets, segments, scored):
     row_count, width = hidden.shape
     groups, tp_count = lax.axis_size("req"), lax.axis_size("tp")
@@ -221,25 +237,32 @@
         ],
     )(hidden, norm_gain.reshape(width // LANES, LANES), targets, segments, scored)
     rows = lax.all_to_all(packed, "req", 0, 0)
-    head = pl.pallas_call(
+    other = pltpu.with_memory_space_constraint(other, pltpu.HBM)
+    staged = width // 2
+    slices = pl.pallas_call(
         stage_kernel,
-        out_shape=VMEM(lm_head.shape, lm_head.dtype),
-        in_specs=[spec(pltpu.HBM)],
-        out_specs=spec(VMEM),
-        scratch_shapes=[pltpu.SemaphoreType.DMA((4,))],
-        cost_estimate=pl.CostEstimate(flops=0, bytes_accessed=2 * lm_head.size * 2, transcendentals=0),
-    )(pltpu.with_memory_space_constraint(lm_head, pltpu.HBM))
+        out_shape=(VMEM(lm_head.shape, lm_head.dtype), VMEM((staged, lm_head.shape[1]), lm_head.dtype)),
+        in_specs=[spec(pltpu.HBM)] * 2,
+        out_specs=(spec(VMEM),) * 2,
+        scratch_shapes=[pltpu.SemaphoreType.DMA((2, 4))],
+        compiler_params=grant(4),
+        cost_estimate=pl.CostEstimate(flops=0, bytes_accessed=3 * 2 * lm_head.size, transcendentals=0),
+    )(pltpu.with_memory_space_constraint(lm_head, pltpu.HBM), other)
     stats, meta = pl.pallas_call(
         score_kernel,
         out_shape=(
             jax.ShapeDtypeStruct((1, STATS * PAIR * share), jnp.float32),
             VMEM((SUBS, lanes), jnp.float32),
         ),
-        in_specs=[spec(VMEM)] * 3,
+        in_specs=[spec(VMEM)] * 3 + [spec(pltpu.HBM)],
         out_specs=(spec(VMEM), spec(VMEM)),
-        scratch_shapes=[VMEM((share, width), jnp.bfloat16)],
-        compiler_params=pltpu.CompilerParams(vmem_limit_bytes=40 * 1024 * 1024),
-    )(rows, pltpu.with_memory_space_constraint(head, VMEM), other)
+        scratch_shapes=[
+            VMEM((share, width), jnp.bfloat16),
+            VMEM((width - staged, lm_head.shape[1]), jnp.bfloat16),
+            pltpu.SemaphoreType.DMA((4,)),
+        ],
+        compiler_params=grant(24),
+    )(rows, *(pltpu.with_memory_space_constraint(part, VMEM) for part in slices), other)
     gathered = sent_to_all(stats, ("req", "tp"))
     return pl.pallas_call(
         functools.partial(finish_kernel, share),

time: 31.6 us -> 31.1 us (0.984)
  waiting for transfers between devices: 6.33 us -> 5.98 us
    pallas_call x1, Pallas kernels: 2.52 us -> 2.08 us  [local(): pl.pallas_call(score_kernel, out_shape=(jax.ShapeDtypeStruct((1, STATS *...]
    all_to_all x1, waiting for transfers between devices: 6.32 us -> 5.98 us  [local(): rows = lax.all_to_all(packed, 'req', 0, 0)]
    pallas_call x1, Pallas kernels: 1.55 us -> 1.89 us  [local(): pl.pallas_call(stage_kernel, out_shape=(VMEM(lm_head.shape, lm_head.dtype...]
  transfers between devices with their start and end apart: 2 -> 2, of which waited for: 1 -> 1; matrix products, arithmetic and copies ran while one was open for 0% -> 0% of each run, Pallas kernels for 10% -> 12%
where the time goes in v7:
time: 31.1 us; the launch traced here: 30.8 us
  blocking collectives  9.79 us (31%)
  starting transfers between devices  7.36 us (24%)
  Pallas kernels  6.99 us (22%)
  waiting for transfers between devices  5.98 us (19%)
  between operations  0.66 us (2%)
    all_to_all x1, blocking collectives, sent_to_all(): return lax.all_to_all(copies, axis, 0, 0).reshape((-1,) + block.shape[1:])  9.79 us
    all_to_all x1, starting transfers between devices, local(): rows = lax.all_to_all(packed, 'req', 0, 0)  6.85 us
    all_to_all x1, waiting for transfers between devices, local(): rows = lax.all_to_all(packed, 'req', 0, 0)  5.98 us
    pallas_call x1, Pallas kernels, local(): pl.pallas_call(score_kernel, out_shape=(jax.ShapeDtypeStruct((1, STATS *...  2.08 us
    pallas_call x1, Pallas kernels, local(): pl.pallas_call(stage_kernel, out_shape=(VMEM(lm_head.shape, lm_head.dtype...  1.89 us
    pallas_call x1, Pallas kernels, local(): pl.pallas_call(functools.partial(pack_kernel, share), out_shape=VMEM((gro...  1.68 us
    pallas_call x1, Pallas kernels, local(): pl.pallas_call(functools.partial(finish_kernel, share), out_shape=(jax.Sh...  1.35 us
  transfers between devices with their start and end apart: 2, of which 1 were waited for; matrix products, arithmetic and copies ran while one was open for 0% of the time, Pallas kernels for 12%

profile of v7, /device:TPU:0, one launch (start us, length us, event | category | flops | bytes accessed | tf_op | source)
XLA Modules:
  0.0 30.8 jit_solution(2849858485346286647)
XLA Ops:
  0.6 0.5 %collective-permute-start = (bf16[4096,256]{1,0:T(8,128)(2,1)}, bf16[4096,256]{1,0:T(8,128)(2,1)}, u32[]{:S(2)}, u32[]{:S(2)}) collective-permute-start(bf16[4096,256]{1,0:T(8,128)(2,1)} %own_ref.1), channel_id=1, source_target_pairs={{0,1},{1,0},{2,3},{3,2},{4,5},{5,4},{6,7},{7,6},{8,9},{9,8},{10,11... | collective-permute-start | bytes 6291464 | tf_op jit(solution)/shard_map/ppermute | solution.py:227
  1.1 1.7 %shard_map.85 = bf16[8,8,1152]{2,1,0:T(8,128)(2,1)} custom-call(bf16[8,4096]{1,0:T(8,128)(2,1)} %hidden_ref.1, bf16[32,128]{1,0:T(8,128)(2,1)} %bitcast.5, s32[8]{0:T(128)} %targets_ref.1, s32[8]{0:T(128)} %segments_ref.1, s32[8]{0:T(128)} %scored_ref.3), custom_call_target="tpu_custom_call" | custom-call | tf_op jit(solution)/shard_map/pallas_call | solution.py:228
  2.8 6.8 %all-to-all-start = ((bf16[8,8,1152]{2,1,0:T(8,128)(2,1)}), bf16[8,8,1152]{2,1,0:T(8,128)(2,1)S(1)}, u32[]{:S(2)}, u32[]{:S(2)}) async-start(bf16[8,8,1152]{2,1,0:T(8,128)(2,1)} %shard_map.85), calls=%async_computation | async-start | bytes 294912 | tf_op jit(solution)/shard_map/all_to_all | solution.py:239
  9.7 0.0 collective-permute-done.other_ref
  9.7 1.9 %shard_map.86 = (bf16[4096,256]{1,0:T(8,128)(2,1)S(1)}, bf16[2048,256]{1,0:T(8,128)(2,1)S(1)}) custom-call(bf16[4096,256]{1,0:T(8,128)(2,1)} %own_ref.1, bf16[4096,256]{1,0:T(8,128)(2,1)} %collective-permute-done.other_ref), custom_call_target="tpu_custom_call" | custom-call | bytes 6291456 | tf_op jit(solution)/shard_map/pallas_call | solution.py:242
  11.6 6.0 %all-to-all-done.rows_ref = bf16[8,8,1152]{2,1,0:T(8,128)(2,1)S(1)} async-done(((bf16[8,8,1152]{2,1,0:T(8,128)(2,1)}), bf16[8,8,1152]{2,1,0:T(8,128)(2,1)S(1)}, u32[]{:S(2)}, u32[]{:S(2)}) %all-to-all-start) | async-done | bytes 147488 | tf_op jit(solution)/shard_map/all_to_all | solution.py:239
  17.6 2.1 %shard_map.87 = (f32[1,128]{1,0:T(1,128)S(1)}, f32[8,128]{1,0:T(8,128)S(1)}) custom-call(bf16[8,8,1152]{2,1,0:T(8,128)(2,1)S(1)} %all-to-all-done.rows_ref, bf16[4096,256]{1,0:T(8,128)(2,1)S(1)} %get-tuple-element.7.own_ref, bf16[2048,256]{1,0:T(8,128)(2,1)S(1)} %get-tuple-element.8.upper_ref, bf16[4096,256]{1,0:T(8,128)(2,1)} %collective-permute-done.other_ref), custom_call_target="tpu_custom_call" | custom-call | tf_op jit(solution)/shard_map/pallas_call | solution.py:251
  19.7 9.8 %all_to_all.10 = f32[32,1,128]{2,1,0:T(1,128)S(1)} all-to-all(f32[32,1,128]{2,1,0:T(1,128)S(1)} %broadcast_in_dim.9), channel_id=1, replica_groups=mesh['req'=8,'tp'=4] {'req','tp'}, dimensions={0} | all-to-all | bytes 32768 | tf_op jit(solution)/shard_map/all_to_all | solution.py:281
  29.5 1.3 %shard_map.88 = (f32[8]{0:T(128)}, f32[8]{0:T(128)}, f32[4]{0:T(128)}) custom-call(s32[8]{0:T(128)} %scored_ref.3, f32[32,128]{1,0:T(8,128)S(1)} %bitcast.3, f32[8,128]{1,0:T(8,128)S(1)} %get-tuple-element.10.meta_ref), custom_call_target="tpu_custom_call" | custom-call | tf_op jit(solution)/shard_map/pallas_call | solution.py:267
  (1 shorter events, 0.0 us)
Async XLA Ops:
  0.6 9.0 %collective-permute-start = (bf16[4096,256]{1,0:T(8,128)(2,1)}, bf16[4096,256]{1,0:T(8,128)(2,1)}, u32[]{:S(2)}, u32[]{:S(2)}) collective-permute-start(bf16[4096,256]{1,0:T(8,128)(2,1)} %own_ref.1), channel_id=1, source_target_pairs={{0,1},{1,0},{2,3},{3,2},{4,5},{5,4},{6,7},{7,6},{8,9},{9,8},{10,11... | collective-permute-start | bytes 6291464 | tf_op jit(solution)/shard_map/ppermute | solution.py:227
  2.8 14.7 %all-to-all-start = ((bf16[8,8,1152]{2,1,0:T(8,128)(2,1)}), bf16[8,8,1152]{2,1,0:T(8,128)(2,1)S(1)}, u32[]{:S(2)}, u32[]{:S(2)}) async-start(bf16[8,8,1152]{2,1,0:T(8,128)(2,1)} %shard_map.85), calls=%async_computation | async-start | bytes 294912 | tf_op jit(solution)/shard_map/all_to_all | solution.py:239

commit v8 on v7

--- a/solution.py
+++ b/solution.py
@@ -31,12 +31,17 @@
     return lax.broadcasted_iota(jnp.int32, shape, axis)
 
 
-def pack_kernel(share, hidden_ref, gain_ref, targets_ref, segments_ref, scored_ref, out_ref, wide_ref, parts_ref, gains_ref):
+def pack_kernel(share, hidden_ref, gain_ref, targets_ref, segments_ref, scored_ref, out_ref, wide_ref, scale_ref, gains_ref, parts_ref):
     row_count, width = hidden_ref.shape
-    parts = SUBS // MINE
-    span = width // parts
-    own, half = lax.axis_index("req"), lax.axis_index("tp") % PAIR
-    wide_ref[...] = hidden_ref[...].astype(jnp.float32)
+    receivers, _, length = out_ref.shape
+    span = length - max(PAIR * share, LANES)
+    pieces = SUBS // MINE
+    own, part = lax.axis_index("req"), lax.axis_index("tp")
+    wide = hidden_ref[...].astype(jnp.float32)
+    for chunk in range(width // LANES):
+        wide_ref[chunk] = wide[:, chunk * LANES : (chunk + 1) * LANES]
+    total = jnp.broadcast_to(jnp.sum(wide * wide, axis=1, keepdims=True), (row_count, LANES))
+    scale_ref[...] = lax.rsqrt(total / width + 1e-05)
     gains_ref[...] = gain_ref[...].astype(jnp.float32)
     ranks, count = ranks_of(scored_ref, row_count)
     source = [jnp.int32(0)] * PICK
@@ -44,43 +49,26 @@
         for r in range(PICK):
             hit = jnp.logical_and(scored_ref[row] == 1, ranks[row] == r)
             source[r] = jnp.where(hit, row, source[r])
-    mine = [source[i] for i in range(MINE)]
-    for h in range(1, PAIR):
-        mine = [jnp.where(half == h, source[h * MINE + i], mine[i]) for i in range(MINE)]
-    for i in range(MINE):
-        for k in range(parts):
-            parts_ref[k * MINE + i : k * MINE + i + 1, :] = wide_ref[pl.ds(mine[i], 1), k * span : (k + 1) * span]
-    values = parts_ref[...]
-    part = jnp.broadcast_to(jnp.sum(values * values, axis=1, keepdims=True), (SUBS, LANES))
-    total = part
-    for k in range(1, parts):
-        total = total + pltpu.roll(part, k * MINE, 0)
-    row_scale = lax.rsqrt(total / width + 1e-05)
-    sub, lane = iota((SUBS, LANES), 0), iota((SUBS, LANES), 1)
-    chunks = span // LANES
-    for at in range(chunks):
-        gain = gains_ref[at : at + 1, :]
-        for k in range(1, parts):
-            gain = jnp.where(sub >= k * MINE, gains_ref[k * chunks + at : k * chunks + at + 1, :], gain)
-        piece = parts_ref[:, at * LANES : (at + 1) * LANES]
-        piece = (piece * row_scale * gain).astype(jnp.bfloat16)
-        for to in range(out_ref.shape[0]):
-            out_ref[to, :, at * LANES : (at + 1) * LANES] = piece
-    width_side = out_ref.shape[2] - span
-    sub, lane = iota((SUBS, width_side), 0), iota((SUBS, width_side), 1)
-    at_row, at_half = lane % share - own * MINE, lane // share
-    side = jnp.zeros((SUBS, width_side), jnp.int32)
-    for i in range(MINE):
-        target = targets_ref[mine[i]]
-        digits = jnp.where(sub == 0, target & 255, jnp.where(sub == 1, (target >> 8) & 255, target >> 16))
-        fields = jnp.zeros((SUBS, width_side), jnp.int32)
-        for h in range(PAIR):
-            r = h * MINE + i
-            field = jnp.where(sub == 3, segments_ref[source[r]], (count > r).astype(jnp.int32))
-            fields = jnp.where(at_half == h, field, fields)
-        side = jnp.where(at_row == i, jnp.where(sub < 3, digits, jnp.where(sub < 5, fields, 0)), side)
+    for r in range(PICK):
+        scale = scale_ref[pl.ds(source[r], 1), :]
+        for j in range(pieces):
+            at = j * MINE + r % MINE
+            for chunk in range(span // LANES):
+                column = (part * pieces + j) * (span // LANES) + chunk
+                values = wide_ref[column, pl.ds(source[r], 1), :]
+                gain = gains_ref[pl.ds(column, 1), :]
+                parts_ref[r // MINE, at : at + 1, chunk * LANES : (chunk + 1) * LANES] = values * scale * gain
+    for to in range(receivers):
+        out_ref[to, :, :span] = parts_ref[to % PAIR].astype(jnp.bfloat16)
+    sub, lane = iota((SUBS, length - span), 0), iota((SUBS, length - span), 1)
+    side = jnp.zeros((SUBS, length - span), jnp.int32)
+    for r in range(PICK):
+        target = targets_ref[source[r]]
+        field = jnp.where(sub == 0, target & 255, jnp.where(sub == 1, (target >> 8) & 255, target >> 16))
+        field = jnp.where(sub < 3, field, jnp.where(sub == 3, segments_ref[source[r]], (count > r).astype(jnp.int32)))
+        side = jnp.where(lane == r // MINE * share + own * MINE + r % MINE, field, side)
     side = side.astype(jnp.float32).astype(jnp.bfloat16)
-    for to in range(out_ref.shape[0]):
+    for to in range(receivers):
         out_ref[to, :, span:] = side
 
 
@@ -109,24 +97,28 @@
     ]
     for copy in copies:
         copy.start()
-    groups = rows_ref.shape[0]
-    parts = SUBS // MINE
-    span = width // parts
+    tp, tp_count = lax.axis_index("tp"), lax.axis_size("tp")
+    groups = rows_ref.shape[0] // tp_count
+    pieces = SUBS // MINE
+    span = width // (tp_count * pieces)
     share = groups * MINE
-    tp, tp_count = lax.axis_index("tp"), lax.axis_size("tp")
     half = tp % PAIR
     place = lax.axis_index("req") * tp_count + tp
-    count = groups * SUBS
+    batch = min(groups, 8)
+    count, rows_of = batch * tp_count * SUBS, batch * MINE
     into, out_of = iota((count, count), 0), iota((count, count), 1)
-    wanted = into % share // MINE * SUBS + into // share * MINE + into % MINE
+    wanted = into % rows_of // MINE * (tp_count * SUBS) + into // rows_of * MINE + into % MINE
     order = jnp.where(out_of == wanted, 1.0, 0.0).astype(jnp.bfloat16)
-    rows = rows_ref[:, :, :span].reshape(count, span)
-    ordered = jnp.dot(order, rows, preferred_element_type=jnp.float32).astype(jnp.bfloat16)
-    for k in range(parts):
-        ordered_ref[:, k * span : (k + 1) * span] = ordered[k * share : (k + 1) * share]
+    for first in range(0, groups, batch):
+        rows = rows_ref[first * tp_count : (first + batch) * tp_count, :, :span].reshape(count, span)
+        ordered = jnp.dot(order, rows, preferred_element_type=jnp.float32).astype(jnp.bfloat16)
+        for k in range(tp_count * pieces):
+            ordered_ref[first * MINE : first * MINE + rows_of, k * span : (k + 1) * span] = ordered[
+                k * rows_of : (k + 1) * rows_of
+            ]
     meta = rows_ref[0, :, span:].astype(jnp.float32)
     for q in range(1, groups):
-        meta = meta + rows_ref[q, :, span:].astype(jnp.float32)
+        meta = meta + rows_ref[q * tp_count, :, span:].astype(jnp.float32)
     meta_ref[...] = meta
     own_logits = jnp.dot(ordered_ref[...], own_ref[...], preferred_element_type=jnp.float32)
     other_logits = jnp.dot(ordered_ref[:, :staged], upper_ref[...], preferred_element_type=jnp.float32)
@@ -136,8 +128,9 @@
     logits = jnp.concatenate([own_logits, other_logits], axis=1)
     lanes = max(share, LANES)
     sub, lane = iota((share, lanes), 0), iota((share, lanes), 1)
-    ids = meta[0:1, :lanes] + 256.0 * meta[1:2, :lanes] + 65536.0 * meta[2:3, :lanes]
-    ids = jnp.sum(jnp.where(lane == sub, ids, 0.0), axis=1, keepdims=True).astype(jnp.int32)
+    ids = meta[0:1, :] + 256.0 * meta[1:2, :] + 65536.0 * meta[2:3, :]
+    wanted = iota((share, meta.shape[1]), 1) == half * share + iota((share, meta.shape[1]), 0)
+    ids = jnp.sum(jnp.where(wanted, ids, 0.0), axis=1, keepdims=True).astype(jnp.int32)
     row_top = jnp.max(logits, axis=1, keepdims=True)
     scaled = jnp.exp(logits - row_top)
     row_total = jnp.sum(scaled, axis=1, keepdims=True)
@@ -217,7 +210,7 @@
 def local(hidden, norm_gain, lm_head, targets, segments, scored):
     row_count, width = hidden.shape
     groups, tp_count = lax.axis_size("req"), lax.axis_size("tp")
-    span = width * MINE // SUBS
+    span = width * MINE // SUBS // tp_count
     share = groups * MINE
     lanes = max(PAIR * share, LANES)
 
@@ -227,16 +220,17 @@
     other = lax.ppermute(lm_head, "tp", [(i, i + 1 - 2 * (i % PAIR)) for i in range(tp_count)])
     packed = pl.pallas_call(
         functools.partial(pack_kernel, share),
-        out_shape=VMEM((groups, SUBS, span + lanes), jnp.bfloat16),
+        out_shape=jax.ShapeDtypeStruct((groups * tp_count, SUBS, span + lanes), jnp.bfloat16),
         in_specs=[spec(VMEM)] * 2 + [spec(SMEM)] * 3,
         out_specs=spec(VMEM),
         scratch_shapes=[
-            VMEM((row_count, width), jnp.float32),
-            VMEM((SUBS, span), jnp.float32),
+            VMEM((width // LANES, row_count, LANES), jnp.float32),
+            VMEM((row_count, LANES), jnp.float32),
             VMEM((width // LANES, LANES), jnp.float32),
+            VMEM((PAIR, SUBS, span), jnp.float32),
         ],
     )(hidden, norm_gain.reshape(width // LANES, LANES), targets, segments, scored)
-    rows = lax.all_to_all(packed, "req", 0, 0)
+    rows = lax.all_to_all(packed, ("req", "tp"), 0, 0)
     other = pltpu.with_memory_space_constraint(other, pltpu.HBM)
     staged = width // 2
     slices = pl.pallas_call(

time: 31.1 us -> 32.1 us (1.032)
  waiting for transfers between devices: 5.98 us -> 6.98 us
    all_to_all x1, waiting for transfers between devices: 5.98 us -> 6.98 us  [local(): rows = lax.all_to_all(packed, ('req', 'tp'), 0, 0)]
  transfers between devices with their start and end apart: 2 -> 2, of which waited for: 1 -> 1; matrix products, arithmetic and copies ran while one was open for 0% -> 0% of each run, Pallas kernels for 12% -> 11%
where the time goes in v8:
time: 32.1 us; the launch traced here: 31.8 us
  blocking collectives  9.67 us (30%)
  starting transfers between devices  7.48 us (23%)
  Pallas kernels  7 us (22%)
  waiting for transfers between devices  6.98 us (22%)
  between operations  0.67 us (2%)
    all_to_all x1, blocking collectives, sent_to_all(): return lax.all_to_all(copies, axis, 0, 0).reshape((-1,) + block.shape[1:])  9.67 us
    all_to_all x1, waiting for transfers between devices, local(): rows = lax.all_to_all(packed, ('req', 'tp'), 0, 0)  6.98 us
    all_to_all x1, starting transfers between devices, local(): rows = lax.all_to_all(packed, ('req', 'tp'), 0, 0)  6.96 us
    pallas_call x1, Pallas kernels, local(): pl.pallas_call(score_kernel, out_shape=(jax.ShapeDtypeStruct((1, STATS *...  2.07 us
    pallas_call x1, Pallas kernels, local(): pl.pallas_call(stage_kernel, out_shape=(VMEM(lm_head.shape, lm_head.dtype...  1.89 us
    pallas_call x1, Pallas kernels, local(): pl.pallas_call(functools.partial(pack_kernel, share), out_shape=jax.Shape...  1.69 us
    pallas_call x1, Pallas kernels, local(): pl.pallas_call(functools.partial(finish_kernel, share), out_shape=(jax.Sh...  1.35 us
  transfers between devices with their start and end apart: 2, of which 1 were waited for; matrix products, arithmetic and copies ran while one was open for 0% of the time, Pallas kernels for 11%

profile of v8, /device:TPU:0, one launch (start us, length us, event | category | flops | bytes accessed | tf_op | source)
XLA Modules:
  0.0 31.8 jit_solution(17503432647839074876)
XLA Ops:
  0.6 0.5 %collective-permute-start = (bf16[4096,256]{1,0:T(8,128)(2,1)}, bf16[4096,256]{1,0:T(8,128)(2,1)}, u32[]{:S(2)}, u32[]{:S(2)}) collective-permute-start(bf16[4096,256]{1,0:T(8,128)(2,1)} %own_ref.1), channel_id=1, source_target_pairs={{0,1},{1,0},{2,3},{3,2},{4,5},{5,4},{6,7},{7,6},{8,9},{9,8},{10,11... | collective-permute-start | bytes 6291464 | tf_op jit(solution)/shard_map/ppermute | solution.py:220
  1.1 1.7 %shard_map.85 = bf16[32,8,384]{2,1,0:T(8,128)(2,1)} custom-call(bf16[8,4096]{1,0:T(8,128)(2,1)} %hidden_ref.1, bf16[32,128]{1,0:T(8,128)(2,1)} %bitcast.5, s32[8]{0:T(128)} %targets_ref.1, s32[8]{0:T(128)} %segments_ref.1, s32[8]{0:T(128)} %scored_ref.3), custom_call_target="tpu_custom_call" | custom-call | tf_op jit(solution)/shard_map/pallas_call | solution.py:221
  2.8 7.0 %all-to-all-start = ((bf16[32,8,384]{2,1,0:T(8,128)(2,1)}), bf16[32,8,384]{2,1,0:T(8,128)(2,1)S(1)}, u32[]{:S(2)}, u32[]{:S(2)}) async-start(bf16[32,8,384]{2,1,0:T(8,128)(2,1)} %shard_map.85), calls=%async_computation | async-start | bytes 393216 | tf_op jit(solution)/shard_map/all_to_all | solution.py:233
  9.8 0.0 collective-permute-done.other_ref
  9.8 1.9 %shard_map.86 = (bf16[4096,256]{1,0:T(8,128)(2,1)S(1)}, bf16[2048,256]{1,0:T(8,128)(2,1)S(1)}) custom-call(bf16[4096,256]{1,0:T(8,128)(2,1)} %own_ref.1, bf16[4096,256]{1,0:T(8,128)(2,1)} %collective-permute-done.other_ref), custom_call_target="tpu_custom_call" | custom-call | bytes 6291456 | tf_op jit(solution)/shard_map/pallas_call | solution.py:236
  11.7 7.0 %all-to-all-done.rows_ref = bf16[32,8,384]{2,1,0:T(8,128)(2,1)S(1)} async-done(((bf16[32,8,384]{2,1,0:T(8,128)(2,1)}), bf16[32,8,384]{2,1,0:T(8,128)(2,1)S(1)}, u32[]{:S(2)}, u32[]{:S(2)}) %all-to-all-start) | async-done | bytes 196640 | tf_op jit(solution)/shard_map/all_to_all | solution.py:233
  18.7 2.1 %shard_map.87 = (f32[1,128]{1,0:T(1,128)S(1)}, f32[8,128]{1,0:T(8,128)S(1)}) custom-call(bf16[32,8,384]{2,1,0:T(8,128)(2,1)S(1)} %all-to-all-done.rows_ref, bf16[4096,256]{1,0:T(8,128)(2,1)S(1)} %get-tuple-element.7.own_ref, bf16[2048,256]{1,0:T(8,128)(2,1)S(1)} %get-tuple-element.8.upper_ref, bf16[4096,256]{1,0:T(8,128)(2,1)} %collective-permute-done.other_ref), custom_call_target="tpu_custom_call" | custom-call | tf_op jit(solution)/shard_map/pallas_call | solution.py:245
  20.8 9.7 %all_to_all.10 = f32[32,1,128]{2,1,0:T(1,128)S(1)} all-to-all(f32[32,1,128]{2,1,0:T(1,128)S(1)} %broadcast_in_dim.9), channel_id=1, replica_groups=mesh['req'=8,'tp'=4] {'req','tp'}, dimensions={0} | all-to-all | bytes 32768 | tf_op jit(solution)/shard_map/all_to_all | solution.py:275
  30.5 1.3 %shard_map.88 = (f32[8]{0:T(128)}, f32[8]{0:T(128)}, f32[4]{0:T(128)}) custom-call(s32[8]{0:T(128)} %scored_ref.3, f32[32,128]{1,0:T(8,128)S(1)} %bitcast.3, f32[8,128]{1,0:T(8,128)S(1)} %get-tuple-element.10.meta_ref), custom_call_target="tpu_custom_call" | custom-call | tf_op jit(solution)/shard_map/pallas_call | solution.py:261
  (1 shorter events, 0.0 us)
Async XLA Ops:
  0.6 9.2 %collective-permute-start = (bf16[4096,256]{1,0:T(8,128)(2,1)}, bf16[4096,256]{1,0:T(8,128)(2,1)}, u32[]{:S(2)}, u32[]{:S(2)}) collective-permute-start(bf16[4096,256]{1,0:T(8,128)(2,1)} %own_ref.1), channel_id=1, source_target_pairs={{0,1},{1,0},{2,3},{3,2},{4,5},{5,4},{6,7},{7,6},{8,9},{9,8},{10,11... | collective-permute-start | bytes 6291464 | tf_op jit(solution)/shard_map/ppermute | solution.py:220
  2.8 15.9 %all-to-all-start = ((bf16[32,8,384]{2,1,0:T(8,128)(2,1)}), bf16[32,8,384]{2,1,0:T(8,128)(2,1)S(1)}, u32[]{:S(2)}, u32[]{:S(2)}) async-start(bf16[32,8,384]{2,1,0:T(8,128)(2,1)} %shard_map.85), calls=%async_computation | async-start | bytes 393216 | tf_op jit(solution)/shard_map/all_to_all | solution.py:233

commit v9 on v7

--- a/solution.py
+++ b/solution.py
@@ -76,9 +76,9 @@
         fields = jnp.zeros((SUBS, width_side), jnp.int32)
         for h in range(PAIR):
             r = h * MINE + i
-            field = jnp.where(sub == 3, segments_ref[source[r]], (count > r).astype(jnp.int32))
-            fields = jnp.where(at_half == h, field, fields)
-        side = jnp.where(at_row == i, jnp.where(sub < 3, digits, jnp.where(sub < 5, fields, 0)), side)
+            field = jnp.where(sub == 4, (count > r).astype(jnp.int32), source[r])
+            fields = jnp.where(at_half == h, jnp.where(sub == 3, segments_ref[source[r]], field), fields)
+        side = jnp.where(at_row == i, jnp.where(sub < 3, digits, fields), side)
     side = side.astype(jnp.float32).astype(jnp.bfloat16)
     for to in range(out_ref.shape[0]):
         out_ref[to, :, span:] = side
@@ -163,8 +163,8 @@
                 stats_ref[:, first : first + share] = jnp.where(half == h, line, 0.0 if at else -jnp.inf)
 
 
-def finish_kernel(share, scored_ref, stats_ref, meta_ref, logprob_ref, entropy_ref, seq_ref):
-    row_count = scored_ref.shape[0]
+def finish_kernel(share, stats_ref, meta_ref, logprob_ref, entropy_ref, seq_ref):
+    row_count = logprob_ref.shape[0]
     used = PAIR * share
     lanes = max(used, LANES)
 
@@ -180,34 +180,21 @@
     row_weighted = jnp.sum(stat(2) * weight, axis=0, keepdims=True)
     picked = jnp.sum(stat(3), axis=0, keepdims=True)
     log_norm = row_top + jnp.log(row_total)
-    in_use = jnp.logical_and(meta_ref[4:5, :] > 0.5, iota((1, lanes), 1) < used)
+    lane, sub = iota((1, lanes), 1), iota((SUBS, lanes), 0)
+    in_use = jnp.logical_and(meta_ref[4:5, :] > 0.5, lane < used)
     logprob = jnp.where(in_use, picked - log_norm, 0.0)
     entropy = jnp.where(in_use, log_norm - row_weighted / row_total, 0.0)
-    sub, lane = iota((SUBS, LANES), 0), iota((SUBS, LANES), 1)
-    segment = meta_ref[3:4, :].astype(jnp.int32)
-    sums = jnp.sum(jnp.where(segment == iota((SUBS, lanes), 0), logprob, 0.0), axis=1, keepdims=True)
-    seqs = jnp.sum(jnp.where(sub == lane, sums, 0.0), axis=0, keepdims=True)
-    seq_ref[...] = seqs[0, :SEQS]
-    ranks, _ = ranks_of(scored_ref, row_count)
-    rank = jnp.zeros((SUBS, LANES), jnp.int32)
-    keep = jnp.zeros((SUBS, LANES), jnp.int32)
-    for row in range(row_count):
-        rank = jnp.where(lane == row, ranks[row], rank)
-        keep = jnp.where(lane == row, scored_ref[row], keep)
-    mine = jnp.zeros((SUBS, LANES), jnp.float32)
-    for h in range(PAIR):
-        first = h * share + lax.axis_index("req") * MINE
-        block = first // LANES
-        own_logprob, own_entropy = logprob[:, :LANES], entropy[:, :LANES]
-        for at in range(1, lanes // LANES):
-            piece = slice(at * LANES, (at + 1) * LANES)
-            own_logprob = jnp.where(block == at, logprob[:, piece], own_logprob)
-            own_entropy = jnp.where(block == at, entropy[:, piece], own_entropy)
-        both = jnp.where(sub == 0, own_logprob, own_entropy)
-        both = jnp.take_along_axis(both, first - block * LANES + rank % MINE, axis=1)
-        mine = jnp.where(jnp.logical_and(rank // MINE == h, keep == 1), both, mine)
-    logprob_ref[...] = mine[0, :row_count]
-    entropy_ref[...] = mine[1, :row_count]
+    segment, place = meta_ref[3:4, :].astype(jnp.int32), meta_ref[5:6, :].astype(jnp.int32)
+    mine = jnp.logical_and(place == sub, lane % share // MINE == lax.axis_index("req"))
+
+    def placed(values, wanted):
+        sums = jnp.sum(jnp.where(wanted, values, 0.0), axis=1, keepdims=True)
+        diagonal = iota((SUBS, LANES), 0) == iota((SUBS, LANES), 1)
+        return jnp.sum(jnp.where(diagonal, sums, 0.0), axis=0)
+
+    logprob_ref[...] = placed(logprob, mine)[:row_count]
+    entropy_ref[...] = placed(entropy, mine)[:row_count]
+    seq_ref[...] = placed(logprob, segment == sub)[:SEQS]
 
 
 def grant(mebibytes):
@@ -271,9 +258,9 @@
             jax.ShapeDtypeStruct((row_count,), jnp.float32),
             jax.ShapeDtypeStruct((SEQS,), jnp.float32),
         ),
-        in_specs=[spec(SMEM), spec(VMEM), spec(VMEM)],
+        in_specs=[spec(VMEM), spec(VMEM)],
         out_specs=(spec(VMEM), spec(VMEM), spec(VMEM)),
-    )(scored, pltpu.with_memory_space_constraint(gathered, VMEM), pltpu.with_memory_space_constraint(meta, VMEM))
+    )(pltpu.with_memory_space_constraint(gathered, VMEM), pltpu.with_memory_space_constraint(meta, VMEM))
 
 
 def sent_to_all(block, axis):

time: 31.1 us -> 30.5 us (0.981)
  Pallas kernels: 6.99 us -> 6.34 us
    pallas_call x1, Pallas kernels: 1.35 us -> 0.69 us  [local(): pl.pallas_call(functools.partial(finish_kernel, share), out_shape=(jax.Sh...]
where the time goes in v9:
time: 30.5 us; the launch traced here: 30.1 us
  blocking collectives  9.79 us (32%)
  starting transfers between devices  7.36 us (24%)
  Pallas kernels  6.34 us (21%)
  waiting for transfers between devices  5.98 us (20%)
  between operations  0.66 us (2%)
    all_to_all x1, blocking collectives, sent_to_all(): return lax.all_to_all(copies, axis, 0, 0).reshape((-1,) + block.shape[1:])  9.79 us
    all_to_all x1, starting transfers between devices, local(): rows = lax.all_to_all(packed, 'req', 0, 0)  6.85 us
    all_to_all x1, waiting for transfers between devices, local(): rows = lax.all_to_all(packed, 'req', 0, 0)  5.98 us
    pallas_call x1, Pallas kernels, local(): pl.pallas_call(score_kernel, out_shape=(jax.ShapeDtypeStruct((1, STATS *...  2.08 us
    pallas_call x1, Pallas kernels, local(): pl.pallas_call(stage_kernel, out_shape=(VMEM(lm_head.shape, lm_head.dtype...  1.89 us
    pallas_call x1, Pallas kernels, local(): pl.pallas_call(functools.partial(pack_kernel, share), out_shape=VMEM((gro...  1.68 us
    pallas_call x1, Pallas kernels, local(): pl.pallas_call(functools.partial(finish_kernel, share), out_shape=(jax.Sh...  0.69 us
  transfers between devices with their start and end apart: 2, of which 1 were waited for; matrix products, arithmetic and copies ran while one was open for 0% of the time, Pallas kernels for 12%

profile of v9, /device:TPU:0, one launch (start us, length us, event | category | flops | bytes accessed | tf_op | source)
XLA Modules:
  0.0 30.1 jit_solution(2767646635649384696)
XLA Ops:
  0.6 0.5 %collective-permute-start = (bf16[4096,256]{1,0:T(8,128)(2,1)}, bf16[4096,256]{1,0:T(8,128)(2,1)}, u32[]{:S(2)}, u32[]{:S(2)}) collective-permute-start(bf16[4096,256]{1,0:T(8,128)(2,1)} %own_ref.1), channel_id=1, source_target_pairs={{0,1},{1,0},{2,3},{3,2},{4,5},{5,4},{6,7},{7,6},{8,9},{9,8},{10,11... | collective-permute-start | bytes 6291464 | tf_op jit(solution)/shard_map/ppermute | solution.py:214
  1.1 1.7 %shard_map.85 = bf16[8,8,1152]{2,1,0:T(8,128)(2,1)} custom-call(bf16[8,4096]{1,0:T(8,128)(2,1)} %hidden_ref.1, bf16[32,128]{1,0:T(8,128)(2,1)} %bitcast.5, s32[8]{0:T(128)} %targets_ref.1, s32[8]{0:T(128)} %segments_ref.1, s32[8]{0:T(128)} %scored_ref.1), custom_call_target="tpu_custom_call" | custom-call | tf_op jit(solution)/shard_map/pallas_call | solution.py:215
  2.8 6.8 %all-to-all-start = ((bf16[8,8,1152]{2,1,0:T(8,128)(2,1)}), bf16[8,8,1152]{2,1,0:T(8,128)(2,1)S(1)}, u32[]{:S(2)}, u32[]{:S(2)}) async-start(bf16[8,8,1152]{2,1,0:T(8,128)(2,1)} %shard_map.85), calls=%async_computation | async-start | bytes 294912 | tf_op jit(solution)/shard_map/all_to_all | solution.py:226
  9.7 0.0 collective-permute-done.other_ref
  9.7 1.9 %shard_map.86 = (bf16[4096,256]{1,0:T(8,128)(2,1)S(1)}, bf16[2048,256]{1,0:T(8,128)(2,1)S(1)}) custom-call(bf16[4096,256]{1,0:T(8,128)(2,1)} %own_ref.1, bf16[4096,256]{1,0:T(8,128)(2,1)} %collective-permute-done.other_ref), custom_call_target="tpu_custom_call" | custom-call | bytes 6291456 | tf_op jit(solution)/shard_map/pallas_call | solution.py:229
  11.6 6.0 %all-to-all-done.rows_ref = bf16[8,8,1152]{2,1,0:T(8,128)(2,1)S(1)} async-done(((bf16[8,8,1152]{2,1,0:T(8,128)(2,1)}), bf16[8,8,1152]{2,1,0:T(8,128)(2,1)S(1)}, u32[]{:S(2)}, u32[]{:S(2)}) %all-to-all-start) | async-done | bytes 147488 | tf_op jit(solution)/shard_map/all_to_all | solution.py:226
  17.6 2.1 %shard_map.87 = (f32[1,128]{1,0:T(1,128)S(1)}, f32[8,128]{1,0:T(8,128)S(1)}) custom-call(bf16[8,8,1152]{2,1,0:T(8,128)(2,1)S(1)} %all-to-all-done.rows_ref, bf16[4096,256]{1,0:T(8,128)(2,1)S(1)} %get-tuple-element.7.own_ref, bf16[2048,256]{1,0:T(8,128)(2,1)S(1)} %get-tuple-element.8.upper_ref, bf16[4096,256]{1,0:T(8,128)(2,1)} %collective-permute-done.other_ref), custom_call_target="tpu_custom_call" | custom-call | tf_op jit(solution)/shard_map/pallas_call | solution.py:238
  19.7 9.8 %all_to_all.10 = f32[32,1,128]{2,1,0:T(1,128)S(1)} all-to-all(f32[32,1,128]{2,1,0:T(1,128)S(1)} %broadcast_in_dim.9), channel_id=1, replica_groups=mesh['req'=8,'tp'=4] {'req','tp'}, dimensions={0} | all-to-all | bytes 32768 | tf_op jit(solution)/shard_map/all_to_all | solution.py:268
  29.5 0.7 %shard_map.88 = (f32[8]{0:T(128)}, f32[8]{0:T(128)}, f32[4]{0:T(128)}) custom-call(f32[32,128]{1,0:T(8,128)S(1)} %bitcast.3, f32[8,128]{1,0:T(8,128)S(1)} %get-tuple-element.10.meta_ref), custom_call_target="tpu_custom_call" | custom-call | tf_op jit(solution)/shard_map/pallas_call | solution.py:254
  (1 shorter events, 0.0 us)
Async XLA Ops:
  0.6 9.0 %collective-permute-start = (bf16[4096,256]{1,0:T(8,128)(2,1)}, bf16[4096,256]{1,0:T(8,128)(2,1)}, u32[]{:S(2)}, u32[]{:S(2)}) collective-permute-start(bf16[4096,256]{1,0:T(8,128)(2,1)} %own_ref.1), channel_id=1, source_target_pairs={{0,1},{1,0},{2,3},{3,2},{4,5},{5,4},{6,7},{7,6},{8,9},{9,8},{10,11... | collective-permute-start | bytes 6291464 | tf_op jit(solution)/shard_map/ppermute | solution.py:214
  2.8 14.7 %all-to-all-start = ((bf16[8,8,1152]{2,1,0:T(8,128)(2,1)}), bf16[8,8,1152]{2,1,0:T(8,128)(2,1)S(1)}, u32[]{:S(2)}, u32[]{:S(2)}) async-start(bf16[8,8,1152]{2,1,0:T(8,128)(2,1)} %shard_map.85), calls=%async_computation | async-start | bytes 294912 | tf_op jit(solution)/shard_map/all_to_all | solution.py:226

commit v10 on v9

--- a/solution.py
+++ b/solution.py
@@ -16,70 +16,79 @@
 STATS = 4
 
 VMEM = pltpu.VMEM
-SMEM = pltpu.SMEM
-
-
-def ranks_of(scored_ref, row_count):
-    ranks, so_far = [], jnp.int32(0)
-    for row in range(row_count):
-        ranks.append(so_far)
-        so_far = so_far + scored_ref[row]
-    return ranks, so_far
+
+
+def over(number, by):
+    return number >> (by.bit_length() - 1) if by & (by - 1) == 0 else number // by
+
+
+def left(number, by):
+    return number & (by - 1) if by & (by - 1) == 0 else number % by
 
 
 def iota(shape, axis):
     return lax.broadcasted_iota(jnp.int32, shape, axis)
 
 
-def pack_kernel(share, hidden_ref, gain_ref, targets_ref, segments_ref, scored_ref, out_ref, wide_ref, parts_ref, gains_ref):
+def pack_kernel(share, hidden_ref, gain_ref, targets_ref, segments_ref, scored_ref, out_ref, gains_ref):
     row_count, width = hidden_ref.shape
     parts = SUBS // MINE
     span = width // parts
-    own, half = lax.axis_index("req"), lax.axis_index("tp") % PAIR
-    wide_ref[...] = hidden_ref[...].astype(jnp.float32)
+    own, half = lax.axis_index("req"), left(lax.axis_index("tp"), PAIR)
     gains_ref[...] = gain_ref[...].astype(jnp.float32)
-    ranks, count = ranks_of(scored_ref, row_count)
-    source = [jnp.int32(0)] * PICK
-    for row in range(row_count):
-        for r in range(PICK):
-            hit = jnp.logical_and(scored_ref[row] == 1, ranks[row] == r)
-            source[r] = jnp.where(hit, row, source[r])
-    mine = [source[i] for i in range(MINE)]
-    for h in range(1, PAIR):
-        mine = [jnp.where(half == h, source[h * MINE + i], mine[i]) for i in range(MINE)]
-    for i in range(MINE):
-        for k in range(parts):
-            parts_ref[k * MINE + i : k * MINE + i + 1, :] = wide_ref[pl.ds(mine[i], 1), k * span : (k + 1) * span]
-    values = parts_ref[...]
+
+    def across(ref):
+        return jnp.broadcast_to(ref[...].reshape(1, row_count), (row_count, row_count)).astype(jnp.float32)
+
+    sub, lane = iota((row_count, row_count), 0), iota((row_count, row_count), 1)
+    scored, targets, segments = across(scored_ref), across(targets_ref), across(segments_ref)
+
+    def down(values, wanted):
+        return jnp.sum(jnp.where(wanted, values, 0.0), axis=1, keepdims=True)
+
+    in_use, target, segment = (down(values, lane == sub) for values in (scored, targets, segments))
+    rank_down = down(scored, lane < sub)
+    rank_across = jnp.sum(jnp.where(sub < lane, in_use, 0.0), axis=0, keepdims=True)
+    wanted = (half * MINE + left(iota((SUBS, row_count), 0), MINE)).astype(jnp.float32)
+    choice = jnp.where(jnp.logical_and(rank_across == wanted, scored[:1, :] > 0.5), 1.0, 0.0)
+    chosen = jnp.dot(choice.astype(jnp.bfloat16), hidden_ref[...], preferred_element_type=jnp.float32)
+    bundle = over(iota((SUBS, span), 0), MINE)
+    values = chosen[:, :span]
+    for k in range(1, parts):
+        values = jnp.where(bundle == k, chosen[:, k * span : (k + 1) * span], values)
     part = jnp.broadcast_to(jnp.sum(values * values, axis=1, keepdims=True), (SUBS, LANES))
     total = part
     for k in range(1, parts):
         total = total + pltpu.roll(part, k * MINE, 0)
     row_scale = lax.rsqrt(total / width + 1e-05)
-    sub, lane = iota((SUBS, LANES), 0), iota((SUBS, LANES), 1)
+    bundle = over(iota((SUBS, LANES), 0), MINE)
     chunks = span // LANES
     for at in range(chunks):
         gain = gains_ref[at : at + 1, :]
         for k in range(1, parts):
-            gain = jnp.where(sub >= k * MINE, gains_ref[k * chunks + at : k * chunks + at + 1, :], gain)
-        piece = parts_ref[:, at * LANES : (at + 1) * LANES]
-        piece = (piece * row_scale * gain).astype(jnp.bfloat16)
+            gain = jnp.where(bundle == k, gains_ref[k * chunks + at : k * chunks + at + 1, :], gain)
+        piece = (values[:, at * LANES : (at + 1) * LANES] * row_scale * gain).astype(jnp.bfloat16)
         for to in range(out_ref.shape[0]):
             out_ref[to, :, at * LANES : (at + 1) * LANES] = piece
     width_side = out_ref.shape[2] - span
-    sub, lane = iota((SUBS, width_side), 0), iota((SUBS, width_side), 1)
-    at_row, at_half = lane % share - own * MINE, lane // share
-    side = jnp.zeros((SUBS, width_side), jnp.int32)
-    for i in range(MINE):
-        target = targets_ref[mine[i]]
-        digits = jnp.where(sub == 0, target & 255, jnp.where(sub == 1, (target >> 8) & 255, target >> 16))
-        fields = jnp.zeros((SUBS, width_side), jnp.int32)
-        for h in range(PAIR):
-            r = h * MINE + i
-            field = jnp.where(sub == 4, (count > r).astype(jnp.int32), source[r])
-            fields = jnp.where(at_half == h, jnp.where(sub == 3, segments_ref[source[r]], field), fields)
-        side = jnp.where(at_row == i, jnp.where(sub < 3, digits, fields), side)
-    side = side.astype(jnp.float32).astype(jnp.bfloat16)
+    lane = iota((row_count, width_side), 1)
+    i = left(lane, share) - own * MINE
+    mine = jnp.logical_and(jnp.logical_and(i >= 0, i < MINE), in_use > 0.5)
+    here = jnp.logical_and(mine, rank_down == (over(lane, share) * MINE + i).astype(jnp.float32))
+    same = jnp.logical_and(mine, rank_down == (half * MINE + i).astype(jnp.float32))
+
+    def field(wanted, numbers):
+        return jnp.sum(jnp.where(wanted, numbers, 0.0), axis=0, keepdims=True)
+
+    number = field(same, target).astype(jnp.int32)
+    place = iota((row_count, 1), 0).astype(jnp.float32)
+    fields = [(number >> shift & 255).astype(jnp.float32) for shift in (0, 8, 16)]
+    fields += [field(here, segment), field(here, jnp.ones_like(place)), field(here, place)]
+    sub = iota((SUBS, width_side), 0)
+    side = jnp.zeros((SUBS, width_side), jnp.float32)
+    for at, line in enumerate(fields):
+        side = jnp.where(sub == at, line, side)
+    side = side.astype(jnp.bfloat16)
     for to in range(out_ref.shape[0]):
         out_ref[to, :, span:] = side
 
@@ -114,11 +123,11 @@
     span = width // parts
     share = groups * MINE
     tp, tp_count = lax.axis_index("tp"), lax.axis_size("tp")
-    half = tp % PAIR
+    half = left(tp, PAIR)
     place = lax.axis_index("req") * tp_count + tp
     count = groups * SUBS
     into, out_of = iota((count, count), 0), iota((count, count), 1)
-    wanted = into % share // MINE * SUBS + into // share * MINE + into % MINE
+    wanted = over(left(into, share), MINE) * SUBS + over(into, share) * MINE + left(into, MINE)
     order = jnp.where(out_of == wanted, 1.0, 0.0).astype(jnp.bfloat16)
     rows = rows_ref[:, :, :span].reshape(count, span)
     ordered = jnp.dot(order, rows, preferred_element_type=jnp.float32).astype(jnp.bfloat16)
@@ -150,11 +159,11 @@
     if PAIR * share * STATS == LANES:
         joined = picked
         for at in range(STATS - 1):
-            joined = jnp.where(lane // (PAIR * share) == at, stats[at], joined)
-        joined = jnp.sum(jnp.where(lane % share == sub, joined, 0.0), axis=0, keepdims=True)
+            joined = jnp.where(over(lane, PAIR * share) == at, stats[at], joined)
+        joined = jnp.sum(jnp.where(left(lane, share) == sub, joined, 0.0), axis=0, keepdims=True)
         lane = iota((1, LANES), 1)
         neutral = jnp.where(lane < PAIR * share, -jnp.inf, 0.0)
-        stats_ref[...] = jnp.where(lane // share % PAIR == half, joined, neutral)
+        stats_ref[...] = jnp.where(left(over(lane, share), PAIR) == half, joined, neutral)
     else:
         for at in range(STATS):
             line = jnp.sum(jnp.where(lane == sub, stats[at], 0.0), axis=0, keepdims=True)
@@ -185,7 +194,7 @@
     logprob = jnp.where(in_use, picked - log_norm, 0.0)
     entropy = jnp.where(in_use, log_norm - row_weighted / row_total, 0.0)
     segment, place = meta_ref[3:4, :].astype(jnp.int32), meta_ref[5:6, :].astype(jnp.int32)
-    mine = jnp.logical_and(place == sub, lane % share // MINE == lax.axis_index("req"))
+    mine = jnp.logical_and(place == sub, over(left(lane, share), MINE) == lax.axis_index("req"))
 
     def placed(values, wanted):
         sums = jnp.sum(jnp.where(wanted, values, 0.0), axis=1, keepdims=True)
@@ -215,11 +224,9 @@
     packed = pl.pallas_call(
         functools.partial(pack_kernel, share),
         out_shape=VMEM((groups, SUBS, span + lanes), jnp.bfloat16),
-        in_specs=[spec(VMEM)] * 2 + [spec(SMEM)] * 3,
+        in_specs=[spec(VMEM)] * 5,
         out_specs=spec(VMEM),
         scratch_shapes=[
-            VMEM((row_count, width), jnp.float32),
-            VMEM((SUBS, span), jnp.float32),
             VMEM((width // LANES, LANES), jnp.float32),
         ],
     )(hidden, norm_gain.reshape(width // LANES, LANES), targets, segments, scored)

time: 30.5 us -> 31.1 us (1.020)
  Pallas kernels: 6.34 us -> 7 us
    pallas_call x1, Pallas kernels: 2.08 us -> 2.54 us  [local(): pl.pallas_call(score_kernel, out_shape=(jax.ShapeDtypeStruct((1, STATS *...]
where the time goes in v10:
time: 31.1 us; the launch traced here: 30.8 us
  blocking collectives  9.8 us (32%)
  starting transfers between devices  7.36 us (24%)
  Pallas kernels  7 us (23%)
  waiting for transfers between devices  5.98 us (19%)
  between operations  0.66 us (2%)
    all_to_all x1, blocking collectives, sent_to_all(): return lax.all_to_all(copies, axis, 0, 0).reshape((-1,) + block.shape[1:])  9.8 us
    all_to_all x1, starting transfers between devices, local(): rows = lax.all_to_all(packed, 'req', 0, 0)  6.85 us
    all_to_all x1, waiting for transfers between devices, local(): rows = lax.all_to_all(packed, 'req', 0, 0)  5.98 us
    pallas_call x1, Pallas kernels, local(): pl.pallas_call(score_kernel, out_shape=(jax.ShapeDtypeStruct((1, STATS *...  2.54 us
    pallas_call x1, Pallas kernels, local(): pl.pallas_call(stage_kernel, out_shape=(VMEM(lm_head.shape, lm_head.dtype...  1.89 us
    pallas_call x1, Pallas kernels, local(): pl.pallas_call(functools.partial(pack_kernel, share), out_shape=VMEM((gro...  1.88 us
    pallas_call x1, Pallas kernels, local(): pl.pallas_call(functools.partial(finish_kernel, share), out_shape=(jax.Sh...  0.69 us
  transfers between devices with their start and end apart: 2, of which 1 were waited for; matrix products, arithmetic and copies ran while one was open for 0% of the time, Pallas kernels for 12%

profile of v10, /device:TPU:0, one launch (start us, length us, event | category | flops | bytes accessed | tf_op | source)
XLA Modules:
  0.0 30.8 jit_solution(5446123660638443863)
XLA Ops:
  0.6 0.5 %collective-permute-start = (bf16[4096,256]{1,0:T(8,128)(2,1)}, bf16[4096,256]{1,0:T(8,128)(2,1)}, u32[]{:S(2)}, u32[]{:S(2)}) collective-permute-start(bf16[4096,256]{1,0:T(8,128)(2,1)} %own_ref.1), channel_id=1, source_target_pairs={{0,1},{1,0},{2,3},{3,2},{4,5},{5,4},{6,7},{7,6},{8,9},{9,8},{10,11... | collective-permute-start | bytes 6291464 | tf_op jit(solution)/shard_map/ppermute | solution.py:223
  1.1 1.9 %shard_map.85 = bf16[8,8,1152]{2,1,0:T(8,128)(2,1)} custom-call(bf16[8,4096]{1,0:T(8,128)(2,1)} %hidden_ref.1, bf16[32,128]{1,0:T(8,128)(2,1)} %bitcast.5, s32[8]{0:T(128)} %targets_ref.1, s32[8]{0:T(128)} %segments_ref.1, s32[8]{0:T(128)} %scored_ref.1), custom_call_target="tpu_custom_call" | custom-call | tf_op jit(solution)/shard_map/pallas_call | solution.py:224
  3.0 6.8 %all-to-all-start = ((bf16[8,8,1152]{2,1,0:T(8,128)(2,1)}), bf16[8,8,1152]{2,1,0:T(8,128)(2,1)S(1)}, u32[]{:S(2)}, u32[]{:S(2)}) async-start(bf16[8,8,1152]{2,1,0:T(8,128)(2,1)} %shard_map.85), calls=%async_computation | async-start | bytes 294912 | tf_op jit(solution)/shard_map/all_to_all | solution.py:233
  9.9 0.0 collective-permute-done.other_ref
  9.9 1.9 %shard_map.86 = (bf16[4096,256]{1,0:T(8,128)(2,1)S(1)}, bf16[2048,256]{1,0:T(8,128)(2,1)S(1)}) custom-call(bf16[4096,256]{1,0:T(8,128)(2,1)} %own_ref.1, bf16[4096,256]{1,0:T(8,128)(2,1)} %collective-permute-done.other_ref), custom_call_target="tpu_custom_call" | custom-call | bytes 6291456 | tf_op jit(solution)/shard_map/pallas_call | solution.py:236
  11.8 6.0 %all-to-all-done.rows_ref = bf16[8,8,1152]{2,1,0:T(8,128)(2,1)S(1)} async-done(((bf16[8,8,1152]{2,1,0:T(8,128)(2,1)}), bf16[8,8,1152]{2,1,0:T(8,128)(2,1)S(1)}, u32[]{:S(2)}, u32[]{:S(2)}) %all-to-all-start) | async-done | bytes 147488 | tf_op jit(solution)/shard_map/all_to_all | solution.py:233
  17.8 2.5 %shard_map.87 = (f32[1,128]{1,0:T(1,128)S(1)}, f32[8,128]{1,0:T(8,128)S(1)}) custom-call(bf16[8,8,1152]{2,1,0:T(8,128)(2,1)S(1)} %all-to-all-done.rows_ref, bf16[4096,256]{1,0:T(8,128)(2,1)S(1)} %get-tuple-element.7.own_ref, bf16[2048,256]{1,0:T(8,128)(2,1)S(1)} %get-tuple-element.8.upper_ref, bf16[4096,256]{1,0:T(8,128)(2,1)} %collective-permute-done.other_ref), custom_call_target="tpu_custom_call" | custom-call | tf_op jit(solution)/shard_map/pallas_call | solution.py:245
  20.3 9.8 %all_to_all.10 = f32[32,1,128]{2,1,0:T(1,128)S(1)} all-to-all(f32[32,1,128]{2,1,0:T(1,128)S(1)} %broadcast_in_dim.9), channel_id=1, replica_groups=mesh['req'=8,'tp'=4] {'req','tp'}, dimensions={0} | all-to-all | bytes 32768 | tf_op jit(solution)/shard_map/all_to_all | solution.py:275
  30.1 0.7 %shard_map.88 = (f32[8]{0:T(128)}, f32[8]{0:T(128)}, f32[4]{0:T(128)}) custom-call(f32[32,128]{1,0:T(8,128)S(1)} %bitcast.3, f32[8,128]{1,0:T(8,128)S(1)} %get-tuple-element.10.meta_ref), custom_call_target="tpu_custom_call" | custom-call | tf_op jit(solution)/shard_map/pallas_call | solution.py:261
  (1 shorter events, 0.0 us)
Async XLA Ops:
  0.6 9.2 %collective-permute-start = (bf16[4096,256]{1,0:T(8,128)(2,1)}, bf16[4096,256]{1,0:T(8,128)(2,1)}, u32[]{:S(2)}, u32[]{:S(2)}) collective-permute-start(bf16[4096,256]{1,0:T(8,128)(2,1)} %own_ref.1), channel_id=1, source_target_pairs={{0,1},{1,0},{2,3},{3,2},{4,5},{5,4},{6,7},{7,6},{8,9},{9,8},{10,11... | collective-permute-start | bytes 6291464 | tf_op jit(solution)/shard_map/ppermute | solution.py:223
  3.0 14.7 %all-to-all-start = ((bf16[8,8,1152]{2,1,0:T(8,128)(2,1)}), bf16[8,8,1152]{2,1,0:T(8,128)(2,1)S(1)}, u32[]{:S(2)}, u32[]{:S(2)}) async-start(bf16[8,8,1152]{2,1,0:T(8,128)(2,1)} %shard_map.85), calls=%async_computation | async-start | bytes 294912 | tf_op jit(solution)/shard_map/all_to_all | solution.py:233

commit v11 on v9

--- a/solution.py
+++ b/solution.py
@@ -128,12 +128,27 @@
     for q in range(1, groups):
         meta = meta + rows_ref[q, :, span:].astype(jnp.float32)
     meta_ref[...] = meta
-    own_logits = jnp.dot(ordered_ref[...], own_ref[...], preferred_element_type=jnp.float32)
-    other_logits = jnp.dot(ordered_ref[:, :staged], upper_ref[...], preferred_element_type=jnp.float32)
+    chunk = 512
+
+    def product(slice_ref, first):
+        def step(i, sums):
+            at = pl.multiple_of(first + i * chunk, chunk)
+            left = ordered_ref[:, pl.ds(at, chunk)]
+            own = own_ref[pl.ds(at, chunk), :]
+            other = slice_ref[pl.ds(pl.multiple_of(i * chunk, chunk), chunk), :]
+            return (
+                sums[0] + jnp.dot(left, own, preferred_element_type=jnp.float32),
+                sums[1] + jnp.dot(left, other, preferred_element_type=jnp.float32),
+            )
+
+        return step
+
+    zeros = jnp.zeros((share, cols), jnp.float32)
+    sums = lax.fori_loop(0, staged // chunk, product(upper_ref, 0), (zeros, zeros))
     for copy in copies:
         copy.wait()
-    other_logits += jnp.dot(ordered_ref[:, staged:], lower_ref[...], preferred_element_type=jnp.float32)
-    logits = jnp.concatenate([own_logits, other_logits], axis=1)
+    sums = lax.fori_loop(0, (width - staged) // chunk, product(lower_ref, staged), sums)
+    logits = jnp.concatenate(sums, axis=1)
     lanes = max(share, LANES)
     sub, lane = iota((share, lanes), 0), iota((share, lanes), 1)
     ids = meta[0:1, :lanes] + 256.0 * meta[1:2, :lanes] + 65536.0 * meta[2:3, :lanes]

time: 30.5 us -> 30.5 us (level)
  no operation moved by 1% of the time
where the time goes in v11:
time: 30.5 us; the launch traced here: 30.2 us
  blocking collectives  9.8 us (32%)
  starting transfers between devices  7.36 us (24%)
  Pallas kernels  6.42 us (21%)
  waiting for transfers between devices  5.98 us (20%)
  between operations  0.66 us (2%)
    all_to_all x1, blocking collectives, sent_to_all(): return lax.all_to_all(copies, axis, 0, 0).reshape((-1,) + block.shape[1:])  9.8 us
    all_to_all x1, starting transfers between devices, local(): rows = lax.all_to_all(packed, 'req', 0, 0)  6.85 us
    all_to_all x1, waiting for transfers between devices, local(): rows = lax.all_to_all(packed, 'req', 0, 0)  5.98 us
    pallas_call x1, Pallas kernels, local(): pl.pallas_call(score_kernel, out_shape=(jax.ShapeDtypeStruct((1, STATS *...  2.16 us
    pallas_call x1, Pallas kernels, local(): pl.pallas_call(stage_kernel, out_shape=(VMEM(lm_head.shape, lm_head.dtype...  1.89 us
    pallas_call x1, Pallas kernels, local(): pl.pallas_call(functools.partial(pack_kernel, share), out_shape=VMEM((gro...  1.68 us
    pallas_call x1, Pallas kernels, local(): pl.pallas_call(functools.partial(finish_kernel, share), out_shape=(jax.Sh...  0.69 us
  transfers between devices with their start and end apart: 2, of which 1 were waited for; matrix products, arithmetic and copies ran while one was open for 0% of the time, Pallas kernels for 12%

profile of v11, /device:TPU:0, one launch (start us, length us, event | category | flops | bytes accessed | tf_op | source)
XLA Modules:
  0.0 30.2 jit_solution(15626415267238333774)
XLA Ops:
  0.6 0.5 %collective-permute-start = (bf16[4096,256]{1,0:T(8,128)(2,1)}, bf16[4096,256]{1,0:T(8,128)(2,1)}, u32[]{:S(2)}, u32[]{:S(2)}) collective-permute-start(bf16[4096,256]{1,0:T(8,128)(2,1)} %own_ref.1), channel_id=1, source_target_pairs={{0,1},{1,0},{2,3},{3,2},{4,5},{5,4},{6,7},{7,6},{8,9},{9,8},{10,11... | collective-permute-start | bytes 6291464 | tf_op jit(solution)/shard_map/ppermute | solution.py:229
  1.1 1.7 %shard_map.85 = bf16[8,8,1152]{2,1,0:T(8,128)(2,1)} custom-call(bf16[8,4096]{1,0:T(8,128)(2,1)} %hidden_ref.1, bf16[32,128]{1,0:T(8,128)(2,1)} %bitcast.5, s32[8]{0:T(128)} %targets_ref.1, s32[8]{0:T(128)} %segments_ref.1, s32[8]{0:T(128)} %scored_ref.1), custom_call_target="tpu_custom_call" | custom-call | tf_op jit(solution)/shard_map/pallas_call | solution.py:230
  2.8 6.8 %all-to-all-start = ((bf16[8,8,1152]{2,1,0:T(8,128)(2,1)}), bf16[8,8,1152]{2,1,0:T(8,128)(2,1)S(1)}, u32[]{:S(2)}, u32[]{:S(2)}) async-start(bf16[8,8,1152]{2,1,0:T(8,128)(2,1)} %shard_map.85), calls=%async_computation | async-start | bytes 294912 | tf_op jit(solution)/shard_map/all_to_all | solution.py:241
  9.7 0.0 collective-permute-done.other_ref
  9.7 1.9 %shard_map.86 = (bf16[4096,256]{1,0:T(8,128)(2,1)S(1)}, bf16[2048,256]{1,0:T(8,128)(2,1)S(1)}) custom-call(bf16[4096,256]{1,0:T(8,128)(2,1)} %own_ref.1, bf16[4096,256]{1,0:T(8,128)(2,1)} %collective-permute-done.other_ref), custom_call_target="tpu_custom_call" | custom-call | bytes 6291456 | tf_op jit(solution)/shard_map/pallas_call | solution.py:244
  11.6 6.0 %all-to-all-done.rows_ref = bf16[8,8,1152]{2,1,0:T(8,128)(2,1)S(1)} async-done(((bf16[8,8,1152]{2,1,0:T(8,128)(2,1)}), bf16[8,8,1152]{2,1,0:T(8,128)(2,1)S(1)}, u32[]{:S(2)}, u32[]{:S(2)}) %all-to-all-start) | async-done | bytes 147488 | tf_op jit(solution)/shard_map/all_to_all | solution.py:241
  17.6 2.2 %shard_map.87 = (f32[1,128]{1,0:T(1,128)S(1)}, f32[8,128]{1,0:T(8,128)S(1)}) custom-call(bf16[8,8,1152]{2,1,0:T(8,128)(2,1)S(1)} %all-to-all-done.rows_ref, bf16[4096,256]{1,0:T(8,128)(2,1)S(1)} %get-tuple-element.7.own_ref, bf16[2048,256]{1,0:T(8,128)(2,1)S(1)} %get-tuple-element.8.upper_ref, bf16[4096,256]{1,0:T(8,128)(2,1)} %collective-permute-done.other_ref), custom_call_target="tpu_custom_call" | custom-call | tf_op jit(solution)/shard_map/pallas_call | solution.py:253
  19.7 9.8 %all_to_all.10 = f32[32,1,128]{2,1,0:T(1,128)S(1)} all-to-all(f32[32,1,128]{2,1,0:T(1,128)S(1)} %broadcast_in_dim.9), channel_id=1, replica_groups=mesh['req'=8,'tp'=4] {'req','tp'}, dimensions={0} | all-to-all | bytes 32768 | tf_op jit(solution)/shard_map/all_to_all | solution.py:283
  29.5 0.7 %shard_map.88 = (f32[8]{0:T(128)}, f32[8]{0:T(128)}, f32[4]{0:T(128)}) custom-call(f32[32,128]{1,0:T(8,128)S(1)} %bitcast.3, f32[8,128]{1,0:T(8,128)S(1)} %get-tuple-element.10.meta_ref), custom_call_target="tpu_custom_call" | custom-call | tf_op jit(solution)/shard_map/pallas_call | solution.py:269
  (1 shorter events, 0.0 us)
Async XLA Ops:
  0.6 9.0 %collective-permute-start = (bf16[4096,256]{1,0:T(8,128)(2,1)}, bf16[4096,256]{1,0:T(8,128)(2,1)}, u32[]{:S(2)}, u32[]{:S(2)}) collective-permute-start(bf16[4096,256]{1,0:T(8,128)(2,1)} %own_ref.1), channel_id=1, source_target_pairs={{0,1},{1,0},{2,3},{3,2},{4,5},{5,4},{6,7},{7,6},{8,9},{9,8},{10,11... | collective-permute-start | bytes 6291464 | tf_op jit(solution)/shard_map/ppermute | solution.py:229
  2.8 14.7 %all-to-all-start = ((bf16[8,8,1152]{2,1,0:T(8,128)(2,1)}), bf16[8,8,1152]{2,1,0:T(8,128)(2,1)S(1)}, u32[]{:S(2)}, u32[]{:S(2)}) async-start(bf16[8,8,1152]{2,1,0:T(8,128)(2,1)} %shard_map.85), calls=%async_computation | async-start | bytes 294912 | tf_op jit(solution)/shard_map/all_to_all | solution.py:241

commit v12 on v9

--- a/solution.py
+++ b/solution.py
@@ -31,11 +31,21 @@
     return lax.broadcasted_iota(jnp.int32, shape, axis)
 
 
+def middle_first(count):
+    quarter = count // 4
+    return [*range(quarter, count - quarter), *range(quarter), *range(count - quarter, count)]
+
+
+def own_slot(count):
+    own, quarter = lax.axis_index("req"), count // 4
+    return jnp.where(own < quarter, own + count - 2 * quarter, jnp.where(own < count - quarter, own - quarter, own))
+
+
 def pack_kernel(share, hidden_ref, gain_ref, targets_ref, segments_ref, scored_ref, out_ref, wide_ref, parts_ref, gains_ref):
     row_count, width = hidden_ref.shape
     parts = SUBS // MINE
     span = width // parts
-    own, half = lax.axis_index("req"), lax.axis_index("tp") % PAIR
+    own, half = own_slot(out_ref.shape[0]), lax.axis_index("tp") % PAIR
     wide_ref[...] = hidden_ref[...].astype(jnp.float32)
     gains_ref[...] = gain_ref[...].astype(jnp.float32)
     ranks, count = ranks_of(scored_ref, row_count)
@@ -185,7 +195,7 @@
     logprob = jnp.where(in_use, picked - log_norm, 0.0)
     entropy = jnp.where(in_use, log_norm - row_weighted / row_total, 0.0)
     segment, place = meta_ref[3:4, :].astype(jnp.int32), meta_ref[5:6, :].astype(jnp.int32)
-    mine = jnp.logical_and(place == sub, lane % share // MINE == lax.axis_index("req"))
+    mine = jnp.logical_and(place == sub, lane % share // MINE == own_slot(share // MINE))
 
     def placed(values, wanted):
         sums = jnp.sum(jnp.where(wanted, values, 0.0), axis=1, keepdims=True)
@@ -223,7 +233,7 @@
             VMEM((width // LANES, LANES), jnp.float32),
         ],
     )(hidden, norm_gain.reshape(width // LANES, LANES), targets, segments, scored)
-    rows = lax.all_to_all(packed, "req", 0, 0)
+    rows = lax.all_to_all(packed, "req", 0, 0, axis_index_groups=[middle_first(groups)])
     other = pltpu.with_memory_space_constraint(other, pltpu.HBM)
     staged = width // 2
     slices = pl.pallas_call(
@@ -250,7 +260,10 @@
         ],
         compiler_params=grant(24),
     )(rows, *(pltpu.with_memory_space_constraint(part, VMEM) for part in slices), other)
-    gathered = sent_to_all(stats, ("req", "tp"))
+    copies = jnp.broadcast_to(stats[None], (groups * tp_count,) + stats.shape)
+    members = [q * tp_count + t for q in middle_first(groups) for t in range(tp_count)]
+    gathered = lax.all_to_all(copies, ("req", "tp"), 0, 0, axis_index_groups=[members])
+    gathered = gathered.reshape(groups * tp_count, stats.shape[1])
     return pl.pallas_call(
         functools.partial(finish_kernel, share),
         out_shape=(
@@ -263,11 +276,6 @@
     )(pltpu.with_memory_space_constraint(gathered, VMEM), pltpu.with_memory_space_constraint(meta, VMEM))
 
 
-def sent_to_all(block, axis):
-    copies = jnp.broadcast_to(block[None], (lax.axis_size(axis),) + block.shape)
-    return lax.all_to_all(copies, axis, 0, 0).reshape((-1,) + block.shape[1:])
-
-
 def solution(mesh):
     return jax.shard_map(
         local,

time: 30.5 us -> 29.5 us (0.967)
  waiting for transfers between devices: 5.98 us -> 4.61 us
  starting transfers between devices: 7.36 us -> 7.93 us
    all_to_all x1, waiting for transfers between devices: 5.98 us -> 4.61 us  [local(): lax.all_to_all(packed, 'req', 0, 0, axis_index_groups=[middle_first(group...]
    all_to_all x1, starting transfers between devices: 6.85 us -> 7.41 us  [local(): lax.all_to_all(packed, 'req', 0, 0, axis_index_groups=[middle_first(group...]
where the time goes in v12:
time: 29.5 us; the launch traced here: 29.2 us
  blocking collectives  9.66 us (33%)
  starting transfers between devices  7.93 us (27%)
  Pallas kernels  6.33 us (21%)
  waiting for transfers between devices  4.61 us (16%)
  between operations  0.66 us (2%)
    all_to_all x1, blocking collectives, local(): lax.all_to_all(copies, ('req', 'tp'), 0, 0, axis_index_groups=[members])  9.66 us
    all_to_all x1, starting transfers between devices, local(): lax.all_to_all(packed, 'req', 0, 0, axis_index_groups=[middle_first(group...  7.41 us
    all_to_all x1, waiting for transfers between devices, local(): lax.all_to_all(packed, 'req', 0, 0, axis_index_groups=[middle_first(group...  4.61 us
    pallas_call x1, Pallas kernels, local(): pl.pallas_call(score_kernel, out_shape=(jax.ShapeDtypeStruct((1, STATS *...  2.08 us
    pallas_call x1, Pallas kernels, local(): pl.pallas_call(stage_kernel, out_shape=(VMEM(lm_head.shape, lm_head.dtype...  1.89 us
    pallas_call x1, Pallas kernels, local(): pl.pallas_call(functools.partial(pack_kernel, share), out_shape=VMEM((gro...  1.68 us
    pallas_call x1, Pallas kernels, local(): pl.pallas_call(functools.partial(finish_kernel, share), out_shape=(jax.Sh...  0.69 us
  transfers between devices with their start and end apart: 2, of which 1 were waited for; matrix products, arithmetic and copies ran while one was open for 0% of the time, Pallas kernels for 12%

profile of v12, /device:TPU:0, one launch (start us, length us, event | category | flops | bytes accessed | tf_op | source)
XLA Modules:
  0.0 29.2 jit_solution(17297732892112861017)
XLA Ops:
  0.6 0.5 %collective-permute-start = (bf16[4096,256]{1,0:T(8,128)(2,1)}, bf16[4096,256]{1,0:T(8,128)(2,1)}, u32[]{:S(2)}, u32[]{:S(2)}) collective-permute-start(bf16[4096,256]{1,0:T(8,128)(2,1)} %own_ref.1), channel_id=1, source_target_pairs={{0,1},{1,0},{2,3},{3,2},{4,5},{5,4},{6,7},{7,6},{8,9},{9,8},{10,11... | collective-permute-start | bytes 6291464 | tf_op jit(solution)/shard_map/ppermute | solution.py:224
  1.1 1.7 %shard_map.85 = bf16[8,8,1152]{2,1,0:T(8,128)(2,1)} custom-call(bf16[8,4096]{1,0:T(8,128)(2,1)} %hidden_ref.1, bf16[32,128]{1,0:T(8,128)(2,1)} %bitcast.5, s32[8]{0:T(128)} %targets_ref.1, s32[8]{0:T(128)} %segments_ref.1, s32[8]{0:T(128)} %scored_ref.1), custom_call_target="tpu_custom_call" | custom-call | tf_op jit(solution)/shard_map/pallas_call | solution.py:225
  2.8 7.4 %all-to-all-start = ((bf16[8,8,1152]{2,1,0:T(8,128)(2,1)}), bf16[8,8,1152]{2,1,0:T(8,128)(2,1)S(1)}, u32[]{:S(2)}, u32[]{:S(2)}) async-start(bf16[8,8,1152]{2,1,0:T(8,128)(2,1)} %shard_map.85), calls=%async_computation | async-start | bytes 294912 | tf_op jit(solution)/shard_map/all_to_all | solution.py:236
  10.2 0.0 collective-permute-done.other_ref
  10.2 1.9 %shard_map.86 = (bf16[4096,256]{1,0:T(8,128)(2,1)S(1)}, bf16[2048,256]{1,0:T(8,128)(2,1)S(1)}) custom-call(bf16[4096,256]{1,0:T(8,128)(2,1)} %own_ref.1, bf16[4096,256]{1,0:T(8,128)(2,1)} %collective-permute-done.other_ref), custom_call_target="tpu_custom_call" | custom-call | bytes 6291456 | tf_op jit(solution)/shard_map/pallas_call | solution.py:239
  12.1 4.6 %all-to-all-done.rows_ref = bf16[8,8,1152]{2,1,0:T(8,128)(2,1)S(1)} async-done(((bf16[8,8,1152]{2,1,0:T(8,128)(2,1)}), bf16[8,8,1152]{2,1,0:T(8,128)(2,1)S(1)}, u32[]{:S(2)}, u32[]{:S(2)}) %all-to-all-start) | async-done | bytes 147488 | tf_op jit(solution)/shard_map/all_to_all | solution.py:236
  16.7 2.1 %shard_map.87 = (f32[1,128]{1,0:T(1,128)S(1)}, f32[8,128]{1,0:T(8,128)S(1)}) custom-call(bf16[8,8,1152]{2,1,0:T(8,128)(2,1)S(1)} %all-to-all-done.rows_ref, bf16[4096,256]{1,0:T(8,128)(2,1)S(1)} %get-tuple-element.7.own_ref, bf16[2048,256]{1,0:T(8,128)(2,1)S(1)} %get-tuple-element.8.upper_ref, bf16[4096,256]{1,0:T(8,128)(2,1)} %collective-permute-done.other_ref), custom_call_target="tpu_custom_call" | custom-call | tf_op jit(solution)/shard_map/pallas_call | solution.py:248
  18.8 9.7 %all_to_all.10 = f32[32,1,128]{2,1,0:T(1,128)S(1)} all-to-all(f32[32,1,128]{2,1,0:T(1,128)S(1)} %broadcast_in_dim.9), channel_id=1, replica_groups={{8,9,10,11,12,13,14,15,16,17,18,19,20,21,22,23,0,1,2,3,4,5,6,7,24,25,26..., dimensions={0} | all-to-all | bytes 32768 | tf_op jit(solution)/shard_map/all_to_all | solution.py:265
  28.5 0.7 %shard_map.88 = (f32[8]{0:T(128)}, f32[8]{0:T(128)}, f32[4]{0:T(128)}) custom-call(f32[32,128]{1,0:T(8,128)S(1)} %bitcast.3, f32[8,128]{1,0:T(8,128)S(1)} %get-tuple-element.10.meta_ref), custom_call_target="tpu_custom_call" | custom-call | tf_op jit(solution)/shard_map/pallas_call | solution.py:267
  (1 shorter events, 0.0 us)
Async XLA Ops:
  0.6 9.6 %collective-permute-start = (bf16[4096,256]{1,0:T(8,128)(2,1)}, bf16[4096,256]{1,0:T(8,128)(2,1)}, u32[]{:S(2)}, u32[]{:S(2)}) collective-permute-start(bf16[4096,256]{1,0:T(8,128)(2,1)} %own_ref.1), channel_id=1, source_target_pairs={{0,1},{1,0},{2,3},{3,2},{4,5},{5,4},{6,7},{7,6},{8,9},{9,8},{10,11... | collective-permute-start | bytes 6291464 | tf_op jit(solution)/shard_map/ppermute | solution.py:224
  2.8 13.9 %all-to-all-start = ((bf16[8,8,1152]{2,1,0:T(8,128)(2,1)}), bf16[8,8,1152]{2,1,0:T(8,128)(2,1)S(1)}, u32[]{:S(2)}, u32[]{:S(2)}) async-start(bf16[8,8,1152]{2,1,0:T(8,128)(2,1)} %shard_map.85), calls=%async_computation | async-start | bytes 294912 | tf_op jit(solution)/shard_map/all_to_all | solution.py:236

commit v13 on v12

--- a/solution.py
+++ b/solution.py
@@ -31,14 +31,8 @@
     return lax.broadcasted_iota(jnp.int32, shape, axis)
 
 
-def middle_first(count):
-    quarter = count // 4
-    return [*range(quarter, count - quarter), *range(quarter), *range(count - quarter, count)]
-
-
 def own_slot(count):
-    own, quarter = lax.axis_index("req"), count // 4
-    return jnp.where(own < quarter, own + count - 2 * quarter, jnp.where(own < count - quarter, own - quarter, own))
+    return count - 1 - lax.axis_index("req")
 
 
 def pack_kernel(share, hidden_ref, gain_ref, targets_ref, segments_ref, scored_ref, out_ref, wide_ref, parts_ref, gains_ref):
@@ -233,7 +227,7 @@
             VMEM((width // LANES, LANES), jnp.float32),
         ],
     )(hidden, norm_gain.reshape(width // LANES, LANES), targets, segments, scored)
-    rows = lax.all_to_all(packed, "req", 0, 0, axis_index_groups=[middle_first(groups)])
+    rows = lax.all_to_all(packed, "req", 0, 0, axis_index_groups=[[*reversed(range(groups))]])
     other = pltpu.with_memory_space_constraint(other, pltpu.HBM)
     staged = width // 2
     slices = pl.pallas_call(
@@ -261,7 +255,7 @@
         compiler_params=grant(24),
     )(rows, *(pltpu.with_memory_space_constraint(part, VMEM) for part in slices), other)
     copies = jnp.broadcast_to(stats[None], (groups * tp_count,) + stats.shape)
-    members = [q * tp_count + t for q in middle_first(groups) for t in range(tp_count)]
+    members = [*reversed(range(groups * tp_count))]
     gathered = lax.all_to_all(copies, ("req", "tp"), 0, 0, axis_index_groups=[members])
     gathered = gathered.reshape(groups * tp_count, stats.shape[1])
     return pl.pallas_call(

time: 29.5 us -> 31.2 us (1.058)
  blocking collectives: 9.66 us -> 11.4 us
  waiting for transfers between devices: 4.61 us -> 3.05 us
  starting transfers between devices: 7.93 us -> 9.41 us
    all_to_all x1, blocking collectives: 9.66 us -> 11.4 us  [local(): lax.all_to_all(copies, ('req', 'tp'), 0, 0, axis_index_groups=[members])]
    all_to_all x1, waiting for transfers between devices: 4.61 us -> 3.05 us  [local(): lax.all_to_all(packed, 'req', 0, 0, axis_index_groups=[[*reversed(range(g...]
    all_to_all x1, starting transfers between devices: 7.41 us -> 8.89 us  [local(): lax.all_to_all(packed, 'req', 0, 0, axis_index_groups=[[*reversed(range(g...]
where the time goes in v13:
time: 31.2 us; the launch traced here: 30.9 us
  blocking collectives  11.4 us (37%)
  starting transfers between devices  9.41 us (30%)
  Pallas kernels  6.33 us (20%)
  waiting for transfers between devices  3.05 us (10%)
  between operations  0.66 us (2%)
    all_to_all x1, blocking collectives, local(): lax.all_to_all(copies, ('req', 'tp'), 0, 0, axis_index_groups=[members])  11.4 us
    all_to_all x1, starting transfers between devices, local(): lax.all_to_all(packed, 'req', 0, 0, axis_index_groups=[[*reversed(range(g...  8.89 us
    all_to_all x1, waiting for transfers between devices, local(): lax.all_to_all(packed, 'req', 0, 0, axis_index_groups=[[*reversed(range(g...  3.05 us
    pallas_call x1, Pallas kernels, local(): pl.pallas_call(score_kernel, out_shape=(jax.ShapeDtypeStruct((1, STATS *...  2.08 us
    pallas_call x1, Pallas kernels, local(): pl.pallas_call(stage_kernel, out_shape=(VMEM(lm_head.shape, lm_head.dtype...  1.89 us
    pallas_call x1, Pallas kernels, local(): pl.pallas_call(functools.partial(pack_kernel, share), out_shape=VMEM((gro...  1.68 us
    pallas_call x1, Pallas kernels, local(): pl.pallas_call(functools.partial(finish_kernel, share), out_shape=(jax.Sh...  0.69 us
  transfers between devices with their start and end apart: 2, of which 1 were waited for; matrix products, arithmetic and copies ran while one was open for 0% of the time, Pallas kernels for 12%

profile of v13, /device:TPU:0, one launch (start us, length us, event | category | flops | bytes accessed | tf_op | source)
XLA Modules:
  0.0 30.9 jit_solution(2252423008102203580)
XLA Ops:
  0.6 0.5 %collective-permute-start = (bf16[4096,256]{1,0:T(8,128)(2,1)}, bf16[4096,256]{1,0:T(8,128)(2,1)}, u32[]{:S(2)}, u32[]{:S(2)}) collective-permute-start(bf16[4096,256]{1,0:T(8,128)(2,1)} %own_ref.1), channel_id=1, source_target_pairs={{0,1},{1,0},{2,3},{3,2},{4,5},{5,4},{6,7},{7,6},{8,9},{9,8},{10,11... | collective-permute-start | bytes 6291464 | tf_op jit(solution)/shard_map/ppermute | solution.py:218
  1.1 1.7 %shard_map.85 = bf16[8,8,1152]{2,1,0:T(8,128)(2,1)} custom-call(bf16[8,4096]{1,0:T(8,128)(2,1)} %hidden_ref.1, bf16[32,128]{1,0:T(8,128)(2,1)} %bitcast.5, s32[8]{0:T(128)} %targets_ref.1, s32[8]{0:T(128)} %segments_ref.1, s32[8]{0:T(128)} %scored_ref.1), custom_call_target="tpu_custom_call" | custom-call | tf_op jit(solution)/shard_map/pallas_call | solution.py:219
  2.8 8.9 %all-to-all-start = ((bf16[8,8,1152]{2,1,0:T(8,128)(2,1)}), bf16[8,8,1152]{2,1,0:T(8,128)(2,1)S(1)}, u32[]{:S(2)}, u32[]{:S(2)}) async-start(bf16[8,8,1152]{2,1,0:T(8,128)(2,1)} %shard_map.85), calls=%async_computation | async-start | bytes 294912 | tf_op jit(solution)/shard_map/all_to_all | solution.py:230
  11.7 0.0 collective-permute-done.other_ref
  11.7 1.9 %shard_map.86 = (bf16[4096,256]{1,0:T(8,128)(2,1)S(1)}, bf16[2048,256]{1,0:T(8,128)(2,1)S(1)}) custom-call(bf16[4096,256]{1,0:T(8,128)(2,1)} %own_ref.1, bf16[4096,256]{1,0:T(8,128)(2,1)} %collective-permute-done.other_ref), custom_call_target="tpu_custom_call" | custom-call | bytes 6291456 | tf_op jit(solution)/shard_map/pallas_call | solution.py:233
  13.6 3.1 %all-to-all-done.rows_ref = bf16[8,8,1152]{2,1,0:T(8,128)(2,1)S(1)} async-done(((bf16[8,8,1152]{2,1,0:T(8,128)(2,1)}), bf16[8,8,1152]{2,1,0:T(8,128)(2,1)S(1)}, u32[]{:S(2)}, u32[]{:S(2)}) %all-to-all-start) | async-done | bytes 147488 | tf_op jit(solution)/shard_map/all_to_all | solution.py:230
  16.7 2.1 %shard_map.87 = (f32[1,128]{1,0:T(1,128)S(1)}, f32[8,128]{1,0:T(8,128)S(1)}) custom-call(bf16[8,8,1152]{2,1,0:T(8,128)(2,1)S(1)} %all-to-all-done.rows_ref, bf16[4096,256]{1,0:T(8,128)(2,1)S(1)} %get-tuple-element.7.own_ref, bf16[2048,256]{1,0:T(8,128)(2,1)S(1)} %get-tuple-element.8.upper_ref, bf16[4096,256]{1,0:T(8,128)(2,1)} %collective-permute-done.other_ref), custom_call_target="tpu_custom_call" | custom-call | tf_op jit(solution)/shard_map/pallas_call | solution.py:242
  18.8 11.4 %all_to_all.10 = f32[32,1,128]{2,1,0:T(1,128)S(1)} all-to-all(f32[32,1,128]{2,1,0:T(1,128)S(1)} %broadcast_in_dim.9), channel_id=1, replica_groups={{31,30,29,28,27,26,25,24,23,22,21,20,19,18,17,16,15,14,13,12,11,10,9,8,..., dimensions={0} | all-to-all | bytes 32768 | tf_op jit(solution)/shard_map/all_to_all | solution.py:259
  30.2 0.7 %shard_map.88 = (f32[8]{0:T(128)}, f32[8]{0:T(128)}, f32[4]{0:T(128)}) custom-call(f32[32,128]{1,0:T(8,128)S(1)} %bitcast.3, f32[8,128]{1,0:T(8,128)S(1)} %get-tuple-element.10.meta_ref), custom_call_target="tpu_custom_call" | custom-call | tf_op jit(solution)/shard_map/pallas_call | solution.py:261
  (1 shorter events, 0.0 us)
Async XLA Ops:
  0.6 11.1 %collective-permute-start = (bf16[4096,256]{1,0:T(8,128)(2,1)}, bf16[4096,256]{1,0:T(8,128)(2,1)}, u32[]{:S(2)}, u32[]{:S(2)}) collective-permute-start(bf16[4096,256]{1,0:T(8,128)(2,1)} %own_ref.1), channel_id=1, source_target_pairs={{0,1},{1,0},{2,3},{3,2},{4,5},{5,4},{6,7},{7,6},{8,9},{9,8},{10,11... | collective-permute-start | bytes 6291464 | tf_op jit(solution)/shard_map/ppermute | solution.py:218
  2.8 13.8 %all-to-all-start = ((bf16[8,8,1152]{2,1,0:T(8,128)(2,1)}), bf16[8,8,1152]{2,1,0:T(8,128)(2,1)S(1)}, u32[]{:S(2)}, u32[]{:S(2)}) async-start(bf16[8,8,1152]{2,1,0:T(8,128)(2,1)} %shard_map.85), calls=%async_computation | async-start | bytes 294912 | tf_op jit(solution)/shard_map/all_to_all | solution.py:230

commit v14 on v12

--- a/solution.py
+++ b/solution.py
@@ -33,11 +33,12 @@
 
 def middle_first(count):
     quarter = count // 4
-    return [*range(quarter, count - quarter), *range(quarter), *range(count - quarter, count)]
+    order = [*range(quarter, count - quarter), *range(quarter), *range(count - quarter, count)]
+    return [count - 1 - index for index in order]
 
 
 def own_slot(count):
-    own, quarter = lax.axis_index("req"), count // 4
+    own, quarter = count - 1 - lax.axis_index("req"), count // 4
     return jnp.where(own < quarter, own + count - 2 * quarter, jnp.where(own < count - quarter, own - quarter, own))
 
 

time: 29.5 us -> 30.3 us (1.027)
  blocking collectives: 9.66 us -> 12.2 us
  waiting for transfers between devices: 4.61 us -> 2.41 us
  starting transfers between devices: 7.93 us -> 8.39 us
    all_to_all x1, blocking collectives: 9.66 us -> 12.2 us  [local(): lax.all_to_all(copies, ('req', 'tp'), 0, 0, axis_index_groups=[members])]
    all_to_all x1, waiting for transfers between devices: 4.61 us -> 2.41 us  [local(): lax.all_to_all(packed, 'req', 0, 0, axis_index_groups=[middle_first(group...]
    all_to_all x1, starting transfers between devices: 7.41 us -> 7.88 us  [local(): lax.all_to_all(packed, 'req', 0, 0, axis_index_groups=[middle_first(group...]
where the time goes in v14:
time: 30.3 us; the launch traced here: 30 us
  blocking collectives  12.2 us (40%)
  starting transfers between devices  8.39 us (28%)
  Pallas kernels  6.33 us (21%)
  waiting for transfers between devices  2.41 us (8%)
  between operations  0.66 us (2%)
    all_to_all x1, blocking collectives, local(): lax.all_to_all(copies, ('req', 'tp'), 0, 0, axis_index_groups=[members])  12.2 us
    all_to_all x1, starting transfers between devices, local(): lax.all_to_all(packed, 'req', 0, 0, axis_index_groups=[middle_first(group...  7.88 us
    all_to_all x1, waiting for transfers between devices, local(): lax.all_to_all(packed, 'req', 0, 0, axis_index_groups=[middle_first(group...  2.41 us
    pallas_call x1, Pallas kernels, local(): pl.pallas_call(score_kernel, out_shape=(jax.ShapeDtypeStruct((1, STATS *...  2.08 us
    pallas_call x1, Pallas kernels, local(): pl.pallas_call(stage_kernel, out_shape=(VMEM(lm_head.shape, lm_head.dtype...  1.89 us
    pallas_call x1, Pallas kernels, local(): pl.pallas_call(functools.partial(pack_kernel, share), out_shape=VMEM((gro...  1.68 us
    pallas_call x1, Pallas kernels, local(): pl.pallas_call(functools.partial(finish_kernel, share), out_shape=(jax.Sh...  0.69 us
  transfers between devices with their start and end apart: 2, of which 1 were waited for; matrix products, arithmetic and copies ran while one was open for 0% of the time, Pallas kernels for 12%

profile of v14, /device:TPU:0, one launch (start us, length us, event | category | flops | bytes accessed | tf_op | source)
XLA Modules:
  0.0 30.0 jit_solution(6741754048015546783)
XLA Ops:
  0.6 0.5 %collective-permute-start = (bf16[4096,256]{1,0:T(8,128)(2,1)}, bf16[4096,256]{1,0:T(8,128)(2,1)}, u32[]{:S(2)}, u32[]{:S(2)}) collective-permute-start(bf16[4096,256]{1,0:T(8,128)(2,1)} %own_ref.1), channel_id=1, source_target_pairs={{0,1},{1,0},{2,3},{3,2},{4,5},{5,4},{6,7},{7,6},{8,9},{9,8},{10,11... | collective-permute-start | bytes 6291464 | tf_op jit(solution)/shard_map/ppermute | solution.py:225
  1.1 1.7 %shard_map.85 = bf16[8,8,1152]{2,1,0:T(8,128)(2,1)} custom-call(bf16[8,4096]{1,0:T(8,128)(2,1)} %hidden_ref.1, bf16[32,128]{1,0:T(8,128)(2,1)} %bitcast.5, s32[8]{0:T(128)} %targets_ref.1, s32[8]{0:T(128)} %segments_ref.1, s32[8]{0:T(128)} %scored_ref.1), custom_call_target="tpu_custom_call" | custom-call | tf_op jit(solution)/shard_map/pallas_call | solution.py:226
  2.8 7.9 %all-to-all-start = ((bf16[8,8,1152]{2,1,0:T(8,128)(2,1)}), bf16[8,8,1152]{2,1,0:T(8,128)(2,1)S(1)}, u32[]{:S(2)}, u32[]{:S(2)}) async-start(bf16[8,8,1152]{2,1,0:T(8,128)(2,1)} %shard_map.85), calls=%async_computation | async-start | bytes 294912 | tf_op jit(solution)/shard_map/all_to_all | solution.py:237
  10.7 0.0 collective-permute-done.other_ref
  10.7 1.9 %shard_map.86 = (bf16[4096,256]{1,0:T(8,128)(2,1)S(1)}, bf16[2048,256]{1,0:T(8,128)(2,1)S(1)}) custom-call(bf16[4096,256]{1,0:T(8,128)(2,1)} %own_ref.1, bf16[4096,256]{1,0:T(8,128)(2,1)} %collective-permute-done.other_ref), custom_call_target="tpu_custom_call" | custom-call | bytes 6291456 | tf_op jit(solution)/shard_map/pallas_call | solution.py:240
  12.6 2.4 %all-to-all-done.rows_ref = bf16[8,8,1152]{2,1,0:T(8,128)(2,1)S(1)} async-done(((bf16[8,8,1152]{2,1,0:T(8,128)(2,1)}), bf16[8,8,1152]{2,1,0:T(8,128)(2,1)S(1)}, u32[]{:S(2)}, u32[]{:S(2)}) %all-to-all-start) | async-done | bytes 147488 | tf_op jit(solution)/shard_map/all_to_all | solution.py:237
  15.0 2.1 %shard_map.87 = (f32[1,128]{1,0:T(1,128)S(1)}, f32[8,128]{1,0:T(8,128)S(1)}) custom-call(bf16[8,8,1152]{2,1,0:T(8,128)(2,1)S(1)} %all-to-all-done.rows_ref, bf16[4096,256]{1,0:T(8,128)(2,1)S(1)} %get-tuple-element.7.own_ref, bf16[2048,256]{1,0:T(8,128)(2,1)S(1)} %get-tuple-element.8.upper_ref, bf16[4096,256]{1,0:T(8,128)(2,1)} %collective-permute-done.other_ref), custom_call_target="tpu_custom_call" | custom-call | tf_op jit(solution)/shard_map/pallas_call | solution.py:249
  17.1 12.2 %all_to_all.10 = f32[32,1,128]{2,1,0:T(1,128)S(1)} all-to-all(f32[32,1,128]{2,1,0:T(1,128)S(1)} %broadcast_in_dim.9), channel_id=1, replica_groups={{20,21,22,23,16,17,18,19,12,13,14,15,8,9,10,11,28,29,30,31,24,25,26,27,..., dimensions={0} | all-to-all | bytes 32768 | tf_op jit(solution)/shard_map/all_to_all | solution.py:266
  29.3 0.7 %shard_map.88 = (f32[8]{0:T(128)}, f32[8]{0:T(128)}, f32[4]{0:T(128)}) custom-call(f32[32,128]{1,0:T(8,128)S(1)} %bitcast.3, f32[8,128]{1,0:T(8,128)S(1)} %get-tuple-element.10.meta_ref), custom_call_target="tpu_custom_call" | custom-call | tf_op jit(solution)/shard_map/pallas_call | solution.py:268
  (1 shorter events, 0.0 us)
Async XLA Ops:
  0.6 10.1 %collective-permute-start = (bf16[4096,256]{1,0:T(8,128)(2,1)}, bf16[4096,256]{1,0:T(8,128)(2,1)}, u32[]{:S(2)}, u32[]{:S(2)}) collective-permute-start(bf16[4096,256]{1,0:T(8,128)(2,1)} %own_ref.1), channel_id=1, source_target_pairs={{0,1},{1,0},{2,3},{3,2},{4,5},{5,4},{6,7},{7,6},{8,9},{9,8},{10,11... | collective-permute-start | bytes 6291464 | tf_op jit(solution)/shard_map/ppermute | solution.py:225
  2.8 12.2 %all-to-all-start = ((bf16[8,8,1152]{2,1,0:T(8,128)(2,1)}), bf16[8,8,1152]{2,1,0:T(8,128)(2,1)S(1)}, u32[]{:S(2)}, u32[]{:S(2)}) async-start(bf16[8,8,1152]{2,1,0:T(8,128)(2,1)} %shard_map.85), calls=%async_computation | async-start | bytes 294912 | tf_op jit(solution)/shard_map/all_to_all | solution.py:237

commit v15 on v13

--- a/solution.py
+++ b/solution.py
@@ -31,8 +31,15 @@
     return lax.broadcasted_iota(jnp.int32, shape, axis)
 
 
+def members(count):
+    quarter = count // 4
+    return [*reversed(range(quarter, count - quarter)), *range(quarter), *range(count - quarter, count)]
+
+
 def own_slot(count):
-    return count - 1 - lax.axis_index("req")
+    own, quarter = lax.axis_index("req"), count // 4
+    middle = count - quarter - 1 - own
+    return jnp.where(own < quarter, own + count - 2 * quarter, jnp.where(own < count - quarter, middle, own))
 
 
 def pack_kernel(share, hidden_ref, gain_ref, targets_ref, segments_ref, scored_ref, out_ref, wide_ref, parts_ref, gains_ref):
@@ -227,7 +234,7 @@
             VMEM((width // LANES, LANES), jnp.float32),
         ],
     )(hidden, norm_gain.reshape(width // LANES, LANES), targets, segments, scored)
-    rows = lax.all_to_all(packed, "req", 0, 0, axis_index_groups=[[*reversed(range(groups))]])
+    rows = lax.all_to_all(packed, "req", 0, 0, axis_index_groups=[members(groups)])
     other = pltpu.with_memory_space_constraint(other, pltpu.HBM)
     staged = width // 2
     slices = pl.pallas_call(
@@ -255,8 +262,7 @@
         compiler_params=grant(24),
     )(rows, *(pltpu.with_memory_space_constraint(part, VMEM) for part in slices), other)
     copies = jnp.broadcast_to(stats[None], (groups * tp_count,) + stats.shape)
-    members = [*reversed(range(groups * tp_count))]
-    gathered = lax.all_to_all(copies, ("req", "tp"), 0, 0, axis_index_groups=[members])
+    gathered = lax.all_to_all(copies, ("req", "tp"), 0, 0)
     gathered = gathered.reshape(groups * tp_count, stats.shape[1])
     return pl.pallas_call(
         functools.partial(finish_kernel, share),

time: 31.2 us -> 29.5 us (0.946)
  starting transfers between devices: 9.41 us -> 8.37 us
  blocking collectives: 11.4 us -> 11 us
    all_to_all x1, starting transfers between devices: 8.89 us -> 7.86 us  [local(): lax.all_to_all(packed, 'req', 0, 0, axis_index_groups=[members(groups)])]
    all_to_all x1, blocking collectives: 11.4 us -> 11 us  [local(): gathered = lax.all_to_all(copies, ('req', 'tp'), 0, 0)]
where the time goes in v15:
time: 29.5 us; the launch traced here: 29.2 us
  blocking collectives  11 us (37%)
  starting transfers between devices  8.37 us (28%)
  Pallas kernels  6.34 us (21%)
  waiting for transfers between devices  2.83 us (10%)
  between operations  0.66 us (2%)
    all_to_all x1, blocking collectives, local(): gathered = lax.all_to_all(copies, ('req', 'tp'), 0, 0)  11 us
    all_to_all x1, starting transfers between devices, local(): lax.all_to_all(packed, 'req', 0, 0, axis_index_groups=[members(groups)])  7.86 us
    all_to_all x1, waiting for transfers between devices, local(): lax.all_to_all(packed, 'req', 0, 0, axis_index_groups=[members(groups)])  2.83 us
    pallas_call x1, Pallas kernels, local(): pl.pallas_call(score_kernel, out_shape=(jax.ShapeDtypeStruct((1, STATS *...  2.08 us
    pallas_call x1, Pallas kernels, local(): pl.pallas_call(stage_kernel, out_shape=(VMEM(lm_head.shape, lm_head.dtype...  1.89 us
    pallas_call x1, Pallas kernels, local(): pl.pallas_call(functools.partial(pack_kernel, share), out_shape=VMEM((gro...  1.68 us
    pallas_call x1, Pallas kernels, local(): pl.pallas_call(functools.partial(finish_kernel, share), out_shape=(jax.Sh...  0.69 us
  transfers between devices with their start and end apart: 2, of which 1 were waited for; matrix products, arithmetic and copies ran while one was open for 0% of the time, Pallas kernels for 12%

profile of v15, /device:TPU:0, one launch (start us, length us, event | category | flops | bytes accessed | tf_op | source)
XLA Modules:
  0.0 29.2 jit_solution(5152947682093632049)
XLA Ops:
  0.6 0.5 %collective-permute-start = (bf16[4096,256]{1,0:T(8,128)(2,1)}, bf16[4096,256]{1,0:T(8,128)(2,1)}, u32[]{:S(2)}, u32[]{:S(2)}) collective-permute-start(bf16[4096,256]{1,0:T(8,128)(2,1)} %own_ref.1), channel_id=1, source_target_pairs={{0,1},{1,0},{2,3},{3,2},{4,5},{5,4},{6,7},{7,6},{8,9},{9,8},{10,11... | collective-permute-start | bytes 6291464 | tf_op jit(solution)/shard_map/ppermute | solution.py:225
  1.1 1.7 %shard_map.85 = bf16[8,8,1152]{2,1,0:T(8,128)(2,1)} custom-call(bf16[8,4096]{1,0:T(8,128)(2,1)} %hidden_ref.1, bf16[32,128]{1,0:T(8,128)(2,1)} %bitcast.5, s32[8]{0:T(128)} %targets_ref.1, s32[8]{0:T(128)} %segments_ref.1, s32[8]{0:T(128)} %scored_ref.1), custom_call_target="tpu_custom_call" | custom-call | tf_op jit(solution)/shard_map/pallas_call | solution.py:226
  2.8 7.9 %all-to-all-start = ((bf16[8,8,1152]{2,1,0:T(8,128)(2,1)}), bf16[8,8,1152]{2,1,0:T(8,128)(2,1)S(1)}, u32[]{:S(2)}, u32[]{:S(2)}) async-start(bf16[8,8,1152]{2,1,0:T(8,128)(2,1)} %shard_map.85), calls=%async_computation | async-start | bytes 294912 | tf_op jit(solution)/shard_map/all_to_all | solution.py:237
  10.7 0.0 collective-permute-done.other_ref
  10.7 1.9 %shard_map.86 = (bf16[4096,256]{1,0:T(8,128)(2,1)S(1)}, bf16[2048,256]{1,0:T(8,128)(2,1)S(1)}) custom-call(bf16[4096,256]{1,0:T(8,128)(2,1)} %own_ref.1, bf16[4096,256]{1,0:T(8,128)(2,1)} %collective-permute-done.other_ref), custom_call_target="tpu_custom_call" | custom-call | bytes 6291456 | tf_op jit(solution)/shard_map/pallas_call | solution.py:240
  12.6 2.8 %all-to-all-done.rows_ref = bf16[8,8,1152]{2,1,0:T(8,128)(2,1)S(1)} async-done(((bf16[8,8,1152]{2,1,0:T(8,128)(2,1)}), bf16[8,8,1152]{2,1,0:T(8,128)(2,1)S(1)}, u32[]{:S(2)}, u32[]{:S(2)}) %all-to-all-start) | async-done | bytes 147488 | tf_op jit(solution)/shard_map/all_to_all | solution.py:237
  15.4 2.1 %shard_map.87 = (f32[1,128]{1,0:T(1,128)S(1)}, f32[8,128]{1,0:T(8,128)S(1)}) custom-call(bf16[8,8,1152]{2,1,0:T(8,128)(2,1)S(1)} %all-to-all-done.rows_ref, bf16[4096,256]{1,0:T(8,128)(2,1)S(1)} %get-tuple-element.7.own_ref, bf16[2048,256]{1,0:T(8,128)(2,1)S(1)} %get-tuple-element.8.upper_ref, bf16[4096,256]{1,0:T(8,128)(2,1)} %collective-permute-done.other_ref), custom_call_target="tpu_custom_call" | custom-call | tf_op jit(solution)/shard_map/pallas_call | solution.py:249
  17.5 11.0 %all_to_all.10 = f32[32,1,128]{2,1,0:T(1,128)S(1)} all-to-all(f32[32,1,128]{2,1,0:T(1,128)S(1)} %broadcast_in_dim.9), channel_id=1, replica_groups=mesh['req'=8,'tp'=4] {'req','tp'}, dimensions={0} | all-to-all | bytes 32768 | tf_op jit(solution)/shard_map/all_to_all | solution.py:265
  28.5 0.7 %shard_map.88 = (f32[8]{0:T(128)}, f32[8]{0:T(128)}, f32[4]{0:T(128)}) custom-call(f32[32,128]{1,0:T(8,128)S(1)} %bitcast.3, f32[8,128]{1,0:T(8,128)S(1)} %get-tuple-element.10.meta_ref), custom_call_target="tpu_custom_call" | custom-call | tf_op jit(solution)/shard_map/pallas_call | solution.py:267
  (1 shorter events, 0.0 us)
Async XLA Ops:
  0.6 10.1 %collective-permute-start = (bf16[4096,256]{1,0:T(8,128)(2,1)}, bf16[4096,256]{1,0:T(8,128)(2,1)}, u32[]{:S(2)}, u32[]{:S(2)}) collective-permute-start(bf16[4096,256]{1,0:T(8,128)(2,1)} %own_ref.1), channel_id=1, source_target_pairs={{0,1},{1,0},{2,3},{3,2},{4,5},{5,4},{6,7},{7,6},{8,9},{9,8},{10,11... | collective-permute-start | bytes 6291464 | tf_op jit(solution)/shard_map/ppermute | solution.py:225
  2.8 12.6 %all-to-all-start = ((bf16[8,8,1152]{2,1,0:T(8,128)(2,1)}), bf16[8,8,1152]{2,1,0:T(8,128)(2,1)S(1)}, u32[]{:S(2)}, u32[]{:S(2)}) async-start(bf16[8,8,1152]{2,1,0:T(8,128)(2,1)} %shard_map.85), calls=%async_computation | async-start | bytes 294912 | tf_op jit(solution)/shard_map/all_to_all | solution.py:237

commit v16 on v15

--- a/solution.py
+++ b/solution.py
@@ -222,7 +222,8 @@
     def spec(space):
         return pl.BlockSpec(memory_space=space)
 
-    other = lax.ppermute(lm_head, "tp", [(i, i + 1 - 2 * (i % PAIR)) for i in range(tp_count)])
+    swap = [(i, i + 1 - 2 * (i % PAIR)) for i in range(tp_count)]
+    other = lax.ppermute(lm_head, "tp", swap)
     packed = pl.pallas_call(
         functools.partial(pack_kernel, share),
         out_shape=VMEM((groups, SUBS, span + lanes), jnp.bfloat16),
@@ -261,9 +262,12 @@
         ],
         compiler_params=grant(24),
     )(rows, *(pltpu.with_memory_space_constraint(part, VMEM) for part in slices), other)
-    copies = jnp.broadcast_to(stats[None], (groups * tp_count,) + stats.shape)
-    gathered = lax.all_to_all(copies, ("req", "tp"), 0, 0)
-    gathered = gathered.reshape(groups * tp_count, stats.shape[1])
+    swapped = lax.ppermute(stats, "tp", swap)
+    stats = jnp.where(iota(stats.shape, 1) < PAIR * share, jnp.maximum(stats, swapped), stats + swapped)
+    chips = groups * tp_count // PAIR
+    copies = jnp.broadcast_to(stats[None], (chips,) + stats.shape)
+    listed = [[q * tp_count + t for q in members(groups) for t in range(at, tp_count, PAIR)] for at in range(PAIR)]
+    gathered = lax.all_to_all(copies, ("req", "tp"), 0, 0, axis_index_groups=listed).reshape(chips, stats.shape[1])
     return pl.pallas_call(
         functools.partial(finish_kernel, share),
         out_shape=(

time: 29.5 us -> 29.9 us (1.014)
  waiting for transfers between devices: 2.83 us -> 3.94 us
  blocking collectives: 11 us -> 10.2 us
    ppermute x1 -> x2, waiting for transfers between devices: 0.01 us -> 1.11 us  [the longest x1 1.11 us: local(): swapped = lax.ppermute(stats, 'tp', swap)]
    all_to_all x1, blocking collectives: 11 us -> 10.2 us  [local(): lax.all_to_all(copies, ('req', 'tp'), 0, 0, axis_index_groups=listed)]
  transfers between devices with their start and end apart: 2 -> 3, of which waited for: 1 -> 2; matrix products, arithmetic and copies ran while one was open for 0% -> 0% of each run, Pallas kernels for 12% -> 12%
where the time goes in v16:
time: 29.9 us; the launch traced here: 29.5 us
  blocking collectives  10.2 us (34%)
  starting transfers between devices  8.44 us (28%)
  Pallas kernels  6.33 us (21%)
  waiting for transfers between devices  3.94 us (13%)
  between operations  0.66 us (2%)
    all_to_all x1, blocking collectives, local(): lax.all_to_all(copies, ('req', 'tp'), 0, 0, axis_index_groups=listed)  10.2 us
    all_to_all x1, starting transfers between devices, local(): lax.all_to_all(packed, 'req', 0, 0, axis_index_groups=[members(groups)])  7.86 us
    all_to_all x1, waiting for transfers between devices, local(): lax.all_to_all(packed, 'req', 0, 0, axis_index_groups=[members(groups)])  2.83 us
    pallas_call x1, Pallas kernels, local(): pl.pallas_call(score_kernel, out_shape=(jax.ShapeDtypeStruct((1, STATS *...  2.08 us
    pallas_call x1, Pallas kernels, local(): pl.pallas_call(stage_kernel, out_shape=(VMEM(lm_head.shape, lm_head.dtype...  1.89 us
    pallas_call x1, Pallas kernels, local(): pl.pallas_call(functools.partial(pack_kernel, share), out_shape=VMEM((gro...  1.68 us
    ppermute x1, waiting for transfers between devices, local(): swapped = lax.ppermute(stats, 'tp', swap)  1.11 us
    pallas_call x1, Pallas kernels, local(): pl.pallas_call(functools.partial(finish_kernel, share), out_shape=(jax.Sh...  0.69 us
  transfers between devices with their start and end apart: 3, of which 2 were waited for; matrix products, arithmetic and copies ran while one was open for 0% of the time, Pallas kernels for 12%

profile of v16, /device:TPU:0, one launch (start us, length us, event | category | flops | bytes accessed | tf_op | source)
XLA Modules:
  0.0 29.5 jit_solution(9445382768094927721)
XLA Ops:
  0.6 0.5 %collective-permute-start = (bf16[4096,256]{1,0:T(8,128)(2,1)}, bf16[4096,256]{1,0:T(8,128)(2,1)}, u32[]{:S(2)}, u32[]{:S(2)}) collective-permute-start(bf16[4096,256]{1,0:T(8,128)(2,1)} %own_ref.1), channel_id=1, source_target_pairs={{0,1},{1,0},{2,3},{3,2},{4,5},{5,4},{6,7},{7,6},{8,9},{9,8},{10,11... | collective-permute-start | bytes 6291464 | tf_op jit(solution)/shard_map/ppermute | solution.py:226
  1.1 1.7 %shard_map.85 = bf16[8,8,1152]{2,1,0:T(8,128)(2,1)} custom-call(bf16[8,4096]{1,0:T(8,128)(2,1)} %hidden_ref.1, bf16[32,128]{1,0:T(8,128)(2,1)} %bitcast.5, s32[8]{0:T(128)} %targets_ref.1, s32[8]{0:T(128)} %segments_ref.1, s32[8]{0:T(128)} %scored_ref.1), custom_call_target="tpu_custom_call" | custom-call | tf_op jit(solution)/shard_map/pallas_call | solution.py:227
  2.8 7.9 %all-to-all-start = ((bf16[8,8,1152]{2,1,0:T(8,128)(2,1)}), bf16[8,8,1152]{2,1,0:T(8,128)(2,1)S(1)}, u32[]{:S(2)}, u32[]{:S(2)}) async-start(bf16[8,8,1152]{2,1,0:T(8,128)(2,1)} %shard_map.85), calls=%async_computation | async-start | bytes 294912 | tf_op jit(solution)/shard_map/all_to_all | solution.py:238
  10.7 0.0 collective-permute-done.other_ref
  10.7 1.9 %shard_map.86 = (bf16[4096,256]{1,0:T(8,128)(2,1)S(1)}, bf16[2048,256]{1,0:T(8,128)(2,1)S(1)}) custom-call(bf16[4096,256]{1,0:T(8,128)(2,1)} %own_ref.1, bf16[4096,256]{1,0:T(8,128)(2,1)} %collective-permute-done.other_ref), custom_call_target="tpu_custom_call" | custom-call | bytes 6291456 | tf_op jit(solution)/shard_map/pallas_call | solution.py:241
  12.6 2.8 %all-to-all-done.rows_ref = bf16[8,8,1152]{2,1,0:T(8,128)(2,1)S(1)} async-done(((bf16[8,8,1152]{2,1,0:T(8,128)(2,1)}), bf16[8,8,1152]{2,1,0:T(8,128)(2,1)S(1)}, u32[]{:S(2)}, u32[]{:S(2)}) %all-to-all-start) | async-done | bytes 147488 | tf_op jit(solution)/shard_map/all_to_all | solution.py:238
  15.4 2.1 %shard_map.87 = (f32[1,128]{1,0:T(1,128)S(1)}, f32[8,128]{1,0:T(8,128)S(1)}) custom-call(bf16[8,8,1152]{2,1,0:T(8,128)(2,1)S(1)} %all-to-all-done.rows_ref, bf16[4096,256]{1,0:T(8,128)(2,1)S(1)} %get-tuple-element.7.own_ref, bf16[2048,256]{1,0:T(8,128)(2,1)S(1)} %get-tuple-element.8.upper_ref, bf16[4096,256]{1,0:T(8,128)(2,1)} %collective-permute-done.other_ref), custom_call_target="tpu_custom_call" | custom-call | tf_op jit(solution)/shard_map/pallas_call | solution.py:250
  17.5 0.1 collective-permute-start.1
  17.6 1.1 %collective-permute-done.1 = f32[1,128]{1,0:T(1,128)S(1)} collective-permute-done((f32[1,128]{1,0:T(1,128)S(1)}, f32[1,128]{1,0:T(1,128)S(1)}, u32[]{:S(2)}, u32[]{:S(2)}) %collective-permute-start.1) | collective-permute-done | bytes 544 | tf_op jit(solution)/shard_map/ppermute | solution.py:265
  18.7 10.2 %all_to_all.10 = f32[16,1,128]{2,1,0:T(1,128)S(1)} all-to-all(f32[16,1,128]{2,1,0:T(1,128)S(1)} %broadcast_in_dim.9), channel_id=1, replica_groups={{20,22,16,18,12,14,8,10,0,2,4,6,24,26,28,30},{21,23,17,19,13,15,9,11,1,..., dimensions={0} | all-to-all | bytes 16384 | tf_op jit(solution)/shard_map/all_to_all | solution.py:270
  28.9 0.7 %shard_map.88 = (f32[8]{0:T(128)}, f32[8]{0:T(128)}, f32[4]{0:T(128)}) custom-call(f32[16,128]{1,0:T(8,128)S(1)} %bitcast.4, f32[8,128]{1,0:T(8,128)S(1)} %get-tuple-element.10.meta_ref), custom_call_target="tpu_custom_call" | custom-call | tf_op jit(solution)/shard_map/pallas_call | solution.py:271
  (2 shorter events, 0.0 us)
Async XLA Ops:
  0.6 10.1 %collective-permute-start = (bf16[4096,256]{1,0:T(8,128)(2,1)}, bf16[4096,256]{1,0:T(8,128)(2,1)}, u32[]{:S(2)}, u32[]{:S(2)}) collective-permute-start(bf16[4096,256]{1,0:T(8,128)(2,1)} %own_ref.1), channel_id=1, source_target_pairs={{0,1},{1,0},{2,3},{3,2},{4,5},{5,4},{6,7},{7,6},{8,9},{9,8},{10,11... | collective-permute-start | bytes 6291464 | tf_op jit(solution)/shard_map/ppermute | solution.py:226
  2.8 12.6 %all-to-all-start = ((bf16[8,8,1152]{2,1,0:T(8,128)(2,1)}), bf16[8,8,1152]{2,1,0:T(8,128)(2,1)S(1)}, u32[]{:S(2)}, u32[]{:S(2)}) async-start(bf16[8,8,1152]{2,1,0:T(8,128)(2,1)} %shard_map.85), calls=%async_computation | async-start | bytes 294912 | tf_op jit(solution)/shard_map/all_to_all | solution.py:238
  17.5 1.2 %collective-permute-start.1 = (f32[1,128]{1,0:T(1,128)S(1)}, f32[1,128]{1,0:T(1,128)S(1)}, u32[]{:S(2)}, u32[]{:S(2)}) collective-permute-start(f32[1,128]{1,0:T(1,128)S(1)} %get-tuple-element.9), channel_id=1, source_target_pairs={{0,1},{1,0},{2,3},{3,2},{4,5},{5,4},{6,7},{7,6},{8,9},{9,8},{10,11... | collective-permute-start | bytes 1544 | tf_op jit(solution)/shard_map/ppermute | solution.py:265

commit v17 on v15

--- a/solution.py
+++ b/solution.py
@@ -32,14 +32,14 @@
 
 
 def members(count):
-    quarter = count // 4
-    return [*reversed(range(quarter, count - quarter)), *range(quarter), *range(count - quarter, count)]
+    ring = [*range(0, count, 2), *reversed(range(1, count, 2))]
+    return ring[5 * count // 8 :] + ring[: 5 * count // 8]
 
 
 def own_slot(count):
-    own, quarter = lax.axis_index("req"), count // 4
-    middle = count - quarter - 1 - own
-    return jnp.where(own < quarter, own + count - 2 * quarter, jnp.where(own < count - quarter, middle, own))
+    own = lax.axis_index("req")
+    at = jnp.where(own % 2 == 0, own // 2, count - 1 - own // 2) - 5 * count // 8
+    return jnp.where(at < 0, at + count, at)
 
 
 def pack_kernel(share, hidden_ref, gain_ref, targets_ref, segments_ref, scored_ref, out_ref, wide_ref, parts_ref, gains_ref):

time: 29.5 us -> 30.4 us (1.031)
  blocking collectives: 11 us -> 11.5 us
  waiting for transfers between devices: 2.83 us -> 3.23 us
    all_to_all x1, blocking collectives: 11 us -> 11.5 us  [local(): gathered = lax.all_to_all(copies, ('req', 'tp'), 0, 0)]
    all_to_all x1, waiting for transfers between devices: 2.83 us -> 3.23 us  [local(): lax.all_to_all(packed, 'req', 0, 0, axis_index_groups=[members(groups)])]
where the time goes in v17:
time: 30.4 us; the launch traced here: 30.1 us
  blocking collectives  11.5 us (38%)
  starting transfers between devices  8.37 us (28%)
  Pallas kernels  6.34 us (21%)
  waiting for transfers between devices  3.23 us (11%)
  between operations  0.66 us (2%)
    all_to_all x1, blocking collectives, local(): gathered = lax.all_to_all(copies, ('req', 'tp'), 0, 0)  11.5 us
    all_to_all x1, starting transfers between devices, local(): lax.all_to_all(packed, 'req', 0, 0, axis_index_groups=[members(groups)])  7.85 us
    all_to_all x1, waiting for transfers between devices, local(): lax.all_to_all(packed, 'req', 0, 0, axis_index_groups=[members(groups)])  3.23 us
    pallas_call x1, Pallas kernels, local(): pl.pallas_call(score_kernel, out_shape=(jax.ShapeDtypeStruct((1, STATS *...  2.08 us
    pallas_call x1, Pallas kernels, local(): pl.pallas_call(stage_kernel, out_shape=(VMEM(lm_head.shape, lm_head.dtype...  1.89 us
    pallas_call x1, Pallas kernels, local(): pl.pallas_call(functools.partial(pack_kernel, share), out_shape=VMEM((gro...  1.68 us
    pallas_call x1, Pallas kernels, local(): pl.pallas_call(functools.partial(finish_kernel, share), out_shape=(jax.Sh...  0.69 us
  transfers between devices with their start and end apart: 2, of which 1 were waited for; matrix products, arithmetic and copies ran while one was open for 0% of the time, Pallas kernels for 12%

profile of v17, /device:TPU:0, one launch (start us, length us, event | category | flops | bytes accessed | tf_op | source)
XLA Modules:
  0.0 30.1 jit_solution(10914320599222002684)
XLA Ops:
  0.6 0.5 %collective-permute-start = (bf16[4096,256]{1,0:T(8,128)(2,1)}, bf16[4096,256]{1,0:T(8,128)(2,1)}, u32[]{:S(2)}, u32[]{:S(2)}) collective-permute-start(bf16[4096,256]{1,0:T(8,128)(2,1)} %own_ref.1), channel_id=1, source_target_pairs={{0,1},{1,0},{2,3},{3,2},{4,5},{5,4},{6,7},{7,6},{8,9},{9,8},{10,11... | collective-permute-start | bytes 6291464 | tf_op jit(solution)/shard_map/ppermute | solution.py:225
  1.1 1.7 %shard_map.85 = bf16[8,8,1152]{2,1,0:T(8,128)(2,1)} custom-call(bf16[8,4096]{1,0:T(8,128)(2,1)} %hidden_ref.1, bf16[32,128]{1,0:T(8,128)(2,1)} %bitcast.5, s32[8]{0:T(128)} %targets_ref.1, s32[8]{0:T(128)} %segments_ref.1, s32[8]{0:T(128)} %scored_ref.1), custom_call_target="tpu_custom_call" | custom-call | tf_op jit(solution)/shard_map/pallas_call | solution.py:226
  2.8 7.8 %all-to-all-start = ((bf16[8,8,1152]{2,1,0:T(8,128)(2,1)}), bf16[8,8,1152]{2,1,0:T(8,128)(2,1)S(1)}, u32[]{:S(2)}, u32[]{:S(2)}) async-start(bf16[8,8,1152]{2,1,0:T(8,128)(2,1)} %shard_map.85), calls=%async_computation | async-start | bytes 294912 | tf_op jit(solution)/shard_map/all_to_all | solution.py:237
  10.7 0.0 collective-permute-done.other_ref
  10.7 1.9 %shard_map.86 = (bf16[4096,256]{1,0:T(8,128)(2,1)S(1)}, bf16[2048,256]{1,0:T(8,128)(2,1)S(1)}) custom-call(bf16[4096,256]{1,0:T(8,128)(2,1)} %own_ref.1, bf16[4096,256]{1,0:T(8,128)(2,1)} %collective-permute-done.other_ref), custom_call_target="tpu_custom_call" | custom-call | bytes 6291456 | tf_op jit(solution)/shard_map/pallas_call | solution.py:240
  12.6 3.2 %all-to-all-done.rows_ref = bf16[8,8,1152]{2,1,0:T(8,128)(2,1)S(1)} async-done(((bf16[8,8,1152]{2,1,0:T(8,128)(2,1)}), bf16[8,8,1152]{2,1,0:T(8,128)(2,1)S(1)}, u32[]{:S(2)}, u32[]{:S(2)}) %all-to-all-start) | async-done | bytes 147488 | tf_op jit(solution)/shard_map/all_to_all | solution.py:237
  15.8 2.1 %shard_map.87 = (f32[1,128]{1,0:T(1,128)S(1)}, f32[8,128]{1,0:T(8,128)S(1)}) custom-call(bf16[8,8,1152]{2,1,0:T(8,128)(2,1)S(1)} %all-to-all-done.rows_ref, bf16[4096,256]{1,0:T(8,128)(2,1)S(1)} %get-tuple-element.7.own_ref, bf16[2048,256]{1,0:T(8,128)(2,1)S(1)} %get-tuple-element.8.upper_ref, bf16[4096,256]{1,0:T(8,128)(2,1)} %collective-permute-done.other_ref), custom_call_target="tpu_custom_call" | custom-call | tf_op jit(solution)/shard_map/pallas_call | solution.py:249
  17.9 11.5 %all_to_all.10 = f32[32,1,128]{2,1,0:T(1,128)S(1)} all-to-all(f32[32,1,128]{2,1,0:T(1,128)S(1)} %broadcast_in_dim.9), channel_id=1, replica_groups=mesh['req'=8,'tp'=4] {'req','tp'}, dimensions={0} | all-to-all | bytes 32768 | tf_op jit(solution)/shard_map/all_to_all | solution.py:265
  29.4 0.7 %shard_map.88 = (f32[8]{0:T(128)}, f32[8]{0:T(128)}, f32[4]{0:T(128)}) custom-call(f32[32,128]{1,0:T(8,128)S(1)} %bitcast.3, f32[8,128]{1,0:T(8,128)S(1)} %get-tuple-element.10.meta_ref), custom_call_target="tpu_custom_call" | custom-call | tf_op jit(solution)/shard_map/pallas_call | solution.py:267
  (1 shorter events, 0.0 us)
Async XLA Ops:
  0.6 10.0 %collective-permute-start = (bf16[4096,256]{1,0:T(8,128)(2,1)}, bf16[4096,256]{1,0:T(8,128)(2,1)}, u32[]{:S(2)}, u32[]{:S(2)}) collective-permute-start(bf16[4096,256]{1,0:T(8,128)(2,1)} %own_ref.1), channel_id=1, source_target_pairs={{0,1},{1,0},{2,3},{3,2},{4,5},{5,4},{6,7},{7,6},{8,9},{9,8},{10,11... | collective-permute-start | bytes 6291464 | tf_op jit(solution)/shard_map/ppermute | solution.py:225
  2.8 13.0 %all-to-all-start = ((bf16[8,8,1152]{2,1,0:T(8,128)(2,1)}), bf16[8,8,1152]{2,1,0:T(8,128)(2,1)S(1)}, u32[]{:S(2)}, u32[]{:S(2)}) async-start(bf16[8,8,1152]{2,1,0:T(8,128)(2,1)} %shard_map.85), calls=%async_computation | async-start | bytes 294912 | tf_op jit(solution)/shard_map/all_to_all | solution.py:237

commit v18 on v15

--- a/solution.py
+++ b/solution.py
@@ -31,14 +31,15 @@
     return lax.broadcasted_iota(jnp.int32, shape, axis)
 
 
-def members(count):
+def members(count, half):
     quarter = count // 4
-    return [*reversed(range(quarter, count - quarter)), *range(quarter), *range(count - quarter, count)]
-
-
-def own_slot(count):
+    middle = range(quarter, count - quarter)
+    return [*(middle if half else reversed(middle)), *range(quarter), *range(count - quarter, count)]
+
+
+def own_slot(count, half):
     own, quarter = lax.axis_index("req"), count // 4
-    middle = count - quarter - 1 - own
+    middle = jnp.where(half == 1, own - quarter, count - quarter - 1 - own)
     return jnp.where(own < quarter, own + count - 2 * quarter, jnp.where(own < count - quarter, middle, own))
 
 
@@ -46,7 +47,7 @@
     row_count, width = hidden_ref.shape
     parts = SUBS // MINE
     span = width // parts
-    own, half = own_slot(out_ref.shape[0]), lax.axis_index("tp") % PAIR
+    half = lax.axis_index("tp") % PAIR
     wide_ref[...] = hidden_ref[...].astype(jnp.float32)
     gains_ref[...] = gain_ref[...].astype(jnp.float32)
     ranks, count = ranks_of(scored_ref, row_count)
@@ -79,7 +80,9 @@
             out_ref[to, :, at * LANES : (at + 1) * LANES] = piece
     width_side = out_ref.shape[2] - span
     sub, lane = iota((SUBS, width_side), 0), iota((SUBS, width_side), 1)
-    at_row, at_half = lane % share - own * MINE, lane // share
+    count_to, at_half = out_ref.shape[0], lane // share
+    at_mine = lane % share - own_slot(count_to, half) * MINE
+    at_row = lane % share - jnp.where(at_half == 1, own_slot(count_to, 1), own_slot(count_to, 0)) * MINE
     side = jnp.zeros((SUBS, width_side), jnp.int32)
     for i in range(MINE):
         target = targets_ref[mine[i]]
@@ -89,7 +92,8 @@
             r = h * MINE + i
             field = jnp.where(sub == 4, (count > r).astype(jnp.int32), source[r])
             fields = jnp.where(at_half == h, jnp.where(sub == 3, segments_ref[source[r]], field), fields)
-        side = jnp.where(at_row == i, jnp.where(sub < 3, digits, fields), side)
+        side = jnp.where(jnp.logical_and(sub < 3, at_mine == i), digits, side)
+        side = jnp.where(jnp.logical_and(sub >= 3, at_row == i), fields, side)
     side = side.astype(jnp.float32).astype(jnp.bfloat16)
     for to in range(out_ref.shape[0]):
         out_ref[to, :, span:] = side
@@ -196,7 +200,8 @@
     logprob = jnp.where(in_use, picked - log_norm, 0.0)
     entropy = jnp.where(in_use, log_norm - row_weighted / row_total, 0.0)
     segment, place = meta_ref[3:4, :].astype(jnp.int32), meta_ref[5:6, :].astype(jnp.int32)
-    mine = jnp.logical_and(place == sub, lane % share // MINE == own_slot(share // MINE))
+    slot = jnp.where(lane // share == 1, own_slot(share // MINE, 1), own_slot(share // MINE, 0))
+    mine = jnp.logical_and(place == sub, lane % share // MINE == slot)
 
     def placed(values, wanted):
         sums = jnp.sum(jnp.where(wanted, values, 0.0), axis=1, keepdims=True)
@@ -234,7 +239,8 @@
             VMEM((width // LANES, LANES), jnp.float32),
         ],
     )(hidden, norm_gain.reshape(width // LANES, LANES), targets, segments, scored)
-    rows = lax.all_to_all(packed, "req", 0, 0, axis_index_groups=[members(groups)])
+    listed = [[q * tp_count + t for q in members(groups, t % PAIR)] for t in range(tp_count)]
+    rows = lax.all_to_all(packed, ("req", "tp"), 0, 0, axis_index_groups=listed)
     other = pltpu.with_memory_space_constraint(other, pltpu.HBM)
     staged = width // 2
     slices = pl.pallas_call(

time: 29.5 us -> 29.5 us (level)
  waiting for transfers between devices: 2.83 us -> 2.51 us
  blocking collectives: 11 us -> 11.3 us
    all_to_all x1, waiting for transfers between devices: 2.83 us -> 2.51 us  [local(): rows = lax.all_to_all(packed, ('req', 'tp'), 0, 0, axis_index_groups=listed)]
where the time goes in v18:
time: 29.5 us; the launch traced here: 29.2 us
  blocking collectives  11.3 us (38%)
  starting transfers between devices  8.37 us (28%)
  Pallas kernels  6.33 us (21%)
  waiting for transfers between devices  2.51 us (9%)
  between operations  0.66 us (2%)
    all_to_all x1, blocking collectives, local(): gathered = lax.all_to_all(copies, ('req', 'tp'), 0, 0)  11.3 us
    all_to_all x1, starting transfers between devices, local(): rows = lax.all_to_all(packed, ('req', 'tp'), 0, 0, axis_index_groups=listed)  7.86 us
    all_to_all x1, waiting for transfers between devices, local(): rows = lax.all_to_all(packed, ('req', 'tp'), 0, 0, axis_index_groups=listed)  2.51 us
    pallas_call x1, Pallas kernels, local(): pl.pallas_call(score_kernel, out_shape=(jax.ShapeDtypeStruct((1, STATS *...  2.08 us
    pallas_call x1, Pallas kernels, local(): pl.pallas_call(stage_kernel, out_shape=(VMEM(lm_head.shape, lm_head.dtype...  1.89 us
    pallas_call x1, Pallas kernels, local(): pl.pallas_call(functools.partial(pack_kernel, share), out_shape=VMEM((gro...  1.68 us
    pallas_call x1, Pallas kernels, local(): pl.pallas_call(functools.partial(finish_kernel, share), out_shape=(jax.Sh...  0.69 us
  transfers between devices with their start and end apart: 2, of which 1 were waited for; matrix products, arithmetic and copies ran while one was open for 0% of the time, Pallas kernels for 12%

profile of v18, /device:TPU:0, one launch (start us, length us, event | category | flops | bytes accessed | tf_op | source)
XLA Modules:
  0.0 29.2 jit_solution(8293952873537501939)
XLA Ops:
  0.6 0.5 %collective-permute-start = (bf16[4096,256]{1,0:T(8,128)(2,1)}, bf16[4096,256]{1,0:T(8,128)(2,1)}, u32[]{:S(2)}, u32[]{:S(2)}) collective-permute-start(bf16[4096,256]{1,0:T(8,128)(2,1)} %own_ref.1), channel_id=1, source_target_pairs={{0,1},{1,0},{2,3},{3,2},{4,5},{5,4},{6,7},{7,6},{8,9},{9,8},{10,11... | collective-permute-start | bytes 6291464 | tf_op jit(solution)/shard_map/ppermute | solution.py:230
  1.1 1.7 %shard_map.85 = bf16[8,8,1152]{2,1,0:T(8,128)(2,1)} custom-call(bf16[8,4096]{1,0:T(8,128)(2,1)} %hidden_ref.1, bf16[32,128]{1,0:T(8,128)(2,1)} %bitcast.5, s32[8]{0:T(128)} %targets_ref.1, s32[8]{0:T(128)} %segments_ref.1, s32[8]{0:T(128)} %scored_ref.1), custom_call_target="tpu_custom_call" | custom-call | tf_op jit(solution)/shard_map/pallas_call | solution.py:231
  2.8 7.9 %all-to-all-start = ((bf16[8,8,1152]{2,1,0:T(8,128)(2,1)}), bf16[8,8,1152]{2,1,0:T(8,128)(2,1)S(1)}, u32[]{:S(2)}, u32[]{:S(2)}) async-start(bf16[8,8,1152]{2,1,0:T(8,128)(2,1)} %shard_map.85), calls=%async_computation | async-start | bytes 294912 | tf_op jit(solution)/shard_map/all_to_all | solution.py:243
  10.7 0.0 collective-permute-done.other_ref
  10.7 1.9 %shard_map.86 = (bf16[4096,256]{1,0:T(8,128)(2,1)S(1)}, bf16[2048,256]{1,0:T(8,128)(2,1)S(1)}) custom-call(bf16[4096,256]{1,0:T(8,128)(2,1)} %own_ref.1, bf16[4096,256]{1,0:T(8,128)(2,1)} %collective-permute-done.other_ref), custom_call_target="tpu_custom_call" | custom-call | bytes 6291456 | tf_op jit(solution)/shard_map/pallas_call | solution.py:246
  12.6 2.5 %all-to-all-done.rows_ref = bf16[8,8,1152]{2,1,0:T(8,128)(2,1)S(1)} async-done(((bf16[8,8,1152]{2,1,0:T(8,128)(2,1)}), bf16[8,8,1152]{2,1,0:T(8,128)(2,1)S(1)}, u32[]{:S(2)}, u32[]{:S(2)}) %all-to-all-start) | async-done | bytes 147488 | tf_op jit(solution)/shard_map/all_to_all | solution.py:243
  15.1 2.1 %shard_map.87 = (f32[1,128]{1,0:T(1,128)S(1)}, f32[8,128]{1,0:T(8,128)S(1)}) custom-call(bf16[8,8,1152]{2,1,0:T(8,128)(2,1)S(1)} %all-to-all-done.rows_ref, bf16[4096,256]{1,0:T(8,128)(2,1)S(1)} %get-tuple-element.7.own_ref, bf16[2048,256]{1,0:T(8,128)(2,1)S(1)} %get-tuple-element.8.upper_ref, bf16[4096,256]{1,0:T(8,128)(2,1)} %collective-permute-done.other_ref), custom_call_target="tpu_custom_call" | custom-call | tf_op jit(solution)/shard_map/pallas_call | solution.py:255
  17.2 11.3 %all_to_all.10 = f32[32,1,128]{2,1,0:T(1,128)S(1)} all-to-all(f32[32,1,128]{2,1,0:T(1,128)S(1)} %broadcast_in_dim.9), channel_id=1, replica_groups=mesh['req'=8,'tp'=4] {'req','tp'}, dimensions={0} | all-to-all | bytes 32768 | tf_op jit(solution)/shard_map/all_to_all | solution.py:271
  28.5 0.7 %shard_map.88 = (f32[8]{0:T(128)}, f32[8]{0:T(128)}, f32[4]{0:T(128)}) custom-call(f32[32,128]{1,0:T(8,128)S(1)} %bitcast.3, f32[8,128]{1,0:T(8,128)S(1)} %get-tuple-element.10.meta_ref), custom_call_target="tpu_custom_call" | custom-call | tf_op jit(solution)/shard_map/pallas_call | solution.py:273
  (1 shorter events, 0.0 us)
Async XLA Ops:
  0.6 10.1 %collective-permute-start = (bf16[4096,256]{1,0:T(8,128)(2,1)}, bf16[4096,256]{1,0:T(8,128)(2,1)}, u32[]{:S(2)}, u32[]{:S(2)}) collective-permute-start(bf16[4096,256]{1,0:T(8,128)(2,1)} %own_ref.1), channel_id=1, source_target_pairs={{0,1},{1,0},{2,3},{3,2},{4,5},{5,4},{6,7},{7,6},{8,9},{9,8},{10,11... | collective-permute-start | bytes 6291464 | tf_op jit(solution)/shard_map/ppermute | solution.py:230
  2.8 12.3 %all-to-all-start = ((bf16[8,8,1152]{2,1,0:T(8,128)(2,1)}), bf16[8,8,1152]{2,1,0:T(8,128)(2,1)S(1)}, u32[]{:S(2)}, u32[]{:S(2)}) async-start(bf16[8,8,1152]{2,1,0:T(8,128)(2,1)} %shard_map.85), calls=%async_computation | async-start | bytes 294912 | tf_op jit(solution)/shard_map/all_to_all | solution.py:243

commit v19 on v15

--- a/solution.py
+++ b/solution.py
@@ -42,11 +42,29 @@
     return jnp.where(own < quarter, own + count - 2 * quarter, jnp.where(own < count - quarter, middle, own))
 
 
-def pack_kernel(share, hidden_ref, gain_ref, targets_ref, segments_ref, scored_ref, out_ref, wide_ref, parts_ref, gains_ref):
+def pack_kernel(share, hidden_hbm, gain_hbm, targets_hbm, segments_hbm, scored_hbm, out_ref, *scratch):
+    hidden_ref, gain_ref, targets_ref, segments_ref, scored_ref, wide_ref, parts_ref, gains_ref, block_ref = scratch[:9]
+    in_sems, out_sems = scratch[9:]
+    reads = [
+        pltpu.make_async_copy(source, to, in_sems.at[at])
+        for at, (source, to) in enumerate(
+            (
+                (scored_hbm, scored_ref),
+                (targets_hbm, targets_ref),
+                (segments_hbm, segments_ref),
+                (hidden_hbm, hidden_ref),
+                (gain_hbm, gain_ref),
+            )
+        )
+    ]
+    for read in reads:
+        read.start()
     row_count, width = hidden_ref.shape
     parts = SUBS // MINE
     span = width // parts
     own, half = own_slot(out_ref.shape[0]), lax.axis_index("tp") % PAIR
+    for read in reads:
+        read.wait()
     wide_ref[...] = hidden_ref[...].astype(jnp.float32)
     gains_ref[...] = gain_ref[...].astype(jnp.float32)
     ranks, count = ranks_of(scored_ref, row_count)
@@ -74,9 +92,7 @@
         for k in range(1, parts):
             gain = jnp.where(sub >= k * MINE, gains_ref[k * chunks + at : k * chunks + at + 1, :], gain)
         piece = parts_ref[:, at * LANES : (at + 1) * LANES]
-        piece = (piece * row_scale * gain).astype(jnp.bfloat16)
-        for to in range(out_ref.shape[0]):
-            out_ref[to, :, at * LANES : (at + 1) * LANES] = piece
+        block_ref[:, at * LANES : (at + 1) * LANES] = (piece * row_scale * gain).astype(jnp.bfloat16)
     width_side = out_ref.shape[2] - span
     sub, lane = iota((SUBS, width_side), 0), iota((SUBS, width_side), 1)
     at_row, at_half = lane % share - own * MINE, lane // share
@@ -90,12 +106,15 @@
             field = jnp.where(sub == 4, (count > r).astype(jnp.int32), source[r])
             fields = jnp.where(at_half == h, jnp.where(sub == 3, segments_ref[source[r]], field), fields)
         side = jnp.where(at_row == i, jnp.where(sub < 3, digits, fields), side)
-    side = side.astype(jnp.float32).astype(jnp.bfloat16)
-    for to in range(out_ref.shape[0]):
-        out_ref[to, :, span:] = side
-
-
-def stage_kernel(own_ref, other_ref, own_out, other_out, sems):
+    block_ref[:, span:] = side.astype(jnp.float32).astype(jnp.bfloat16)
+    writes = [pltpu.make_async_copy(block_ref, out_ref.at[to], out_sems.at[to]) for to in range(out_ref.shape[0])]
+    for write in writes:
+        write.start()
+    for write in writes:
+        write.wait()
+
+
+def stage_kernel(share, own_ref, other_ref, own_out, other_out, order_out, sems):
     copies = []
     for at, (source, out) in enumerate(((own_ref, own_out), (other_ref, other_out))):
         depth = out.shape[0] // sems.shape[1]
@@ -104,11 +123,14 @@
             copies.append(pltpu.make_async_copy(source.at[piece], out.at[piece], sems.at[at, i]))
     for copy in copies:
         copy.start()
+    into, out_of = iota(order_out.shape, 0), iota(order_out.shape, 1)
+    wanted = into % share // MINE * SUBS + into // share * MINE + into % MINE
+    order_out[...] = jnp.where(out_of == wanted, 1.0, 0.0).astype(jnp.bfloat16)
     for copy in copies:
         copy.wait()
 
 
-def score_kernel(rows_ref, own_ref, upper_ref, other_ref, stats_ref, meta_ref, ordered_ref, lower_ref, sems):
+def score_kernel(rows_ref, own_ref, upper_ref, order_ref, other_ref, stats_ref, meta_ref, ordered_ref, lower_ref, sems):
     width, cols = own_ref.shape
     staged = upper_ref.shape[0]
     depth = lower_ref.shape[0] // sems.shape[0]
@@ -128,11 +150,8 @@
     half = tp % PAIR
     place = lax.axis_index("req") * tp_count + tp
     count = groups * SUBS
-    into, out_of = iota((count, count), 0), iota((count, count), 1)
-    wanted = into % share // MINE * SUBS + into // share * MINE + into % MINE
-    order = jnp.where(out_of == wanted, 1.0, 0.0).astype(jnp.bfloat16)
     rows = rows_ref[:, :, :span].reshape(count, span)
-    ordered = jnp.dot(order, rows, preferred_element_type=jnp.float32).astype(jnp.bfloat16)
+    ordered = jnp.dot(order_ref[...], rows, preferred_element_type=jnp.float32).astype(jnp.bfloat16)
     for k in range(parts):
         ordered_ref[:, k * span : (k + 1) * span] = ordered[k * share : (k + 1) * share]
     meta = rows_ref[0, :, span:].astype(jnp.float32)
@@ -225,23 +244,33 @@
     other = lax.ppermute(lm_head, "tp", [(i, i + 1 - 2 * (i % PAIR)) for i in range(tp_count)])
     packed = pl.pallas_call(
         functools.partial(pack_kernel, share),
-        out_shape=VMEM((groups, SUBS, span + lanes), jnp.bfloat16),
-        in_specs=[spec(VMEM)] * 2 + [spec(SMEM)] * 3,
-        out_specs=spec(VMEM),
+        out_shape=jax.ShapeDtypeStruct((groups, SUBS, span + lanes), jnp.bfloat16),
+        in_specs=[spec(pltpu.HBM)] * 5,
+        out_specs=spec(pltpu.HBM),
         scratch_shapes=[
+            VMEM((row_count, width), jnp.bfloat16),
+            VMEM((width // LANES, LANES), jnp.bfloat16),
+            *[SMEM((row_count,), jnp.int32)] * 3,
             VMEM((row_count, width), jnp.float32),
             VMEM((SUBS, span), jnp.float32),
             VMEM((width // LANES, LANES), jnp.float32),
+            VMEM((SUBS, span + lanes), jnp.bfloat16),
+            pltpu.SemaphoreType.DMA((5,)),
+            pltpu.SemaphoreType.DMA((groups,)),
         ],
     )(hidden, norm_gain.reshape(width // LANES, LANES), targets, segments, scored)
     rows = lax.all_to_all(packed, "req", 0, 0, axis_index_groups=[members(groups)])
     other = pltpu.with_memory_space_constraint(other, pltpu.HBM)
-    staged = width // 2
+    staged = width * 9 // 16
     slices = pl.pallas_call(
-        stage_kernel,
-        out_shape=(VMEM(lm_head.shape, lm_head.dtype), VMEM((staged, lm_head.shape[1]), lm_head.dtype)),
+        functools.partial(stage_kernel, share),
+        out_shape=(
+            VMEM(lm_head.shape, lm_head.dtype),
+            VMEM((staged, lm_head.shape[1]), lm_head.dtype),
+            VMEM((groups * SUBS, groups * SUBS), jnp.bfloat16),
+        ),
         in_specs=[spec(pltpu.HBM)] * 2,
-        out_specs=(spec(VMEM),) * 2,
+        out_specs=(spec(VMEM),) * 3,
         scratch_shapes=[pltpu.SemaphoreType.DMA((2, 4))],
         compiler_params=grant(4),
         cost_estimate=pl.CostEstimate(flops=0, bytes_accessed=3 * 2 * lm_head.size, transcendentals=0),
@@ -252,7 +281,7 @@
             jax.ShapeDtypeStruct((1, STATS * PAIR * share), jnp.float32),
             VMEM((SUBS, lanes), jnp.float32),
         ),
-        in_specs=[spec(VMEM)] * 3 + [spec(pltpu.HBM)],
+        in_specs=[spec(VMEM)] * 4 + [spec(pltpu.HBM)],
         out_specs=(spec(VMEM), spec(VMEM)),
         scratch_shapes=[
             VMEM((share, width), jnp.bfloat16),

time: 29.5 us -> 29.7 us (level)
  transfers between devices with their start and end apart: 2 -> 2, of which waited for: 1 -> 1; matrix products, arithmetic and copies ran while one was open for 0% -> 0% of each run, Pallas kernels for 12% -> 13%
where the time goes in v19:
time: 29.7 us; the launch traced here: 29.4 us
  blocking collectives  11 us (37%)
  starting transfers between devices  8.39 us (28%)
  Pallas kernels  6.54 us (22%)
  waiting for transfers between devices  2.79 us (9%)
  between operations  0.67 us (2%)
    all_to_all x1, blocking collectives, local(): gathered = lax.all_to_all(copies, ('req', 'tp'), 0, 0)  11 us
    all_to_all x1, starting transfers between devices, local(): lax.all_to_all(packed, 'req', 0, 0, axis_index_groups=[members(groups)])  7.87 us
    all_to_all x1, waiting for transfers between devices, local(): lax.all_to_all(packed, 'req', 0, 0, axis_index_groups=[members(groups)])  2.78 us
    pallas_call x1, Pallas kernels, local(): pl.pallas_call(score_kernel, out_shape=(jax.ShapeDtypeStruct((1, STATS *...  2.16 us
    pallas_call x1, Pallas kernels, local(): pl.pallas_call(functools.partial(stage_kernel, share), out_shape=(VMEM(lm...  1.93 us
    pallas_call x1, Pallas kernels, local(): pl.pallas_call(functools.partial(pack_kernel, share), out_shape=jax.Shape...  1.76 us
    pallas_call x1, Pallas kernels, local(): pl.pallas_call(functools.partial(finish_kernel, share), out_shape=(jax.Sh...  0.69 us
  transfers between devices with their start and end apart: 2, of which 1 were waited for; matrix products, arithmetic and copies ran while one was open for 0% of the time, Pallas kernels for 13%

profile of v19, /device:TPU:0, one launch (start us, length us, event | category | flops | bytes accessed | tf_op | source)
XLA Modules:
  0.0 29.4 jit_solution(1193825897868507046)
XLA Ops:
  0.6 0.5 %collective-permute-start = (bf16[4096,256]{1,0:T(8,128)(2,1)}, bf16[4096,256]{1,0:T(8,128)(2,1)}, u32[]{:S(2)}, u32[]{:S(2)}) collective-permute-start(bf16[4096,256]{1,0:T(8,128)(2,1)} %own_ref.1), channel_id=1, source_target_pairs={{0,1},{1,0},{2,3},{3,2},{4,5},{5,4},{6,7},{7,6},{8,9},{9,8},{10,11... | collective-permute-start | bytes 6291464 | tf_op jit(solution)/shard_map/ppermute | solution.py:244
  1.1 1.8 %shard_map.85 = bf16[8,8,1152]{2,1,0:T(8,128)(2,1)} custom-call(bf16[8,4096]{1,0:T(8,128)(2,1)} %hidden_hbm.1, bf16[32,128]{1,0:T(8,128)(2,1)} %bitcast.5, s32[8]{0:T(128)} %targets_hbm.1, s32[8]{0:T(128)} %segments_hbm.1, s32[8]{0:T(128)} %scored_hbm.1), custom_call_target="tpu_custom_call" | custom-call | tf_op jit(solution)/shard_map/pallas_call | solution.py:245
  2.9 7.9 %all-to-all-start = ((bf16[8,8,1152]{2,1,0:T(8,128)(2,1)}), bf16[8,8,1152]{2,1,0:T(8,128)(2,1)S(1)}, u32[]{:S(2)}, u32[]{:S(2)}) async-start(bf16[8,8,1152]{2,1,0:T(8,128)(2,1)} %shard_map.85), calls=%async_computation | async-start | bytes 294912 | tf_op jit(solution)/shard_map/all_to_all | solution.py:262
  10.8 0.0 collective-permute-done.other_ref
  10.8 1.9 %shard_map.86 = (bf16[4096,256]{1,0:T(8,128)(2,1)S(1)}, bf16[2304,256]{1,0:T(8,128)(2,1)S(1)}, bf16[64,64]{1,0:T(8,128)(2,1)S(1)}) custom-call(bf16[4096,256]{1,0:T(8,128)(2,1)} %own_ref.1, bf16[4096,256]{1,0:T(8,128)(2,1)} %collective-permute-done.other_ref), custom_call_target="tpu_custom_call" | custom-call | bytes 6291456 | tf_op jit(solution)/shard_map/pallas_call | solution.py:265
  12.7 2.8 %all-to-all-done.rows_ref = bf16[8,8,1152]{2,1,0:T(8,128)(2,1)S(1)} async-done(((bf16[8,8,1152]{2,1,0:T(8,128)(2,1)}), bf16[8,8,1152]{2,1,0:T(8,128)(2,1)S(1)}, u32[]{:S(2)}, u32[]{:S(2)}) %all-to-all-start) | async-done | bytes 147488 | tf_op jit(solution)/shard_map/all_to_all | solution.py:262
  15.5 2.2 %shard_map.87 = (f32[1,128]{1,0:T(1,128)S(1)}, f32[8,128]{1,0:T(8,128)S(1)}) custom-call(bf16[8,8,1152]{2,1,0:T(8,128)(2,1)S(1)} %all-to-all-done.rows_ref, bf16[4096,256]{1,0:T(8,128)(2,1)S(1)} %get-tuple-element.8.own_ref, bf16[2304,256]{1,0:T(8,128)(2,1)S(1)} %get-tuple-element.9.upper_ref, bf16[64,64]{1,0:T(8,128)(2,1)S(1)} %get-tuple-element.10.order_ref, ...), custom_call_target="tpu_custom_call" | custom-call | tf_op jit(solution)/shard_map/pallas_call | solution.py:278
  17.7 11.0 %all_to_all.10 = f32[32,1,128]{2,1,0:T(1,128)S(1)} all-to-all(f32[32,1,128]{2,1,0:T(1,128)S(1)} %broadcast_in_dim.9), channel_id=1, replica_groups=mesh['req'=8,'tp'=4] {'req','tp'}, dimensions={0} | all-to-all | bytes 32768 | tf_op jit(solution)/shard_map/all_to_all | solution.py:294
  28.7 0.7 %shard_map.88 = (f32[8]{0:T(128)}, f32[8]{0:T(128)}, f32[4]{0:T(128)}) custom-call(f32[32,128]{1,0:T(8,128)S(1)} %bitcast.3, f32[8,128]{1,0:T(8,128)S(1)} %get-tuple-element.12.meta_ref), custom_call_target="tpu_custom_call" | custom-call | tf_op jit(solution)/shard_map/pallas_call | solution.py:296
  (1 shorter events, 0.0 us)
Async XLA Ops:
  0.6 10.2 %collective-permute-start = (bf16[4096,256]{1,0:T(8,128)(2,1)}, bf16[4096,256]{1,0:T(8,128)(2,1)}, u32[]{:S(2)}, u32[]{:S(2)}) collective-permute-start(bf16[4096,256]{1,0:T(8,128)(2,1)} %own_ref.1), channel_id=1, source_target_pairs={{0,1},{1,0},{2,3},{3,2},{4,5},{5,4},{6,7},{7,6},{8,9},{9,8},{10,11... | collective-permute-start | bytes 6291464 | tf_op jit(solution)/shard_map/ppermute | solution.py:244
  2.9 12.6 %all-to-all-start = ((bf16[8,8,1152]{2,1,0:T(8,128)(2,1)}), bf16[8,8,1152]{2,1,0:T(8,128)(2,1)S(1)}, u32[]{:S(2)}, u32[]{:S(2)}) async-start(bf16[8,8,1152]{2,1,0:T(8,128)(2,1)} %shard_map.85), calls=%async_computation | async-start | bytes 294912 | tf_op jit(solution)/shard_map/all_to_all | solution.py:262

commit v20 on v15

--- a/solution.py
+++ b/solution.py
@@ -139,12 +139,27 @@
     for q in range(1, groups):
         meta = meta + rows_ref[q, :, span:].astype(jnp.float32)
     meta_ref[...] = meta
-    own_logits = jnp.dot(ordered_ref[...], own_ref[...], preferred_element_type=jnp.float32)
-    other_logits = jnp.dot(ordered_ref[:, :staged], upper_ref[...], preferred_element_type=jnp.float32)
+    chunk = min(1024, width - staged)
+
+    def product(slice_ref, first):
+        def step(i, sums):
+            at = pl.multiple_of(first + i * chunk, chunk)
+            rows = ordered_ref[:, pl.ds(at, chunk)]
+            own = own_ref[pl.ds(at, chunk), :]
+            other = slice_ref[pl.ds(pl.multiple_of(i * chunk, chunk), chunk), :]
+            return (
+                sums[0] + jnp.dot(rows, own, preferred_element_type=jnp.float32),
+                sums[1] + jnp.dot(rows, other, preferred_element_type=jnp.float32),
+            )
+
+        return step
+
+    zeros = jnp.zeros((share, cols), jnp.float32)
+    sums = lax.fori_loop(0, staged // chunk, product(upper_ref, 0), (zeros, zeros))
     for copy in copies:
         copy.wait()
-    other_logits += jnp.dot(ordered_ref[:, staged:], lower_ref[...], preferred_element_type=jnp.float32)
-    logits = jnp.concatenate([own_logits, other_logits], axis=1)
+    sums = lax.fori_loop(0, (width - staged) // chunk, product(lower_ref, staged), sums)
+    logits = jnp.concatenate(sums, axis=1)
     lanes = max(share, LANES)
     sub, lane = iota((share, lanes), 0), iota((share, lanes), 1)
     ids = meta[0:1, :lanes] + 256.0 * meta[1:2, :lanes] + 65536.0 * meta[2:3, :lanes]

time: 29.5 us -> 29.3 us (level)
  no operation moved by 1% of the time
where the time goes in v20:
time: 29.3 us; the launch traced here: 29 us
  blocking collectives  11 us (38%)
  starting transfers between devices  8.37 us (29%)
  Pallas kernels  6.17 us (21%)
  waiting for transfers between devices  2.83 us (10%)
  between operations  0.66 us (2%)
    all_to_all x1, blocking collectives, local(): gathered = lax.all_to_all(copies, ('req', 'tp'), 0, 0)  11 us
    all_to_all x1, starting transfers between devices, local(): lax.all_to_all(packed, 'req', 0, 0, axis_index_groups=[members(groups)])  7.86 us
    all_to_all x1, waiting for transfers between devices, local(): lax.all_to_all(packed, 'req', 0, 0, axis_index_groups=[members(groups)])  2.83 us
    pallas_call x1, Pallas kernels, local(): pl.pallas_call(score_kernel, out_shape=(jax.ShapeDtypeStruct((1, STATS *...  1.92 us
    pallas_call x1, Pallas kernels, local(): pl.pallas_call(stage_kernel, out_shape=(VMEM(lm_head.shape, lm_head.dtype...  1.89 us
    pallas_call x1, Pallas kernels, local(): pl.pallas_call(functools.partial(pack_kernel, share), out_shape=VMEM((gro...  1.68 us
    pallas_call x1, Pallas kernels, local(): pl.pallas_call(functools.partial(finish_kernel, share), out_shape=(jax.Sh...  0.69 us
  transfers between devices with their start and end apart: 2, of which 1 were waited for; matrix products, arithmetic and copies ran while one was open for 0% of the time, Pallas kernels for 12%

profile of v20, /device:TPU:0, one launch (start us, length us, event | category | flops | bytes accessed | tf_op | source)
XLA Modules:
  0.0 29.0 jit_solution(3583802801082528160)
XLA Ops:
  0.6 0.5 %collective-permute-start = (bf16[4096,256]{1,0:T(8,128)(2,1)}, bf16[4096,256]{1,0:T(8,128)(2,1)}, u32[]{:S(2)}, u32[]{:S(2)}) collective-permute-start(bf16[4096,256]{1,0:T(8,128)(2,1)} %own_ref.1), channel_id=1, source_target_pairs={{0,1},{1,0},{2,3},{3,2},{4,5},{5,4},{6,7},{7,6},{8,9},{9,8},{10,11... | collective-permute-start | bytes 6291464 | tf_op jit(solution)/shard_map/ppermute | solution.py:240
  1.1 1.7 %shard_map.85 = bf16[8,8,1152]{2,1,0:T(8,128)(2,1)} custom-call(bf16[8,4096]{1,0:T(8,128)(2,1)} %hidden_ref.1, bf16[32,128]{1,0:T(8,128)(2,1)} %bitcast.5, s32[8]{0:T(128)} %targets_ref.1, s32[8]{0:T(128)} %segments_ref.1, s32[8]{0:T(128)} %scored_ref.1), custom_call_target="tpu_custom_call" | custom-call | tf_op jit(solution)/shard_map/pallas_call | solution.py:241
  2.8 7.9 %all-to-all-start = ((bf16[8,8,1152]{2,1,0:T(8,128)(2,1)}), bf16[8,8,1152]{2,1,0:T(8,128)(2,1)S(1)}, u32[]{:S(2)}, u32[]{:S(2)}) async-start(bf16[8,8,1152]{2,1,0:T(8,128)(2,1)} %shard_map.85), calls=%async_computation | async-start | bytes 294912 | tf_op jit(solution)/shard_map/all_to_all | solution.py:252
  10.7 0.0 collective-permute-done.other_ref
  10.7 1.9 %shard_map.86 = (bf16[4096,256]{1,0:T(8,128)(2,1)S(1)}, bf16[2048,256]{1,0:T(8,128)(2,1)S(1)}) custom-call(bf16[4096,256]{1,0:T(8,128)(2,1)} %own_ref.1, bf16[4096,256]{1,0:T(8,128)(2,1)} %collective-permute-done.other_ref), custom_call_target="tpu_custom_call" | custom-call | bytes 6291456 | tf_op jit(solution)/shard_map/pallas_call | solution.py:255
  12.6 2.8 %all-to-all-done.rows_ref = bf16[8,8,1152]{2,1,0:T(8,128)(2,1)S(1)} async-done(((bf16[8,8,1152]{2,1,0:T(8,128)(2,1)}), bf16[8,8,1152]{2,1,0:T(8,128)(2,1)S(1)}, u32[]{:S(2)}, u32[]{:S(2)}) %all-to-all-start) | async-done | bytes 147488 | tf_op jit(solution)/shard_map/all_to_all | solution.py:252
  15.4 1.9 %shard_map.87 = (f32[1,128]{1,0:T(1,128)S(1)}, f32[8,128]{1,0:T(8,128)S(1)}) custom-call(bf16[8,8,1152]{2,1,0:T(8,128)(2,1)S(1)} %all-to-all-done.rows_ref, bf16[4096,256]{1,0:T(8,128)(2,1)S(1)} %get-tuple-element.7.own_ref, bf16[2048,256]{1,0:T(8,128)(2,1)S(1)} %get-tuple-element.8.upper_ref, bf16[4096,256]{1,0:T(8,128)(2,1)} %collective-permute-done.other_ref), custom_call_target="tpu_custom_call" | custom-call | tf_op jit(solution)/shard_map/pallas_call | solution.py:264
  17.4 11.0 %all_to_all.10 = f32[32,1,128]{2,1,0:T(1,128)S(1)} all-to-all(f32[32,1,128]{2,1,0:T(1,128)S(1)} %broadcast_in_dim.9), channel_id=1, replica_groups=mesh['req'=8,'tp'=4] {'req','tp'}, dimensions={0} | all-to-all | bytes 32768 | tf_op jit(solution)/shard_map/all_to_all | solution.py:280
  28.3 0.7 %shard_map.88 = (f32[8]{0:T(128)}, f32[8]{0:T(128)}, f32[4]{0:T(128)}) custom-call(f32[32,128]{1,0:T(8,128)S(1)} %bitcast.3, f32[8,128]{1,0:T(8,128)S(1)} %get-tuple-element.10.meta_ref), custom_call_target="tpu_custom_call" | custom-call | tf_op jit(solution)/shard_map/pallas_call | solution.py:282
  (1 shorter events, 0.0 us)
Async XLA Ops:
  0.6 10.1 %collective-permute-start = (bf16[4096,256]{1,0:T(8,128)(2,1)}, bf16[4096,256]{1,0:T(8,128)(2,1)}, u32[]{:S(2)}, u32[]{:S(2)}) collective-permute-start(bf16[4096,256]{1,0:T(8,128)(2,1)} %own_ref.1), channel_id=1, source_target_pairs={{0,1},{1,0},{2,3},{3,2},{4,5},{5,4},{6,7},{7,6},{8,9},{9,8},{10,11... | collective-permute-start | bytes 6291464 | tf_op jit(solution)/shard_map/ppermute | solution.py:240
  2.8 12.6 %all-to-all-start = ((bf16[8,8,1152]{2,1,0:T(8,128)(2,1)}), bf16[8,8,1152]{2,1,0:T(8,128)(2,1)S(1)}, u32[]{:S(2)}, u32[]{:S(2)}) async-start(bf16[8,8,1152]{2,1,0:T(8,128)(2,1)} %shard_map.85), calls=%async_computation | async-start | bytes 294912 | tf_op jit(solution)/shard_map/all_to_all | solution.py:252

commit v21 on v15

--- a/solution.py
+++ b/solution.py
@@ -95,7 +95,7 @@
         out_ref[to, :, span:] = side
 
 
-def stage_kernel(own_ref, other_ref, own_out, other_out, sems):
+def stage_kernel(share, own_ref, other_ref, own_out, other_out, order_out, sems):
     copies = []
     for at, (source, out) in enumerate(((own_ref, own_out), (other_ref, other_out))):
         depth = out.shape[0] // sems.shape[1]
@@ -104,22 +104,23 @@
             copies.append(pltpu.make_async_copy(source.at[piece], out.at[piece], sems.at[at, i]))
     for copy in copies:
         copy.start()
+    into, out_of = iota(order_out.shape, 0), iota(order_out.shape, 1)
+    wanted = into % share // MINE * SUBS + into // share * MINE + into % MINE
+    order_out[...] = jnp.where(out_of == wanted, 1.0, 0.0).astype(jnp.bfloat16)
     for copy in copies:
         copy.wait()
 
 
-def score_kernel(rows_ref, own_ref, upper_ref, other_ref, stats_ref, meta_ref, ordered_ref, lower_ref, sems):
+def score_kernel(rows_ref, own_ref, upper_ref, order_ref, other_ref, stats_ref, meta_ref, ordered_ref, whole_ref, sems):
     width, cols = own_ref.shape
-    staged = upper_ref.shape[0]
-    depth = lower_ref.shape[0] // sems.shape[0]
-    copies = [
-        pltpu.make_async_copy(
-            other_ref.at[pl.ds(staged + i * depth, depth)], lower_ref.at[pl.ds(i * depth, depth)], sems.at[i]
-        )
-        for i in range(sems.shape[0])
-    ]
-    for copy in copies:
-        copy.start()
+    staged, chunk = upper_ref.shape[0], width // sems.shape[0]
+
+    def fetch(source, at):
+        piece = pl.ds(at * chunk, chunk)
+        return pltpu.make_async_copy(source.at[piece], whole_ref.at[piece], sems.at[at])
+
+    for at in range(sems.shape[0]):
+        fetch(upper_ref if at * chunk < staged else other_ref, at).start()
     groups = rows_ref.shape[0]
     parts = SUBS // MINE
     span = width // parts
@@ -128,23 +129,24 @@
     half = tp % PAIR
     place = lax.axis_index("req") * tp_count + tp
     count = groups * SUBS
-    into, out_of = iota((count, count), 0), iota((count, count), 1)
-    wanted = into % share // MINE * SUBS + into // share * MINE + into % MINE
-    order = jnp.where(out_of == wanted, 1.0, 0.0).astype(jnp.bfloat16)
     rows = rows_ref[:, :, :span].reshape(count, span)
-    ordered = jnp.dot(order, rows, preferred_element_type=jnp.float32).astype(jnp.bfloat16)
+    ordered = jnp.dot(order_ref[...], rows, preferred_element_type=jnp.float32).astype(jnp.bfloat16)
     for k in range(parts):
         ordered_ref[:, k * span : (k + 1) * span] = ordered[k * share : (k + 1) * share]
     meta = rows_ref[0, :, span:].astype(jnp.float32)
     for q in range(1, groups):
         meta = meta + rows_ref[q, :, span:].astype(jnp.float32)
     meta_ref[...] = meta
-    own_logits = jnp.dot(ordered_ref[...], own_ref[...], preferred_element_type=jnp.float32)
-    other_logits = jnp.dot(ordered_ref[:, :staged], upper_ref[...], preferred_element_type=jnp.float32)
-    for copy in copies:
-        copy.wait()
-    other_logits += jnp.dot(ordered_ref[:, staged:], lower_ref[...], preferred_element_type=jnp.float32)
-    logits = jnp.concatenate([own_logits, other_logits], axis=1)
+
+    def step(at, sums):
+        piece = pl.ds(pl.multiple_of(at * chunk, chunk), chunk)
+        rows = ordered_ref[:, piece]
+        own = sums[0] + jnp.dot(rows, own_ref[piece, :], preferred_element_type=jnp.float32)
+        fetch(other_ref, at).wait()
+        return own, sums[1] + jnp.dot(rows, whole_ref[piece, :], preferred_element_type=jnp.float32)
+
+    zeros = jnp.zeros((share, cols), jnp.float32)
+    logits = jnp.concatenate(lax.fori_loop(0, width // chunk, step, (zeros, zeros)), axis=1)
     lanes = max(share, LANES)
     sub, lane = iota((share, lanes), 0), iota((share, lanes), 1)
     ids = meta[0:1, :lanes] + 256.0 * meta[1:2, :lanes] + 65536.0 * meta[2:3, :lanes]
@@ -238,10 +240,14 @@
     other = pltpu.with_memory_space_constraint(other, pltpu.HBM)
     staged = width // 2
     slices = pl.pallas_call(
-        stage_kernel,
-        out_shape=(VMEM(lm_head.shape, lm_head.dtype), VMEM((staged, lm_head.shape[1]), lm_head.dtype)),
+        functools.partial(stage_kernel, share),
+        out_shape=(
+            VMEM(lm_head.shape, lm_head.dtype),
+            VMEM((staged, lm_head.shape[1]), lm_head.dtype),
+            VMEM((groups * SUBS, groups * SUBS), jnp.bfloat16),
+        ),
         in_specs=[spec(pltpu.HBM)] * 2,
-        out_specs=(spec(VMEM),) * 2,
+        out_specs=(spec(VMEM),) * 3,
         scratch_shapes=[pltpu.SemaphoreType.DMA((2, 4))],
         compiler_params=grant(4),
         cost_estimate=pl.CostEstimate(flops=0, bytes_accessed=3 * 2 * lm_head.size, transcendentals=0),
@@ -252,11 +258,11 @@
             jax.ShapeDtypeStruct((1, STATS * PAIR * share), jnp.float32),
             VMEM((SUBS, lanes), jnp.float32),
         ),
-        in_specs=[spec(VMEM)] * 3 + [spec(pltpu.HBM)],
+        in_specs=[spec(VMEM)] * 4 + [spec(pltpu.HBM)],
         out_specs=(spec(VMEM), spec(VMEM)),
         scratch_shapes=[
             VMEM((share, width), jnp.bfloat16),
-            VMEM((width - staged, lm_head.shape[1]), jnp.bfloat16),
+            VMEM(lm_head.shape, jnp.bfloat16),
             pltpu.SemaphoreType.DMA((4,)),
         ],
         compiler_params=grant(24),

time: 29.5 us -> 29.9 us (1.014)
  Pallas kernels: 6.34 us -> 6.73 us
    pallas_call x1, Pallas kernels: 2.08 us -> 2.47 us  [local(): pl.pallas_call(score_kernel, out_shape=(jax.ShapeDtypeStruct((1, STATS *...]
where the time goes in v21:
time: 29.9 us; the launch traced here: 29.6 us
  blocking collectives  11 us (37%)
  starting transfers between devices  8.37 us (28%)
  Pallas kernels  6.73 us (23%)
  waiting for transfers between devices  2.83 us (9%)
  between operations  0.66 us (2%)
    all_to_all x1, blocking collectives, local(): gathered = lax.all_to_all(copies, ('req', 'tp'), 0, 0)  11 us
    all_to_all x1, starting transfers between devices, local(): lax.all_to_all(packed, 'req', 0, 0, axis_index_groups=[members(groups)])  7.86 us
    all_to_all x1, waiting for transfers between devices, local(): lax.all_to_all(packed, 'req', 0, 0, axis_index_groups=[members(groups)])  2.83 us
    pallas_call x1, Pallas kernels, local(): pl.pallas_call(score_kernel, out_shape=(jax.ShapeDtypeStruct((1, STATS *...  2.47 us
    pallas_call x1, Pallas kernels, local(): pl.pallas_call(functools.partial(stage_kernel, share), out_shape=(VMEM(lm...  1.89 us
    pallas_call x1, Pallas kernels, local(): pl.pallas_call(functools.partial(pack_kernel, share), out_shape=VMEM((gro...  1.68 us
    pallas_call x1, Pallas kernels, local(): pl.pallas_call(functools.partial(finish_kernel, share), out_shape=(jax.Sh...  0.69 us
  transfers between devices with their start and end apart: 2, of which 1 were waited for; matrix products, arithmetic and copies ran while one was open for 0% of the time, Pallas kernels for 12%

profile of v21, /device:TPU:0, one launch (start us, length us, event | category | flops | bytes accessed | tf_op | source)
XLA Modules:
  0.0 29.6 jit_solution(15344715966697374553)
XLA Ops:
  0.6 0.5 %collective-permute-start = (bf16[4096,256]{1,0:T(8,128)(2,1)}, bf16[4096,256]{1,0:T(8,128)(2,1)}, u32[]{:S(2)}, u32[]{:S(2)}) collective-permute-start(bf16[4096,256]{1,0:T(8,128)(2,1)} %own_ref.1), channel_id=1, source_target_pairs={{0,1},{1,0},{2,3},{3,2},{4,5},{5,4},{6,7},{7,6},{8,9},{9,8},{10,11... | collective-permute-start | bytes 6291464 | tf_op jit(solution)/shard_map/ppermute | solution.py:227
  1.1 1.7 %shard_map.85 = bf16[8,8,1152]{2,1,0:T(8,128)(2,1)} custom-call(bf16[8,4096]{1,0:T(8,128)(2,1)} %hidden_ref.1, bf16[32,128]{1,0:T(8,128)(2,1)} %bitcast.5, s32[8]{0:T(128)} %targets_ref.1, s32[8]{0:T(128)} %segments_ref.1, s32[8]{0:T(128)} %scored_ref.1), custom_call_target="tpu_custom_call" | custom-call | tf_op jit(solution)/shard_map/pallas_call | solution.py:228
  2.8 7.9 %all-to-all-start = ((bf16[8,8,1152]{2,1,0:T(8,128)(2,1)}), bf16[8,8,1152]{2,1,0:T(8,128)(2,1)S(1)}, u32[]{:S(2)}, u32[]{:S(2)}) async-start(bf16[8,8,1152]{2,1,0:T(8,128)(2,1)} %shard_map.85), calls=%async_computation | async-start | bytes 294912 | tf_op jit(solution)/shard_map/all_to_all | solution.py:239
  10.7 0.0 collective-permute-done.other_ref
  10.7 1.9 %shard_map.86 = (bf16[4096,256]{1,0:T(8,128)(2,1)S(1)}, bf16[2048,256]{1,0:T(8,128)(2,1)S(1)}, bf16[64,64]{1,0:T(8,128)(2,1)S(1)}) custom-call(bf16[4096,256]{1,0:T(8,128)(2,1)} %own_ref.1, bf16[4096,256]{1,0:T(8,128)(2,1)} %collective-permute-done.other_ref), custom_call_target="tpu_custom_call" | custom-call | bytes 6291456 | tf_op jit(solution)/shard_map/pallas_call | solution.py:242
  12.6 2.8 %all-to-all-done.rows_ref = bf16[8,8,1152]{2,1,0:T(8,128)(2,1)S(1)} async-done(((bf16[8,8,1152]{2,1,0:T(8,128)(2,1)}), bf16[8,8,1152]{2,1,0:T(8,128)(2,1)S(1)}, u32[]{:S(2)}, u32[]{:S(2)}) %all-to-all-start) | async-done | bytes 147488 | tf_op jit(solution)/shard_map/all_to_all | solution.py:239
  15.4 2.5 %shard_map.87 = (f32[1,128]{1,0:T(1,128)S(1)}, f32[8,128]{1,0:T(8,128)S(1)}) custom-call(bf16[8,8,1152]{2,1,0:T(8,128)(2,1)S(1)} %all-to-all-done.rows_ref, bf16[4096,256]{1,0:T(8,128)(2,1)S(1)} %get-tuple-element.8.own_ref, bf16[2048,256]{1,0:T(8,128)(2,1)S(1)} %get-tuple-element.9.upper_ref, bf16[64,64]{1,0:T(8,128)(2,1)S(1)} %get-tuple-element.10.order_ref, ...), custom_call_target="tpu_custom_call" | custom-call | tf_op jit(solution)/shard_map/pallas_call | solution.py:255
  17.9 11.0 %all_to_all.10 = f32[32,1,128]{2,1,0:T(1,128)S(1)} all-to-all(f32[32,1,128]{2,1,0:T(1,128)S(1)} %broadcast_in_dim.9), channel_id=1, replica_groups=mesh['req'=8,'tp'=4] {'req','tp'}, dimensions={0} | all-to-all | bytes 32768 | tf_op jit(solution)/shard_map/all_to_all | solution.py:271
  28.9 0.7 %shard_map.88 = (f32[8]{0:T(128)}, f32[8]{0:T(128)}, f32[4]{0:T(128)}) custom-call(f32[32,128]{1,0:T(8,128)S(1)} %bitcast.3, f32[8,128]{1,0:T(8,128)S(1)} %get-tuple-element.12.meta_ref), custom_call_target="tpu_custom_call" | custom-call | tf_op jit(solution)/shard_map/pallas_call | solution.py:273
  (1 shorter events, 0.0 us)
Async XLA Ops:
  0.6 10.1 %collective-permute-start = (bf16[4096,256]{1,0:T(8,128)(2,1)}, bf16[4096,256]{1,0:T(8,128)(2,1)}, u32[]{:S(2)}, u32[]{:S(2)}) collective-permute-start(bf16[4096,256]{1,0:T(8,128)(2,1)} %own_ref.1), channel_id=1, source_target_pairs={{0,1},{1,0},{2,3},{3,2},{4,5},{5,4},{6,7},{7,6},{8,9},{9,8},{10,11... | collective-permute-start | bytes 6291464 | tf_op jit(solution)/shard_map/ppermute | solution.py:227
  2.8 12.6 %all-to-all-start = ((bf16[8,8,1152]{2,1,0:T(8,128)(2,1)}), bf16[8,8,1152]{2,1,0:T(8,128)(2,1)S(1)}, u32[]{:S(2)}, u32[]{:S(2)}) async-start(bf16[8,8,1152]{2,1,0:T(8,128)(2,1)} %shard_map.85), calls=%async_computation | async-start | bytes 294912 | tf_op jit(solution)/shard_map/all_to_all | solution.py:239

commit v22 on v21

--- a/solution.py
+++ b/solution.py
@@ -111,16 +111,18 @@
         copy.wait()
 
 
-def score_kernel(rows_ref, own_ref, upper_ref, order_ref, other_ref, stats_ref, meta_ref, ordered_ref, whole_ref, sems):
+def score_kernel(rows_ref, own_ref, upper_ref, order_ref, other_ref, stats_ref, meta_ref, ordered_ref, lower_ref, sems):
     width, cols = own_ref.shape
-    staged, chunk = upper_ref.shape[0], width // sems.shape[0]
-
-    def fetch(source, at):
-        piece = pl.ds(at * chunk, chunk)
-        return pltpu.make_async_copy(source.at[piece], whole_ref.at[piece], sems.at[at])
-
-    for at in range(sems.shape[0]):
-        fetch(upper_ref if at * chunk < staged else other_ref, at).start()
+    staged = upper_ref.shape[0]
+    depth = lower_ref.shape[0] // sems.shape[0]
+    copies = [
+        pltpu.make_async_copy(
+            other_ref.at[pl.ds(staged + i * depth, depth)], lower_ref.at[pl.ds(i * depth, depth)], sems.at[i]
+        )
+        for i in range(sems.shape[0])
+    ]
+    for copy in copies:
+        copy.start()
     groups = rows_ref.shape[0]
     parts = SUBS // MINE
     span = width // parts
@@ -138,15 +140,25 @@
         meta = meta + rows_ref[q, :, span:].astype(jnp.float32)
     meta_ref[...] = meta
 
-    def step(at, sums):
-        piece = pl.ds(pl.multiple_of(at * chunk, chunk), chunk)
-        rows = ordered_ref[:, piece]
-        own = sums[0] + jnp.dot(rows, own_ref[piece, :], preferred_element_type=jnp.float32)
-        fetch(other_ref, at).wait()
-        return own, sums[1] + jnp.dot(rows, whole_ref[piece, :], preferred_element_type=jnp.float32)
+    def product(slice_ref, first, at, depth):
+        piece = pl.ds(pl.multiple_of(at * depth, depth), depth)
+        rows = ordered_ref[:, pl.ds(pl.multiple_of(first + at * depth, depth), depth)]
+        return jnp.dot(rows, slice_ref[piece, :], preferred_element_type=jnp.float32)
+
+    def resident(at, sums):
+        return (
+            sums[0] + product(own_ref, 0, at, width // 2),
+            sums[1] + product(upper_ref, 0, at, staged // 2),
+        )
+
+    def fetched(at, total):
+        return total + product(lower_ref, staged, at, (width - staged) // 2)
 
     zeros = jnp.zeros((share, cols), jnp.float32)
-    logits = jnp.concatenate(lax.fori_loop(0, width // chunk, step, (zeros, zeros)), axis=1)
+    own_logits, other_logits = lax.fori_loop(0, 2, resident, (zeros, zeros))
+    for copy in copies:
+        copy.wait()
+    logits = jnp.concatenate([own_logits, lax.fori_loop(0, 2, fetched, other_logits)], axis=1)
     lanes = max(share, LANES)
     sub, lane = iota((share, lanes), 0), iota((share, lanes), 1)
     ids = meta[0:1, :lanes] + 256.0 * meta[1:2, :lanes] + 65536.0 * meta[2:3, :lanes]
@@ -262,7 +274,7 @@
         out_specs=(spec(VMEM), spec(VMEM)),
         scratch_shapes=[
             VMEM((share, width), jnp.bfloat16),
-            VMEM(lm_head.shape, jnp.bfloat16),
+            VMEM((width - staged, lm_head.shape[1]), jnp.bfloat16),
             pltpu.SemaphoreType.DMA((4,)),
         ],
         compiler_params=grant(24),

time: 29.9 us -> 29.2 us (0.977)
  Pallas kernels: 6.73 us -> 6.04 us
    pallas_call x1, Pallas kernels: 2.47 us -> 1.78 us  [local(): pl.pallas_call(score_kernel, out_shape=(jax.ShapeDtypeStruct((1, STATS *...]
where the time goes in v22:
time: 29.2 us; the launch traced here: 28.9 us
  blocking collectives  11 us (38%)
  starting transfers between devices  8.37 us (29%)
  Pallas kernels  6.04 us (21%)
  waiting for transfers between devices  2.83 us (10%)
  between operations  0.66 us (2%)
    all_to_all x1, blocking collectives, local(): gathered = lax.all_to_all(copies, ('req', 'tp'), 0, 0)  11 us
    all_to_all x1, starting transfers between devices, local(): lax.all_to_all(packed, 'req', 0, 0, axis_index_groups=[members(groups)])  7.86 us
    all_to_all x1, waiting for transfers between devices, local(): lax.all_to_all(packed, 'req', 0, 0, axis_index_groups=[members(groups)])  2.83 us
    pallas_call x1, Pallas kernels, local(): pl.pallas_call(functools.partial(stage_kernel, share), out_shape=(VMEM(lm...  1.89 us
    pallas_call x1, Pallas kernels, local(): pl.pallas_call(score_kernel, out_shape=(jax.ShapeDtypeStruct((1, STATS *...  1.78 us
    pallas_call x1, Pallas kernels, local(): pl.pallas_call(functools.partial(pack_kernel, share), out_shape=VMEM((gro...  1.68 us
    pallas_call x1, Pallas kernels, local(): pl.pallas_call(functools.partial(finish_kernel, share), out_shape=(jax.Sh...  0.69 us
  transfers between devices with their start and end apart: 2, of which 1 were waited for; matrix products, arithmetic and copies ran while one was open for 0% of the time, Pallas kernels for 12%

profile of v22, /device:TPU:0, one launch (start us, length us, event | category | flops | bytes accessed | tf_op | source)
XLA Modules:
  0.0 28.9 jit_solution(2936891741192184812)
XLA Ops:
  0.6 0.5 %collective-permute-start = (bf16[4096,256]{1,0:T(8,128)(2,1)}, bf16[4096,256]{1,0:T(8,128)(2,1)}, u32[]{:S(2)}, u32[]{:S(2)}) collective-permute-start(bf16[4096,256]{1,0:T(8,128)(2,1)} %own_ref.1), channel_id=1, source_target_pairs={{0,1},{1,0},{2,3},{3,2},{4,5},{5,4},{6,7},{7,6},{8,9},{9,8},{10,11... | collective-permute-start | bytes 6291464 | tf_op jit(solution)/shard_map/ppermute | solution.py:239
  1.1 1.7 %shard_map.85 = bf16[8,8,1152]{2,1,0:T(8,128)(2,1)} custom-call(bf16[8,4096]{1,0:T(8,128)(2,1)} %hidden_ref.1, bf16[32,128]{1,0:T(8,128)(2,1)} %bitcast.5, s32[8]{0:T(128)} %targets_ref.1, s32[8]{0:T(128)} %segments_ref.1, s32[8]{0:T(128)} %scored_ref.1), custom_call_target="tpu_custom_call" | custom-call | tf_op jit(solution)/shard_map/pallas_call | solution.py:240
  2.8 7.9 %all-to-all-start = ((bf16[8,8,1152]{2,1,0:T(8,128)(2,1)}), bf16[8,8,1152]{2,1,0:T(8,128)(2,1)S(1)}, u32[]{:S(2)}, u32[]{:S(2)}) async-start(bf16[8,8,1152]{2,1,0:T(8,128)(2,1)} %shard_map.85), calls=%async_computation | async-start | bytes 294912 | tf_op jit(solution)/shard_map/all_to_all | solution.py:251
  10.7 0.0 collective-permute-done.other_ref
  10.7 1.9 %shard_map.86 = (bf16[4096,256]{1,0:T(8,128)(2,1)S(1)}, bf16[2048,256]{1,0:T(8,128)(2,1)S(1)}, bf16[64,64]{1,0:T(8,128)(2,1)S(1)}) custom-call(bf16[4096,256]{1,0:T(8,128)(2,1)} %own_ref.1, bf16[4096,256]{1,0:T(8,128)(2,1)} %collective-permute-done.other_ref), custom_call_target="tpu_custom_call" | custom-call | bytes 6291456 | tf_op jit(solution)/shard_map/pallas_call | solution.py:254
  12.6 2.8 %all-to-all-done.rows_ref = bf16[8,8,1152]{2,1,0:T(8,128)(2,1)S(1)} async-done(((bf16[8,8,1152]{2,1,0:T(8,128)(2,1)}), bf16[8,8,1152]{2,1,0:T(8,128)(2,1)S(1)}, u32[]{:S(2)}, u32[]{:S(2)}) %all-to-all-start) | async-done | bytes 147488 | tf_op jit(solution)/shard_map/all_to_all | solution.py:251
  15.4 1.8 %shard_map.87 = (f32[1,128]{1,0:T(1,128)S(1)}, f32[8,128]{1,0:T(8,128)S(1)}) custom-call(bf16[8,8,1152]{2,1,0:T(8,128)(2,1)S(1)} %all-to-all-done.rows_ref, bf16[4096,256]{1,0:T(8,128)(2,1)S(1)} %get-tuple-element.8.own_ref, bf16[2048,256]{1,0:T(8,128)(2,1)S(1)} %get-tuple-element.9.upper_ref, bf16[64,64]{1,0:T(8,128)(2,1)S(1)} %get-tuple-element.10.order_ref, ...), custom_call_target="tpu_custom_call" | custom-call | tf_op jit(solution)/shard_map/pallas_call | solution.py:267
  17.2 11.0 %all_to_all.10 = f32[32,1,128]{2,1,0:T(1,128)S(1)} all-to-all(f32[32,1,128]{2,1,0:T(1,128)S(1)} %broadcast_in_dim.9), channel_id=1, replica_groups=mesh['req'=8,'tp'=4] {'req','tp'}, dimensions={0} | all-to-all | bytes 32768 | tf_op jit(solution)/shard_map/all_to_all | solution.py:283
  28.2 0.7 %shard_map.88 = (f32[8]{0:T(128)}, f32[8]{0:T(128)}, f32[4]{0:T(128)}) custom-call(f32[32,128]{1,0:T(8,128)S(1)} %bitcast.3, f32[8,128]{1,0:T(8,128)S(1)} %get-tuple-element.12.meta_ref), custom_call_target="tpu_custom_call" | custom-call | tf_op jit(solution)/shard_map/pallas_call | solution.py:285
  (1 shorter events, 0.0 us)
Async XLA Ops:
  0.6 10.1 %collective-permute-start = (bf16[4096,256]{1,0:T(8,128)(2,1)}, bf16[4096,256]{1,0:T(8,128)(2,1)}, u32[]{:S(2)}, u32[]{:S(2)}) collective-permute-start(bf16[4096,256]{1,0:T(8,128)(2,1)} %own_ref.1), channel_id=1, source_target_pairs={{0,1},{1,0},{2,3},{3,2},{4,5},{5,4},{6,7},{7,6},{8,9},{9,8},{10,11... | collective-permute-start | bytes 6291464 | tf_op jit(solution)/shard_map/ppermute | solution.py:239
  2.8 12.6 %all-to-all-start = ((bf16[8,8,1152]{2,1,0:T(8,128)(2,1)}), bf16[8,8,1152]{2,1,0:T(8,128)(2,1)S(1)}, u32[]{:S(2)}, u32[]{:S(2)}) async-start(bf16[8,8,1152]{2,1,0:T(8,128)(2,1)} %shard_map.85), calls=%async_computation | async-start | bytes 294912 | tf_op jit(solution)/shard_map/all_to_all | solution.py:251

commit v23 on v22

--- a/solution.py
+++ b/solution.py
@@ -32,14 +32,12 @@
 
 
 def members(count):
-    quarter = count // 4
-    return [*reversed(range(quarter, count - quarter)), *range(quarter), *range(count - quarter, count)]
+    return [(5 * count // 8 + at) % count for at in range(count)]
 
 
 def own_slot(count):
-    own, quarter = lax.axis_index("req"), count // 4
-    middle = count - quarter - 1 - own
-    return jnp.where(own < quarter, own + count - 2 * quarter, jnp.where(own < count - quarter, middle, own))
+    at = lax.axis_index("req") - 5 * count // 8
+    return jnp.where(at < 0, at + count, at)
 
 
 def pack_kernel(share, hidden_ref, gain_ref, targets_ref, segments_ref, scored_ref, out_ref, wide_ref, parts_ref, gains_ref):

time: 29.2 us -> 29 us (level)
  blocking collectives: 11 us -> 10.6 us
    all_to_all x1, blocking collectives: 11 us -> 10.6 us  [local(): gathered = lax.all_to_all(copies, ('req', 'tp'), 0, 0)]
where the time goes in v23:
time: 29 us; the launch traced here: 28.7 us
  blocking collectives  10.6 us (37%)
  starting transfers between devices  8.37 us (29%)
  Pallas kernels  6.04 us (21%)
  waiting for transfers between devices  3 us (10%)
  between operations  0.66 us (2%)
    all_to_all x1, blocking collectives, local(): gathered = lax.all_to_all(copies, ('req', 'tp'), 0, 0)  10.6 us
    all_to_all x1, starting transfers between devices, local(): lax.all_to_all(packed, 'req', 0, 0, axis_index_groups=[members(groups)])  7.85 us
    all_to_all x1, waiting for transfers between devices, local(): lax.all_to_all(packed, 'req', 0, 0, axis_index_groups=[members(groups)])  3 us
    pallas_call x1, Pallas kernels, local(): pl.pallas_call(functools.partial(stage_kernel, share), out_shape=(VMEM(lm...  1.89 us
    pallas_call x1, Pallas kernels, local(): pl.pallas_call(score_kernel, out_shape=(jax.ShapeDtypeStruct((1, STATS *...  1.78 us
    pallas_call x1, Pallas kernels, local(): pl.pallas_call(functools.partial(pack_kernel, share), out_shape=VMEM((gro...  1.68 us
    pallas_call x1, Pallas kernels, local(): pl.pallas_call(functools.partial(finish_kernel, share), out_shape=(jax.Sh...  0.69 us
  transfers between devices with their start and end apart: 2, of which 1 were waited for; matrix products, arithmetic and copies ran while one was open for 0% of the time, Pallas kernels for 12%

profile of v23, /device:TPU:0, one launch (start us, length us, event | category | flops | bytes accessed | tf_op | source)
XLA Modules:
  0.0 28.7 jit_solution(11130206161274342191)
XLA Ops:
  0.6 0.5 %collective-permute-start = (bf16[4096,256]{1,0:T(8,128)(2,1)}, bf16[4096,256]{1,0:T(8,128)(2,1)}, u32[]{:S(2)}, u32[]{:S(2)}) collective-permute-start(bf16[4096,256]{1,0:T(8,128)(2,1)} %own_ref.1), channel_id=1, source_target_pairs={{0,1},{1,0},{2,3},{3,2},{4,5},{5,4},{6,7},{7,6},{8,9},{9,8},{10,11... | collective-permute-start | bytes 6291464 | tf_op jit(solution)/shard_map/ppermute | solution.py:237
  1.1 1.7 %shard_map.85 = bf16[8,8,1152]{2,1,0:T(8,128)(2,1)} custom-call(bf16[8,4096]{1,0:T(8,128)(2,1)} %hidden_ref.1, bf16[32,128]{1,0:T(8,128)(2,1)} %bitcast.5, s32[8]{0:T(128)} %targets_ref.1, s32[8]{0:T(128)} %segments_ref.1, s32[8]{0:T(128)} %scored_ref.1), custom_call_target="tpu_custom_call" | custom-call | tf_op jit(solution)/shard_map/pallas_call | solution.py:238
  2.8 7.8 %all-to-all-start = ((bf16[8,8,1152]{2,1,0:T(8,128)(2,1)}), bf16[8,8,1152]{2,1,0:T(8,128)(2,1)S(1)}, u32[]{:S(2)}, u32[]{:S(2)}) async-start(bf16[8,8,1152]{2,1,0:T(8,128)(2,1)} %shard_map.85), calls=%async_computation | async-start | bytes 294912 | tf_op jit(solution)/shard_map/all_to_all | solution.py:249
  10.7 0.0 collective-permute-done.other_ref
  10.7 1.9 %shard_map.86 = (bf16[4096,256]{1,0:T(8,128)(2,1)S(1)}, bf16[2048,256]{1,0:T(8,128)(2,1)S(1)}, bf16[64,64]{1,0:T(8,128)(2,1)S(1)}) custom-call(bf16[4096,256]{1,0:T(8,128)(2,1)} %own_ref.1, bf16[4096,256]{1,0:T(8,128)(2,1)} %collective-permute-done.other_ref), custom_call_target="tpu_custom_call" | custom-call | bytes 6291456 | tf_op jit(solution)/shard_map/pallas_call | solution.py:252
  12.6 3.0 %all-to-all-done.rows_ref = bf16[8,8,1152]{2,1,0:T(8,128)(2,1)S(1)} async-done(((bf16[8,8,1152]{2,1,0:T(8,128)(2,1)}), bf16[8,8,1152]{2,1,0:T(8,128)(2,1)S(1)}, u32[]{:S(2)}, u32[]{:S(2)}) %all-to-all-start) | async-done | bytes 147488 | tf_op jit(solution)/shard_map/all_to_all | solution.py:249
  15.6 1.8 %shard_map.87 = (f32[1,128]{1,0:T(1,128)S(1)}, f32[8,128]{1,0:T(8,128)S(1)}) custom-call(bf16[8,8,1152]{2,1,0:T(8,128)(2,1)S(1)} %all-to-all-done.rows_ref, bf16[4096,256]{1,0:T(8,128)(2,1)S(1)} %get-tuple-element.8.own_ref, bf16[2048,256]{1,0:T(8,128)(2,1)S(1)} %get-tuple-element.9.upper_ref, bf16[64,64]{1,0:T(8,128)(2,1)S(1)} %get-tuple-element.10.order_ref, ...), custom_call_target="tpu_custom_call" | custom-call | tf_op jit(solution)/shard_map/pallas_call | solution.py:265
  17.4 10.6 %all_to_all.10 = f32[32,1,128]{2,1,0:T(1,128)S(1)} all-to-all(f32[32,1,128]{2,1,0:T(1,128)S(1)} %broadcast_in_dim.9), channel_id=1, replica_groups=mesh['req'=8,'tp'=4] {'req','tp'}, dimensions={0} | all-to-all | bytes 32768 | tf_op jit(solution)/shard_map/all_to_all | solution.py:281
  28.0 0.7 %shard_map.88 = (f32[8]{0:T(128)}, f32[8]{0:T(128)}, f32[4]{0:T(128)}) custom-call(f32[32,128]{1,0:T(8,128)S(1)} %bitcast.3, f32[8,128]{1,0:T(8,128)S(1)} %get-tuple-element.12.meta_ref), custom_call_target="tpu_custom_call" | custom-call | tf_op jit(solution)/shard_map/pallas_call | solution.py:283
  (1 shorter events, 0.0 us)
Async XLA Ops:
  0.6 10.0 %collective-permute-start = (bf16[4096,256]{1,0:T(8,128)(2,1)}, bf16[4096,256]{1,0:T(8,128)(2,1)}, u32[]{:S(2)}, u32[]{:S(2)}) collective-permute-start(bf16[4096,256]{1,0:T(8,128)(2,1)} %own_ref.1), channel_id=1, source_target_pairs={{0,1},{1,0},{2,3},{3,2},{4,5},{5,4},{6,7},{7,6},{8,9},{9,8},{10,11... | collective-permute-start | bytes 6291464 | tf_op jit(solution)/shard_map/ppermute | solution.py:237
  2.8 12.7 %all-to-all-start = ((bf16[8,8,1152]{2,1,0:T(8,128)(2,1)}), bf16[8,8,1152]{2,1,0:T(8,128)(2,1)S(1)}, u32[]{:S(2)}, u32[]{:S(2)}) async-start(bf16[8,8,1152]{2,1,0:T(8,128)(2,1)} %shard_map.85), calls=%async_computation | async-start | bytes 294912 | tf_op jit(solution)/shard_map/all_to_all | solution.py:249

commit v24 on v23

--- a/solution.py
+++ b/solution.py
@@ -234,7 +234,8 @@
     def spec(space):
         return pl.BlockSpec(memory_space=space)
 
-    other = lax.ppermute(lm_head, "tp", [(i, i + 1 - 2 * (i % PAIR)) for i in range(tp_count)])
+    swap = [(i, i + 1 - 2 * (i % PAIR)) for i in range(tp_count)]
+    other = lax.ppermute(lm_head, "tp", swap)
     packed = pl.pallas_call(
         functools.partial(pack_kernel, share),
         out_shape=VMEM((groups, SUBS, span + lanes), jnp.bfloat16),
@@ -277,9 +278,12 @@
         ],
         compiler_params=grant(24),
     )(rows, *(pltpu.with_memory_space_constraint(part, VMEM) for part in slices), other)
-    copies = jnp.broadcast_to(stats[None], (groups * tp_count,) + stats.shape)
-    gathered = lax.all_to_all(copies, ("req", "tp"), 0, 0)
-    gathered = gathered.reshape(groups * tp_count, stats.shape[1])
+    swapped = lax.ppermute(stats, "tp", swap)
+    stats = jnp.where(iota(stats.shape, 1) < PAIR * share, jnp.maximum(stats, swapped), stats + swapped)
+    chips = groups * tp_count // PAIR
+    copies = jnp.broadcast_to(stats[None], (chips,) + stats.shape)
+    listed = [[*reversed(range(at, groups * tp_count, PAIR))] for at in range(PAIR)]
+    gathered = lax.all_to_all(copies, ("req", "tp"), 0, 0, axis_index_groups=listed).reshape(chips, stats.shape[1])
     return pl.pallas_call(
         functools.partial(finish_kernel, share),
         out_shape=(

time: 29 us -> 28.7 us (0.990)
  blocking collectives: 10.6 us -> 9.1 us
  waiting for transfers between devices: 3 us -> 4.11 us
    all_to_all x1, blocking collectives: 10.6 us -> 9.1 us  [local(): lax.all_to_all(copies, ('req', 'tp'), 0, 0, axis_index_groups=listed)]
    ppermute x1 -> x2, waiting for transfers between devices: 0.01 us -> 1.11 us  [the longest x1 1.11 us: local(): swapped = lax.ppermute(stats, 'tp', swap)]
    ppermute x1 -> x2, starting transfers between devices: 0.52 us -> 0.59 us  [the longest x1 0.52 us: local(): other = lax.ppermute(lm_head, 'tp', swap)]
  transfers between devices with their start and end apart: 2 -> 3, of which waited for: 1 -> 2; matrix products, arithmetic and copies ran while one was open for 0% -> 0% of each run, Pallas kernels for 12% -> 13%
where the time goes in v24:
time: 28.7 us; the launch traced here: 28.4 us
  blocking collectives  9.1 us (32%)
  starting transfers between devices  8.44 us (29%)
  Pallas kernels  6.04 us (21%)
  waiting for transfers between devices  4.11 us (14%)
  between operations  0.66 us (2%)
    all_to_all x1, blocking collectives, local(): lax.all_to_all(copies, ('req', 'tp'), 0, 0, axis_index_groups=listed)  9.1 us
    all_to_all x1, starting transfers between devices, local(): lax.all_to_all(packed, 'req', 0, 0, axis_index_groups=[members(groups)])  7.85 us
    all_to_all x1, waiting for transfers between devices, local(): lax.all_to_all(packed, 'req', 0, 0, axis_index_groups=[members(groups)])  3 us
    pallas_call x1, Pallas kernels, local(): pl.pallas_call(functools.partial(stage_kernel, share), out_shape=(VMEM(lm...  1.89 us
    pallas_call x1, Pallas kernels, local(): pl.pallas_call(score_kernel, out_shape=(jax.ShapeDtypeStruct((1, STATS *...  1.78 us
    pallas_call x1, Pallas kernels, local(): pl.pallas_call(functools.partial(pack_kernel, share), out_shape=VMEM((gro...  1.68 us
    ppermute x1, waiting for transfers between devices, local(): swapped = lax.ppermute(stats, 'tp', swap)  1.11 us
    pallas_call x1, Pallas kernels, local(): pl.pallas_call(functools.partial(finish_kernel, share), out_shape=(jax.Sh...  0.69 us
  transfers between devices with their start and end apart: 3, of which 2 were waited for; matrix products, arithmetic and copies ran while one was open for 0% of the time, Pallas kernels for 13%

profile of v24, /device:TPU:0, one launch (start us, length us, event | category | flops | bytes accessed | tf_op | source)
XLA Modules:
  0.0 28.4 jit_solution(5300821351770326205)
XLA Ops:
  0.6 0.5 %collective-permute-start = (bf16[4096,256]{1,0:T(8,128)(2,1)}, bf16[4096,256]{1,0:T(8,128)(2,1)}, u32[]{:S(2)}, u32[]{:S(2)}) collective-permute-start(bf16[4096,256]{1,0:T(8,128)(2,1)} %own_ref.1), channel_id=1, source_target_pairs={{0,1},{1,0},{2,3},{3,2},{4,5},{5,4},{6,7},{7,6},{8,9},{9,8},{10,11... | collective-permute-start | bytes 6291464 | tf_op jit(solution)/shard_map/ppermute | solution.py:238
  1.1 1.7 %shard_map.85 = bf16[8,8,1152]{2,1,0:T(8,128)(2,1)} custom-call(bf16[8,4096]{1,0:T(8,128)(2,1)} %hidden_ref.1, bf16[32,128]{1,0:T(8,128)(2,1)} %bitcast.5, s32[8]{0:T(128)} %targets_ref.1, s32[8]{0:T(128)} %segments_ref.1, s32[8]{0:T(128)} %scored_ref.1), custom_call_target="tpu_custom_call" | custom-call | tf_op jit(solution)/shard_map/pallas_call | solution.py:239
  2.8 7.8 %all-to-all-start = ((bf16[8,8,1152]{2,1,0:T(8,128)(2,1)}), bf16[8,8,1152]{2,1,0:T(8,128)(2,1)S(1)}, u32[]{:S(2)}, u32[]{:S(2)}) async-start(bf16[8,8,1152]{2,1,0:T(8,128)(2,1)} %shard_map.85), calls=%async_computation | async-start | bytes 294912 | tf_op jit(solution)/shard_map/all_to_all | solution.py:250
  10.7 0.0 collective-permute-done.other_ref
  10.7 1.9 %shard_map.86 = (bf16[4096,256]{1,0:T(8,128)(2,1)S(1)}, bf16[2048,256]{1,0:T(8,128)(2,1)S(1)}, bf16[64,64]{1,0:T(8,128)(2,1)S(1)}) custom-call(bf16[4096,256]{1,0:T(8,128)(2,1)} %own_ref.1, bf16[4096,256]{1,0:T(8,128)(2,1)} %collective-permute-done.other_ref), custom_call_target="tpu_custom_call" | custom-call | bytes 6291456 | tf_op jit(solution)/shard_map/pallas_call | solution.py:253
  12.6 3.0 %all-to-all-done.rows_ref = bf16[8,8,1152]{2,1,0:T(8,128)(2,1)S(1)} async-done(((bf16[8,8,1152]{2,1,0:T(8,128)(2,1)}), bf16[8,8,1152]{2,1,0:T(8,128)(2,1)S(1)}, u32[]{:S(2)}, u32[]{:S(2)}) %all-to-all-start) | async-done | bytes 147488 | tf_op jit(solution)/shard_map/all_to_all | solution.py:250
  15.6 1.8 %shard_map.87 = (f32[1,128]{1,0:T(1,128)S(1)}, f32[8,128]{1,0:T(8,128)S(1)}) custom-call(bf16[8,8,1152]{2,1,0:T(8,128)(2,1)S(1)} %all-to-all-done.rows_ref, bf16[4096,256]{1,0:T(8,128)(2,1)S(1)} %get-tuple-element.8.own_ref, bf16[2048,256]{1,0:T(8,128)(2,1)S(1)} %get-tuple-element.9.upper_ref, bf16[64,64]{1,0:T(8,128)(2,1)S(1)} %get-tuple-element.10.order_ref, ...), custom_call_target="tpu_custom_call" | custom-call | tf_op jit(solution)/shard_map/pallas_call | solution.py:266
  17.4 0.1 collective-permute-start.1
  17.4 1.1 %collective-permute-done.1 = f32[1,128]{1,0:T(1,128)S(1)} collective-permute-done((f32[1,128]{1,0:T(1,128)S(1)}, f32[1,128]{1,0:T(1,128)S(1)}, u32[]{:S(2)}, u32[]{:S(2)}) %collective-permute-start.1) | collective-permute-done | bytes 544 | tf_op jit(solution)/shard_map/ppermute | solution.py:281
  18.6 9.1 %all_to_all.10 = f32[16,1,128]{2,1,0:T(1,128)S(1)} all-to-all(f32[16,1,128]{2,1,0:T(1,128)S(1)} %broadcast_in_dim.9), channel_id=1, replica_groups={{30,28,26,24,22,20,18,16,14,12,10,8,6,4,2,0},{31,29,27,25,23,21,19,17,1..., dimensions={0} | all-to-all | bytes 16384 | tf_op jit(solution)/shard_map/all_to_all | solution.py:286
  27.7 0.7 %shard_map.88 = (f32[8]{0:T(128)}, f32[8]{0:T(128)}, f32[4]{0:T(128)}) custom-call(f32[16,128]{1,0:T(8,128)S(1)} %bitcast.4, f32[8,128]{1,0:T(8,128)S(1)} %get-tuple-element.12.meta_ref), custom_call_target="tpu_custom_call" | custom-call | tf_op jit(solution)/shard_map/pallas_call | solution.py:287
  (2 shorter events, 0.0 us)
Async XLA Ops:
  0.6 10.0 %collective-permute-start = (bf16[4096,256]{1,0:T(8,128)(2,1)}, bf16[4096,256]{1,0:T(8,128)(2,1)}, u32[]{:S(2)}, u32[]{:S(2)}) collective-permute-start(bf16[4096,256]{1,0:T(8,128)(2,1)} %own_ref.1), channel_id=1, source_target_pairs={{0,1},{1,0},{2,3},{3,2},{4,5},{5,4},{6,7},{7,6},{8,9},{9,8},{10,11... | collective-permute-start | bytes 6291464 | tf_op jit(solution)/shard_map/ppermute | solution.py:238
  2.8 12.7 %all-to-all-start = ((bf16[8,8,1152]{2,1,0:T(8,128)(2,1)}), bf16[8,8,1152]{2,1,0:T(8,128)(2,1)S(1)}, u32[]{:S(2)}, u32[]{:S(2)}) async-start(bf16[8,8,1152]{2,1,0:T(8,128)(2,1)} %shard_map.85), calls=%async_computation | async-start | bytes 294912 | tf_op jit(solution)/shard_map/all_to_all | solution.py:250
  17.4 1.2 %collective-permute-start.1 = (f32[1,128]{1,0:T(1,128)S(1)}, f32[1,128]{1,0:T(1,128)S(1)}, u32[]{:S(2)}, u32[]{:S(2)}) collective-permute-start(f32[1,128]{1,0:T(1,128)S(1)} %get-tuple-element.11), channel_id=1, source_target_pairs={{0,1},{1,0},{2,3},{3,2},{4,5},{5,4},{6,7},{7,6},{8,9},{9,8},{10,11... | collective-permute-start | bytes 1544 | tf_op jit(solution)/shard_map/ppermute | solution.py:281

commit v25 on v24

--- a/solution.py
+++ b/solution.py
@@ -27,6 +27,14 @@
     return ranks, so_far
 
 
+def over(number, by):
+    return number >> (by.bit_length() - 1) if by & (by - 1) == 0 else number // by
+
+
+def left(number, by):
+    return number & (by - 1) if by & (by - 1) == 0 else number % by
+
+
 def iota(shape, axis):
     return lax.broadcasted_iota(jnp.int32, shape, axis)
 
@@ -40,13 +48,23 @@
     return jnp.where(at < 0, at + count, at)
 
 
-def pack_kernel(share, hidden_ref, gain_ref, targets_ref, segments_ref, scored_ref, out_ref, wide_ref, parts_ref, gains_ref):
+def pack_kernel(share, hidden_hbm, gain_hbm, targets_hbm, segments_hbm, scored_hbm, out_ref, *scratch):
+    hidden_ref, gain_ref, targets_ref, segments_ref, scored_ref, wide_ref, parts_ref, gains_ref, sems = scratch
+    sources = (scored_hbm, targets_hbm, segments_hbm, hidden_hbm, gain_hbm)
+    places = (scored_ref, targets_ref, segments_ref, hidden_ref, gain_ref)
+    reads = [pltpu.make_async_copy(source, to, sems.at[at]) for at, (source, to) in enumerate(zip(sources, places))]
+    for read in reads:
+        read.start()
     row_count, width = hidden_ref.shape
+    receivers = out_ref.shape[0]
     parts = SUBS // MINE
     span = width // parts
-    own, half = own_slot(out_ref.shape[0]), lax.axis_index("tp") % PAIR
-    wide_ref[...] = hidden_ref[...].astype(jnp.float32)
-    gains_ref[...] = gain_ref[...].astype(jnp.float32)
+    own, half = own_slot(receivers), lax.axis_index("tp") % PAIR
+    width_side = out_ref.shape[2] - span
+    sub, lane = iota((SUBS, width_side), 0), iota((SUBS, width_side), 1)
+    at_row, at_half = left(lane, share) - own * MINE, over(lane, share)
+    for read in reads[:3]:
+        read.wait()
     ranks, count = ranks_of(scored_ref, row_count)
     source = [jnp.int32(0)] * PICK
     for row in range(row_count):
@@ -56,28 +74,6 @@
     mine = [source[i] for i in range(MINE)]
     for h in range(1, PAIR):
         mine = [jnp.where(half == h, source[h * MINE + i], mine[i]) for i in range(MINE)]
-    for i in range(MINE):
-        for k in range(parts):
-            parts_ref[k * MINE + i : k * MINE + i + 1, :] = wide_ref[pl.ds(mine[i], 1), k * span : (k + 1) * span]
-    values = parts_ref[...]
-    part = jnp.broadcast_to(jnp.sum(values * values, axis=1, keepdims=True), (SUBS, LANES))
-    total = part
-    for k in range(1, parts):
-        total = total + pltpu.roll(part, k * MINE, 0)
-    row_scale = lax.rsqrt(total / width + 1e-05)
-    sub, lane = iota((SUBS, LANES), 0), iota((SUBS, LANES), 1)
-    chunks = span // LANES
-    for at in range(chunks):
-        gain = gains_ref[at : at + 1, :]
-        for k in range(1, parts):
-            gain = jnp.where(sub >= k * MINE, gains_ref[k * chunks + at : k * chunks + at + 1, :], gain)
-        piece = parts_ref[:, at * LANES : (at + 1) * LANES]
-        piece = (piece * row_scale * gain).astype(jnp.bfloat16)
-        for to in range(out_ref.shape[0]):
-            out_ref[to, :, at * LANES : (at + 1) * LANES] = piece
-    width_side = out_ref.shape[2] - span
-    sub, lane = iota((SUBS, width_side), 0), iota((SUBS, width_side), 1)
-    at_row, at_half = lane % share - own * MINE, lane // share
     side = jnp.zeros((SUBS, width_side), jnp.int32)
     for i in range(MINE):
         target = targets_ref[mine[i]]
@@ -89,8 +85,31 @@
             fields = jnp.where(at_half == h, jnp.where(sub == 3, segments_ref[source[r]], field), fields)
         side = jnp.where(at_row == i, jnp.where(sub < 3, digits, fields), side)
     side = side.astype(jnp.float32).astype(jnp.bfloat16)
-    for to in range(out_ref.shape[0]):
+    for to in range(receivers):
         out_ref[to, :, span:] = side
+    for read in reads[3:]:
+        read.wait()
+    wide_ref[...] = hidden_ref[...].astype(jnp.float32)
+    gains_ref[...] = gain_ref[...].astype(jnp.float32)
+    for i in range(MINE):
+        for k in range(parts):
+            parts_ref[k * MINE + i : k * MINE + i + 1, :] = wide_ref[pl.ds(mine[i], 1), k * span : (k + 1) * span]
+    values = parts_ref[...]
+    part = jnp.broadcast_to(jnp.sum(values * values, axis=1, keepdims=True), (SUBS, LANES))
+    total = part
+    for k in range(1, parts):
+        total = total + pltpu.roll(part, k * MINE, 0)
+    row_scale = lax.rsqrt(total / width + 1e-05)
+    sub = iota((SUBS, LANES), 0)
+    chunks = span // LANES
+    for at in range(chunks):
+        gain = gains_ref[at : at + 1, :]
+        for k in range(1, parts):
+            gain = jnp.where(sub >= k * MINE, gains_ref[k * chunks + at : k * chunks + at + 1, :], gain)
+        piece = parts_ref[:, at * LANES : (at + 1) * LANES]
+        piece = (piece * row_scale * gain).astype(jnp.bfloat16)
+        for to in range(receivers):
+            out_ref[to, :, at * LANES : (at + 1) * LANES] = piece
 
 
 def stage_kernel(share, own_ref, other_ref, own_out, other_out, order_out, sems):
@@ -238,13 +257,17 @@
     other = lax.ppermute(lm_head, "tp", swap)
     packed = pl.pallas_call(
         functools.partial(pack_kernel, share),
-        out_shape=VMEM((groups, SUBS, span + lanes), jnp.bfloat16),
-        in_specs=[spec(VMEM)] * 2 + [spec(SMEM)] * 3,
+        out_shape=jax.ShapeDtypeStruct((groups, SUBS, span + lanes), jnp.bfloat16),
+        in_specs=[spec(pltpu.HBM)] * 5,
         out_specs=spec(VMEM),
         scratch_shapes=[
+            VMEM((row_count, width), jnp.bfloat16),
+            VMEM((width // LANES, LANES), jnp.bfloat16),
+            *[SMEM((row_count,), jnp.int32)] * 3,
             VMEM((row_count, width), jnp.float32),
             VMEM((SUBS, span), jnp.float32),
             VMEM((width // LANES, LANES), jnp.float32),
+            pltpu.SemaphoreType.DMA((5,)),
         ],
     )(hidden, norm_gain.reshape(width // LANES, LANES), targets, segments, scored)
     rows = lax.all_to_all(packed, "req", 0, 0, axis_index_groups=[members(groups)])

time: 28.7 us -> 28.7 us (level)
  no operation moved by 1% of the time
where the time goes in v25:
time: 28.7 us; the launch traced here: 28.4 us
  blocking collectives  9.1 us (32%)
  starting transfers between devices  8.45 us (29%)
  Pallas kernels  6.04 us (21%)
  waiting for transfers between devices  4.11 us (14%)
  between operations  0.67 us (2%)
    all_to_all x1, blocking collectives, local(): lax.all_to_all(copies, ('req', 'tp'), 0, 0, axis_index_groups=listed)  9.1 us
    all_to_all x1, starting transfers between devices, local(): lax.all_to_all(packed, 'req', 0, 0, axis_index_groups=[members(groups)])  7.86 us
    all_to_all x1, waiting for transfers between devices, local(): lax.all_to_all(packed, 'req', 0, 0, axis_index_groups=[members(groups)])  3 us
    pallas_call x1, Pallas kernels, local(): pl.pallas_call(functools.partial(stage_kernel, share), out_shape=(VMEM(lm...  1.89 us
    pallas_call x1, Pallas kernels, local(): pl.pallas_call(score_kernel, out_shape=(jax.ShapeDtypeStruct((1, STATS *...  1.78 us
    pallas_call x1, Pallas kernels, local(): pl.pallas_call(functools.partial(pack_kernel, share), out_shape=jax.Shape...  1.69 us
    ppermute x1, waiting for transfers between devices, local(): swapped = lax.ppermute(stats, 'tp', swap)  1.11 us
    pallas_call x1, Pallas kernels, local(): pl.pallas_call(functools.partial(finish_kernel, share), out_shape=(jax.Sh...  0.69 us
  transfers between devices with their start and end apart: 3, of which 2 were waited for; matrix products, arithmetic and copies ran while one was open for 0% of the time, Pallas kernels for 13%

profile of v25, /device:TPU:0, one launch (start us, length us, event | category | flops | bytes accessed | tf_op | source)
XLA Modules:
  0.0 28.4 jit_solution(4526917251718319490)
XLA Ops:
  0.6 0.5 %collective-permute-start = (bf16[4096,256]{1,0:T(8,128)(2,1)}, bf16[4096,256]{1,0:T(8,128)(2,1)}, u32[]{:S(2)}, u32[]{:S(2)}) collective-permute-start(bf16[4096,256]{1,0:T(8,128)(2,1)} %own_ref.1), channel_id=1, source_target_pairs={{0,1},{1,0},{2,3},{3,2},{4,5},{5,4},{6,7},{7,6},{8,9},{9,8},{10,11... | collective-permute-start | bytes 6291464 | tf_op jit(solution)/shard_map/ppermute | solution.py:257
  1.1 1.7 %shard_map.85 = bf16[8,8,1152]{2,1,0:T(8,128)(2,1)} custom-call(bf16[8,4096]{1,0:T(8,128)(2,1)} %hidden_hbm.1, bf16[32,128]{1,0:T(8,128)(2,1)} %bitcast.5, s32[8]{0:T(128)} %targets_hbm.1, s32[8]{0:T(128)} %segments_hbm.1, s32[8]{0:T(128)} %scored_hbm.1), custom_call_target="tpu_custom_call" | custom-call | tf_op jit(solution)/shard_map/pallas_call | solution.py:258
  2.8 7.9 %all-to-all-start = ((bf16[8,8,1152]{2,1,0:T(8,128)(2,1)}), bf16[8,8,1152]{2,1,0:T(8,128)(2,1)S(1)}, u32[]{:S(2)}, u32[]{:S(2)}) async-start(bf16[8,8,1152]{2,1,0:T(8,128)(2,1)} %shard_map.85), calls=%async_computation | async-start | bytes 294912 | tf_op jit(solution)/shard_map/all_to_all | solution.py:273
  10.7 0.0 collective-permute-done.other_ref
  10.7 1.9 %shard_map.86 = (bf16[4096,256]{1,0:T(8,128)(2,1)S(1)}, bf16[2048,256]{1,0:T(8,128)(2,1)S(1)}, bf16[64,64]{1,0:T(8,128)(2,1)S(1)}) custom-call(bf16[4096,256]{1,0:T(8,128)(2,1)} %own_ref.1, bf16[4096,256]{1,0:T(8,128)(2,1)} %collective-permute-done.other_ref), custom_call_target="tpu_custom_call" | custom-call | bytes 6291456 | tf_op jit(solution)/shard_map/pallas_call | solution.py:276
  12.6 3.0 %all-to-all-done.rows_ref = bf16[8,8,1152]{2,1,0:T(8,128)(2,1)S(1)} async-done(((bf16[8,8,1152]{2,1,0:T(8,128)(2,1)}), bf16[8,8,1152]{2,1,0:T(8,128)(2,1)S(1)}, u32[]{:S(2)}, u32[]{:S(2)}) %all-to-all-start) | async-done | bytes 147488 | tf_op jit(solution)/shard_map/all_to_all | solution.py:273
  15.6 1.8 %shard_map.87 = (f32[1,128]{1,0:T(1,128)S(1)}, f32[8,128]{1,0:T(8,128)S(1)}) custom-call(bf16[8,8,1152]{2,1,0:T(8,128)(2,1)S(1)} %all-to-all-done.rows_ref, bf16[4096,256]{1,0:T(8,128)(2,1)S(1)} %get-tuple-element.8.own_ref, bf16[2048,256]{1,0:T(8,128)(2,1)S(1)} %get-tuple-element.9.upper_ref, bf16[64,64]{1,0:T(8,128)(2,1)S(1)} %get-tuple-element.10.order_ref, ...), custom_call_target="tpu_custom_call" | custom-call | tf_op jit(solution)/shard_map/pallas_call | solution.py:289
  17.4 0.1 collective-permute-start.1
  17.5 1.1 %collective-permute-done.1 = f32[1,128]{1,0:T(1,128)S(1)} collective-permute-done((f32[1,128]{1,0:T(1,128)S(1)}, f32[1,128]{1,0:T(1,128)S(1)}, u32[]{:S(2)}, u32[]{:S(2)}) %collective-permute-start.1) | collective-permute-done | bytes 544 | tf_op jit(solution)/shard_map/ppermute | solution.py:304
  18.6 9.1 %all_to_all.10 = f32[16,1,128]{2,1,0:T(1,128)S(1)} all-to-all(f32[16,1,128]{2,1,0:T(1,128)S(1)} %broadcast_in_dim.9), channel_id=1, replica_groups={{30,28,26,24,22,20,18,16,14,12,10,8,6,4,2,0},{31,29,27,25,23,21,19,17,1..., dimensions={0} | all-to-all | bytes 16384 | tf_op jit(solution)/shard_map/all_to_all | solution.py:309
  27.7 0.7 %shard_map.88 = (f32[8]{0:T(128)}, f32[8]{0:T(128)}, f32[4]{0:T(128)}) custom-call(f32[16,128]{1,0:T(8,128)S(1)} %bitcast.4, f32[8,128]{1,0:T(8,128)S(1)} %get-tuple-element.12.meta_ref), custom_call_target="tpu_custom_call" | custom-call | tf_op jit(solution)/shard_map/pallas_call | solution.py:310
  (2 shorter events, 0.0 us)
Async XLA Ops:
  0.6 10.1 %collective-permute-start = (bf16[4096,256]{1,0:T(8,128)(2,1)}, bf16[4096,256]{1,0:T(8,128)(2,1)}, u32[]{:S(2)}, u32[]{:S(2)}) collective-permute-start(bf16[4096,256]{1,0:T(8,128)(2,1)} %own_ref.1), channel_id=1, source_target_pairs={{0,1},{1,0},{2,3},{3,2},{4,5},{5,4},{6,7},{7,6},{8,9},{9,8},{10,11... | collective-permute-start | bytes 6291464 | tf_op jit(solution)/shard_map/ppermute | solution.py:257
  2.8 12.8 %all-to-all-start = ((bf16[8,8,1152]{2,1,0:T(8,128)(2,1)}), bf16[8,8,1152]{2,1,0:T(8,128)(2,1)S(1)}, u32[]{:S(2)}, u32[]{:S(2)}) async-start(bf16[8,8,1152]{2,1,0:T(8,128)(2,1)} %shard_map.85), calls=%async_computation | async-start | bytes 294912 | tf_op jit(solution)/shard_map/all_to_all | solution.py:273
  17.4 1.2 %collective-permute-start.1 = (f32[1,128]{1,0:T(1,128)S(1)}, f32[1,128]{1,0:T(1,128)S(1)}, u32[]{:S(2)}, u32[]{:S(2)}) collective-permute-start(f32[1,128]{1,0:T(1,128)S(1)} %get-tuple-element.11), channel_id=1, source_target_pairs={{0,1},{1,0},{2,3},{3,2},{4,5},{5,4},{6,7},{7,6},{8,9},{9,8},{10,11... | collective-permute-start | bytes 1544 | tf_op jit(solution)/shard_map/ppermute | solution.py:304

commit v26 on v24

--- a/solution.py
+++ b/solution.py
@@ -282,7 +282,9 @@
     stats = jnp.where(iota(stats.shape, 1) < PAIR * share, jnp.maximum(stats, swapped), stats + swapped)
     chips = groups * tp_count // PAIR
     copies = jnp.broadcast_to(stats[None], (chips,) + stats.shape)
-    listed = [[*reversed(range(at, groups * tp_count, PAIR))] for at in range(PAIR)]
+    first = 5 * groups // 8
+    order = [*reversed(range(first + 1)), *reversed(range(first + 1, groups))]
+    listed = [[q * tp_count + t for q in order for t in reversed(range(at, tp_count, PAIR))] for at in range(PAIR)]
     gathered = lax.all_to_all(copies, ("req", "tp"), 0, 0, axis_index_groups=listed).reshape(chips, stats.shape[1])
     return pl.pallas_call(
         functools.partial(finish_kernel, share),

time: 28.7 us -> 28.7 us (level)
  no operation moved by 1% of the time
where the time goes in v26:
time: 28.7 us; the launch traced here: 28.3 us
  blocking collectives  9.08 us (32%)
  starting transfers between devices  8.44 us (29%)
  Pallas kernels  6.04 us (21%)
  waiting for transfers between devices  4.11 us (14%)
  between operations  0.66 us (2%)
    all_to_all x1, blocking collectives, local(): lax.all_to_all(copies, ('req', 'tp'), 0, 0, axis_index_groups=listed)  9.08 us
    all_to_all x1, starting transfers between devices, local(): lax.all_to_all(packed, 'req', 0, 0, axis_index_groups=[members(groups)])  7.85 us
    all_to_all x1, waiting for transfers between devices, local(): lax.all_to_all(packed, 'req', 0, 0, axis_index_groups=[members(groups)])  3 us
    pallas_call x1, Pallas kernels, local(): pl.pallas_call(functools.partial(stage_kernel, share), out_shape=(VMEM(lm...  1.89 us
    pallas_call x1, Pallas kernels, local(): pl.pallas_call(score_kernel, out_shape=(jax.ShapeDtypeStruct((1, STATS *...  1.78 us
    pallas_call x1, Pallas kernels, local(): pl.pallas_call(functools.partial(pack_kernel, share), out_shape=VMEM((gro...  1.68 us
    ppermute x1, waiting for transfers between devices, local(): swapped = lax.ppermute(stats, 'tp', swap)  1.11 us
    pallas_call x1, Pallas kernels, local(): pl.pallas_call(functools.partial(finish_kernel, share), out_shape=(jax.Sh...  0.69 us
  transfers between devices with their start and end apart: 3, of which 2 were waited for; matrix products, arithmetic and copies ran while one was open for 0% of the time, Pallas kernels for 13%

profile of v26, /device:TPU:0, one launch (start us, length us, event | category | flops | bytes accessed | tf_op | source)
XLA Modules:
  0.0 28.3 jit_solution(10780228241128872208)
XLA Ops:
  0.6 0.5 %collective-permute-start = (bf16[4096,256]{1,0:T(8,128)(2,1)}, bf16[4096,256]{1,0:T(8,128)(2,1)}, u32[]{:S(2)}, u32[]{:S(2)}) collective-permute-start(bf16[4096,256]{1,0:T(8,128)(2,1)} %own_ref.1), channel_id=1, source_target_pairs={{0,1},{1,0},{2,3},{3,2},{4,5},{5,4},{6,7},{7,6},{8,9},{9,8},{10,11... | collective-permute-start | bytes 6291464 | tf_op jit(solution)/shard_map/ppermute | solution.py:238
  1.1 1.7 %shard_map.85 = bf16[8,8,1152]{2,1,0:T(8,128)(2,1)} custom-call(bf16[8,4096]{1,0:T(8,128)(2,1)} %hidden_ref.1, bf16[32,128]{1,0:T(8,128)(2,1)} %bitcast.5, s32[8]{0:T(128)} %targets_ref.1, s32[8]{0:T(128)} %segments_ref.1, s32[8]{0:T(128)} %scored_ref.1), custom_call_target="tpu_custom_call" | custom-call | tf_op jit(solution)/shard_map/pallas_call | solution.py:239
  2.8 7.8 %all-to-all-start = ((bf16[8,8,1152]{2,1,0:T(8,128)(2,1)}), bf16[8,8,1152]{2,1,0:T(8,128)(2,1)S(1)}, u32[]{:S(2)}, u32[]{:S(2)}) async-start(bf16[8,8,1152]{2,1,0:T(8,128)(2,1)} %shard_map.85), calls=%async_computation | async-start | bytes 294912 | tf_op jit(solution)/shard_map/all_to_all | solution.py:250
  10.7 0.0 collective-permute-done.other_ref
  10.7 1.9 %shard_map.86 = (bf16[4096,256]{1,0:T(8,128)(2,1)S(1)}, bf16[2048,256]{1,0:T(8,128)(2,1)S(1)}, bf16[64,64]{1,0:T(8,128)(2,1)S(1)}) custom-call(bf16[4096,256]{1,0:T(8,128)(2,1)} %own_ref.1, bf16[4096,256]{1,0:T(8,128)(2,1)} %collective-permute-done.other_ref), custom_call_target="tpu_custom_call" | custom-call | bytes 6291456 | tf_op jit(solution)/shard_map/pallas_call | solution.py:253
  12.6 3.0 %all-to-all-done.rows_ref = bf16[8,8,1152]{2,1,0:T(8,128)(2,1)S(1)} async-done(((bf16[8,8,1152]{2,1,0:T(8,128)(2,1)}), bf16[8,8,1152]{2,1,0:T(8,128)(2,1)S(1)}, u32[]{:S(2)}, u32[]{:S(2)}) %all-to-all-start) | async-done | bytes 147488 | tf_op jit(solution)/shard_map/all_to_all | solution.py:250
  15.6 1.8 %shard_map.87 = (f32[1,128]{1,0:T(1,128)S(1)}, f32[8,128]{1,0:T(8,128)S(1)}) custom-call(bf16[8,8,1152]{2,1,0:T(8,128)(2,1)S(1)} %all-to-all-done.rows_ref, bf16[4096,256]{1,0:T(8,128)(2,1)S(1)} %get-tuple-element.8.own_ref, bf16[2048,256]{1,0:T(8,128)(2,1)S(1)} %get-tuple-element.9.upper_ref, bf16[64,64]{1,0:T(8,128)(2,1)S(1)} %get-tuple-element.10.order_ref, ...), custom_call_target="tpu_custom_call" | custom-call | tf_op jit(solution)/shard_map/pallas_call | solution.py:266
  17.4 0.1 collective-permute-start.1
  17.4 1.1 %collective-permute-done.1 = f32[1,128]{1,0:T(1,128)S(1)} collective-permute-done((f32[1,128]{1,0:T(1,128)S(1)}, f32[1,128]{1,0:T(1,128)S(1)}, u32[]{:S(2)}, u32[]{:S(2)}) %collective-permute-start.1) | collective-permute-done | bytes 544 | tf_op jit(solution)/shard_map/ppermute | solution.py:281
  18.6 9.1 %all_to_all.10 = f32[16,1,128]{2,1,0:T(1,128)S(1)} all-to-all(f32[16,1,128]{2,1,0:T(1,128)S(1)} %broadcast_in_dim.9), channel_id=1, replica_groups={{22,20,18,16,14,12,10,8,6,4,2,0,30,28,26,24},{23,21,19,17,15,13,11,9,7,..., dimensions={0} | all-to-all | bytes 16384 | tf_op jit(solution)/shard_map/all_to_all | solution.py:288
  27.6 0.7 %shard_map.88 = (f32[8]{0:T(128)}, f32[8]{0:T(128)}, f32[4]{0:T(128)}) custom-call(f32[16,128]{1,0:T(8,128)S(1)} %bitcast.4, f32[8,128]{1,0:T(8,128)S(1)} %get-tuple-element.12.meta_ref), custom_call_target="tpu_custom_call" | custom-call | tf_op jit(solution)/shard_map/pallas_call | solution.py:289
  (2 shorter events, 0.0 us)
Async XLA Ops:
  0.6 10.0 %collective-permute-start = (bf16[4096,256]{1,0:T(8,128)(2,1)}, bf16[4096,256]{1,0:T(8,128)(2,1)}, u32[]{:S(2)}, u32[]{:S(2)}) collective-permute-start(bf16[4096,256]{1,0:T(8,128)(2,1)} %own_ref.1), channel_id=1, source_target_pairs={{0,1},{1,0},{2,3},{3,2},{4,5},{5,4},{6,7},{7,6},{8,9},{9,8},{10,11... | collective-permute-start | bytes 6291464 | tf_op jit(solution)/shard_map/ppermute | solution.py:238
  2.8 12.7 %all-to-all-start = ((bf16[8,8,1152]{2,1,0:T(8,128)(2,1)}), bf16[8,8,1152]{2,1,0:T(8,128)(2,1)S(1)}, u32[]{:S(2)}, u32[]{:S(2)}) async-start(bf16[8,8,1152]{2,1,0:T(8,128)(2,1)} %shard_map.85), calls=%async_computation | async-start | bytes 294912 | tf_op jit(solution)/shard_map/all_to_all | solution.py:250
  17.4 1.2 %collective-permute-start.1 = (f32[1,128]{1,0:T(1,128)S(1)}, f32[1,128]{1,0:T(1,128)S(1)}, u32[]{:S(2)}, u32[]{:S(2)}) collective-permute-start(f32[1,128]{1,0:T(1,128)S(1)} %get-tuple-element.11), channel_id=1, source_target_pairs={{0,1},{1,0},{2,3},{3,2},{4,5},{5,4},{6,7},{7,6},{8,9},{9,8},{10,11... | collective-permute-start | bytes 1544 | tf_op jit(solution)/shard_map/ppermute | solution.py:281

commit v27 on v26

--- a/solution.py
+++ b/solution.py
@@ -282,7 +282,7 @@
     stats = jnp.where(iota(stats.shape, 1) < PAIR * share, jnp.maximum(stats, swapped), stats + swapped)
     chips = groups * tp_count // PAIR
     copies = jnp.broadcast_to(stats[None], (chips,) + stats.shape)
-    first = 5 * groups // 8
+    first = 3 * groups // 8
     order = [*reversed(range(first + 1)), *reversed(range(first + 1, groups))]
     listed = [[q * tp_count + t for q in order for t in reversed(range(at, tp_count, PAIR))] for at in range(PAIR)]
     gathered = lax.all_to_all(copies, ("req", "tp"), 0, 0, axis_index_groups=listed).reshape(chips, stats.shape[1])

time: 28.7 us -> 29.4 us (1.024)
  blocking collectives: 9.08 us -> 9.8 us
    all_to_all x1, blocking collectives: 9.08 us -> 9.8 us  [local(): lax.all_to_all(copies, ('req', 'tp'), 0, 0, axis_index_groups=listed)]
  transfers between devices with their start and end apart: 3 -> 3, of which waited for: 2 -> 2; matrix products, arithmetic and copies ran while one was open for 0% -> 0% of each run, Pallas kernels for 13% -> 12%
where the time goes in v27:
time: 29.4 us; the launch traced here: 29 us
  blocking collectives  9.8 us (33%)
  starting transfers between devices  8.44 us (29%)
  Pallas kernels  6.04 us (21%)
  waiting for transfers between devices  4.11 us (14%)
  between operations  0.66 us (2%)
    all_to_all x1, blocking collectives, local(): lax.all_to_all(copies, ('req', 'tp'), 0, 0, axis_index_groups=listed)  9.8 us
    all_to_all x1, starting transfers between devices, local(): lax.all_to_all(packed, 'req', 0, 0, axis_index_groups=[members(groups)])  7.85 us
    all_to_all x1, waiting for transfers between devices, local(): lax.all_to_all(packed, 'req', 0, 0, axis_index_groups=[members(groups)])  3 us
    pallas_call x1, Pallas kernels, local(): pl.pallas_call(functools.partial(stage_kernel, share), out_shape=(VMEM(lm...  1.89 us
    pallas_call x1, Pallas kernels, local(): pl.pallas_call(score_kernel, out_shape=(jax.ShapeDtypeStruct((1, STATS *...  1.78 us
    pallas_call x1, Pallas kernels, local(): pl.pallas_call(functools.partial(pack_kernel, share), out_shape=VMEM((gro...  1.68 us
    ppermute x1, waiting for transfers between devices, local(): swapped = lax.ppermute(stats, 'tp', swap)  1.11 us
    pallas_call x1, Pallas kernels, local(): pl.pallas_call(functools.partial(finish_kernel, share), out_shape=(jax.Sh...  0.69 us
  transfers between devices with their start and end apart: 3, of which 2 were waited for; matrix products, arithmetic and copies ran while one was open for 0% of the time, Pallas kernels for 12%

profile of v27, /device:TPU:0, one launch (start us, length us, event | category | flops | bytes accessed | tf_op | source)
XLA Modules:
  0.0 29.0 jit_solution(9970258777316995894)
XLA Ops:
  0.6 0.5 %collective-permute-start = (bf16[4096,256]{1,0:T(8,128)(2,1)}, bf16[4096,256]{1,0:T(8,128)(2,1)}, u32[]{:S(2)}, u32[]{:S(2)}) collective-permute-start(bf16[4096,256]{1,0:T(8,128)(2,1)} %own_ref.1), channel_id=1, source_target_pairs={{0,1},{1,0},{2,3},{3,2},{4,5},{5,4},{6,7},{7,6},{8,9},{9,8},{10,11... | collective-permute-start | bytes 6291464 | tf_op jit(solution)/shard_map/ppermute | solution.py:238
  1.1 1.7 %shard_map.85 = bf16[8,8,1152]{2,1,0:T(8,128)(2,1)} custom-call(bf16[8,4096]{1,0:T(8,128)(2,1)} %hidden_ref.1, bf16[32,128]{1,0:T(8,128)(2,1)} %bitcast.5, s32[8]{0:T(128)} %targets_ref.1, s32[8]{0:T(128)} %segments_ref.1, s32[8]{0:T(128)} %scored_ref.1), custom_call_target="tpu_custom_call" | custom-call | tf_op jit(solution)/shard_map/pallas_call | solution.py:239
  2.8 7.8 %all-to-all-start = ((bf16[8,8,1152]{2,1,0:T(8,128)(2,1)}), bf16[8,8,1152]{2,1,0:T(8,128)(2,1)S(1)}, u32[]{:S(2)}, u32[]{:S(2)}) async-start(bf16[8,8,1152]{2,1,0:T(8,128)(2,1)} %shard_map.85), calls=%async_computation | async-start | bytes 294912 | tf_op jit(solution)/shard_map/all_to_all | solution.py:250
  10.7 0.0 collective-permute-done.other_ref
  10.7 1.9 %shard_map.86 = (bf16[4096,256]{1,0:T(8,128)(2,1)S(1)}, bf16[2048,256]{1,0:T(8,128)(2,1)S(1)}, bf16[64,64]{1,0:T(8,128)(2,1)S(1)}) custom-call(bf16[4096,256]{1,0:T(8,128)(2,1)} %own_ref.1, bf16[4096,256]{1,0:T(8,128)(2,1)} %collective-permute-done.other_ref), custom_call_target="tpu_custom_call" | custom-call | bytes 6291456 | tf_op jit(solution)/shard_map/pallas_call | solution.py:253
  12.6 3.0 %all-to-all-done.rows_ref = bf16[8,8,1152]{2,1,0:T(8,128)(2,1)S(1)} async-done(((bf16[8,8,1152]{2,1,0:T(8,128)(2,1)}), bf16[8,8,1152]{2,1,0:T(8,128)(2,1)S(1)}, u32[]{:S(2)}, u32[]{:S(2)}) %all-to-all-start) | async-done | bytes 147488 | tf_op jit(solution)/shard_map/all_to_all | solution.py:250
  15.6 1.8 %shard_map.87 = (f32[1,128]{1,0:T(1,128)S(1)}, f32[8,128]{1,0:T(8,128)S(1)}) custom-call(bf16[8,8,1152]{2,1,0:T(8,128)(2,1)S(1)} %all-to-all-done.rows_ref, bf16[4096,256]{1,0:T(8,128)(2,1)S(1)} %get-tuple-element.8.own_ref, bf16[2048,256]{1,0:T(8,128)(2,1)S(1)} %get-tuple-element.9.upper_ref, bf16[64,64]{1,0:T(8,128)(2,1)S(1)} %get-tuple-element.10.order_ref, ...), custom_call_target="tpu_custom_call" | custom-call | tf_op jit(solution)/shard_map/pallas_call | solution.py:266
  17.4 0.1 collective-permute-start.1
  17.4 1.1 %collective-permute-done.1 = f32[1,128]{1,0:T(1,128)S(1)} collective-permute-done((f32[1,128]{1,0:T(1,128)S(1)}, f32[1,128]{1,0:T(1,128)S(1)}, u32[]{:S(2)}, u32[]{:S(2)}) %collective-permute-start.1) | collective-permute-done | bytes 544 | tf_op jit(solution)/shard_map/ppermute | solution.py:281
  18.6 9.8 %all_to_all.10 = f32[16,1,128]{2,1,0:T(1,128)S(1)} all-to-all(f32[16,1,128]{2,1,0:T(1,128)S(1)} %broadcast_in_dim.9), channel_id=1, replica_groups={{14,12,10,8,6,4,2,0,30,28,26,24,22,20,18,16},{15,13,11,9,7,5,3,1,31,29,..., dimensions={0} | all-to-all | bytes 16384 | tf_op jit(solution)/shard_map/all_to_all | solution.py:288
  28.4 0.7 %shard_map.88 = (f32[8]{0:T(128)}, f32[8]{0:T(128)}, f32[4]{0:T(128)}) custom-call(f32[16,128]{1,0:T(8,128)S(1)} %bitcast.4, f32[8,128]{1,0:T(8,128)S(1)} %get-tuple-element.12.meta_ref), custom_call_target="tpu_custom_call" | custom-call | tf_op jit(solution)/shard_map/pallas_call | solution.py:289
  (2 shorter events, 0.0 us)
Async XLA Ops:
  0.6 10.0 %collective-permute-start = (bf16[4096,256]{1,0:T(8,128)(2,1)}, bf16[4096,256]{1,0:T(8,128)(2,1)}, u32[]{:S(2)}, u32[]{:S(2)}) collective-permute-start(bf16[4096,256]{1,0:T(8,128)(2,1)} %own_ref.1), channel_id=1, source_target_pairs={{0,1},{1,0},{2,3},{3,2},{4,5},{5,4},{6,7},{7,6},{8,9},{9,8},{10,11... | collective-permute-start | bytes 6291464 | tf_op jit(solution)/shard_map/ppermute | solution.py:238
  2.8 12.7 %all-to-all-start = ((bf16[8,8,1152]{2,1,0:T(8,128)(2,1)}), bf16[8,8,1152]{2,1,0:T(8,128)(2,1)S(1)}, u32[]{:S(2)}, u32[]{:S(2)}) async-start(bf16[8,8,1152]{2,1,0:T(8,128)(2,1)} %shard_map.85), calls=%async_computation | async-start | bytes 294912 | tf_op jit(solution)/shard_map/all_to_all | solution.py:250
  17.4 1.2 %collective-permute-start.1 = (f32[1,128]{1,0:T(1,128)S(1)}, f32[1,128]{1,0:T(1,128)S(1)}, u32[]{:S(2)}, u32[]{:S(2)}) collective-permute-start(f32[1,128]{1,0:T(1,128)S(1)} %get-tuple-element.11), channel_id=1, source_target_pairs={{0,1},{1,0},{2,3},{3,2},{4,5},{5,4},{6,7},{7,6},{8,9},{9,8},{10,11... | collective-permute-start | bytes 1544 | tf_op jit(solution)/shard_map/ppermute | solution.py:281

commit v28 on v24

--- a/solution.py
+++ b/solution.py
@@ -32,11 +32,11 @@
 
 
 def members(count):
-    return [(5 * count // 8 + at) % count for at in range(count)]
+    return [(count // 2 + at) % count for at in range(count)]
 
 
 def own_slot(count):
-    at = lax.axis_index("req") - 5 * count // 8
+    at = lax.axis_index("req") - count // 2
     return jnp.where(at < 0, at + count, at)
 
 

time: 28.7 us -> 28.9 us (level)
  waiting for transfers between devices: 4.11 us -> 4.73 us
  starting transfers between devices: 8.44 us -> 8 us
    all_to_all x1, waiting for transfers between devices: 3 us -> 3.62 us  [local(): lax.all_to_all(packed, 'req', 0, 0, axis_index_groups=[members(groups)])]
    all_to_all x1, starting transfers between devices: 7.85 us -> 7.41 us  [local(): lax.all_to_all(packed, 'req', 0, 0, axis_index_groups=[members(groups)])]
where the time goes in v28:
time: 28.9 us; the launch traced here: 28.5 us
  blocking collectives  9.1 us (31%)
  starting transfers between devices  8 us (28%)
  Pallas kernels  6.04 us (21%)
  waiting for transfers between devices  4.73 us (16%)
  between operations  0.66 us (2%)
    all_to_all x1, blocking collectives, local(): lax.all_to_all(copies, ('req', 'tp'), 0, 0, axis_index_groups=listed)  9.1 us
    all_to_all x1, starting transfers between devices, local(): lax.all_to_all(packed, 'req', 0, 0, axis_index_groups=[members(groups)])  7.41 us
    all_to_all x1, waiting for transfers between devices, local(): lax.all_to_all(packed, 'req', 0, 0, axis_index_groups=[members(groups)])  3.62 us
    pallas_call x1, Pallas kernels, local(): pl.pallas_call(functools.partial(stage_kernel, share), out_shape=(VMEM(lm...  1.89 us
    pallas_call x1, Pallas kernels, local(): pl.pallas_call(score_kernel, out_shape=(jax.ShapeDtypeStruct((1, STATS *...  1.78 us
    pallas_call x1, Pallas kernels, local(): pl.pallas_call(functools.partial(pack_kernel, share), out_shape=VMEM((gro...  1.68 us
    ppermute x1, waiting for transfers between devices, local(): swapped = lax.ppermute(stats, 'tp', swap)  1.11 us
    pallas_call x1, Pallas kernels, local(): pl.pallas_call(functools.partial(finish_kernel, share), out_shape=(jax.Sh...  0.69 us
  transfers between devices with their start and end apart: 3, of which 2 were waited for; matrix products, arithmetic and copies ran while one was open for 0% of the time, Pallas kernels for 13%

profile of v28, /device:TPU:0, one launch (start us, length us, event | category | flops | bytes accessed | tf_op | source)
XLA Modules:
  0.0 28.5 jit_solution(8563364202941640258)
XLA Ops:
  0.6 0.5 %collective-permute-start = (bf16[4096,256]{1,0:T(8,128)(2,1)}, bf16[4096,256]{1,0:T(8,128)(2,1)}, u32[]{:S(2)}, u32[]{:S(2)}) collective-permute-start(bf16[4096,256]{1,0:T(8,128)(2,1)} %own_ref.1), channel_id=1, source_target_pairs={{0,1},{1,0},{2,3},{3,2},{4,5},{5,4},{6,7},{7,6},{8,9},{9,8},{10,11... | collective-permute-start | bytes 6291464 | tf_op jit(solution)/shard_map/ppermute | solution.py:238
  1.1 1.7 %shard_map.85 = bf16[8,8,1152]{2,1,0:T(8,128)(2,1)} custom-call(bf16[8,4096]{1,0:T(8,128)(2,1)} %hidden_ref.1, bf16[32,128]{1,0:T(8,128)(2,1)} %bitcast.5, s32[8]{0:T(128)} %targets_ref.1, s32[8]{0:T(128)} %segments_ref.1, s32[8]{0:T(128)} %scored_ref.1), custom_call_target="tpu_custom_call" | custom-call | tf_op jit(solution)/shard_map/pallas_call | solution.py:239
  2.8 7.4 %all-to-all-start = ((bf16[8,8,1152]{2,1,0:T(8,128)(2,1)}), bf16[8,8,1152]{2,1,0:T(8,128)(2,1)S(1)}, u32[]{:S(2)}, u32[]{:S(2)}) async-start(bf16[8,8,1152]{2,1,0:T(8,128)(2,1)} %shard_map.85), calls=%async_computation | async-start | bytes 294912 | tf_op jit(solution)/shard_map/all_to_all | solution.py:250
  10.2 0.0 collective-permute-done.other_ref
  10.2 1.9 %shard_map.86 = (bf16[4096,256]{1,0:T(8,128)(2,1)S(1)}, bf16[2048,256]{1,0:T(8,128)(2,1)S(1)}, bf16[64,64]{1,0:T(8,128)(2,1)S(1)}) custom-call(bf16[4096,256]{1,0:T(8,128)(2,1)} %own_ref.1, bf16[4096,256]{1,0:T(8,128)(2,1)} %collective-permute-done.other_ref), custom_call_target="tpu_custom_call" | custom-call | bytes 6291456 | tf_op jit(solution)/shard_map/pallas_call | solution.py:253
  12.1 3.6 %all-to-all-done.rows_ref = bf16[8,8,1152]{2,1,0:T(8,128)(2,1)S(1)} async-done(((bf16[8,8,1152]{2,1,0:T(8,128)(2,1)}), bf16[8,8,1152]{2,1,0:T(8,128)(2,1)S(1)}, u32[]{:S(2)}, u32[]{:S(2)}) %all-to-all-start) | async-done | bytes 147488 | tf_op jit(solution)/shard_map/all_to_all | solution.py:250
  15.8 1.8 %shard_map.87 = (f32[1,128]{1,0:T(1,128)S(1)}, f32[8,128]{1,0:T(8,128)S(1)}) custom-call(bf16[8,8,1152]{2,1,0:T(8,128)(2,1)S(1)} %all-to-all-done.rows_ref, bf16[4096,256]{1,0:T(8,128)(2,1)S(1)} %get-tuple-element.8.own_ref, bf16[2048,256]{1,0:T(8,128)(2,1)S(1)} %get-tuple-element.9.upper_ref, bf16[64,64]{1,0:T(8,128)(2,1)S(1)} %get-tuple-element.10.order_ref, ...), custom_call_target="tpu_custom_call" | custom-call | tf_op jit(solution)/shard_map/pallas_call | solution.py:266
  17.5 0.1 collective-permute-start.1
  17.6 1.1 %collective-permute-done.1 = f32[1,128]{1,0:T(1,128)S(1)} collective-permute-done((f32[1,128]{1,0:T(1,128)S(1)}, f32[1,128]{1,0:T(1,128)S(1)}, u32[]{:S(2)}, u32[]{:S(2)}) %collective-permute-start.1) | collective-permute-done | bytes 544 | tf_op jit(solution)/shard_map/ppermute | solution.py:281
  18.7 9.1 %all_to_all.10 = f32[16,1,128]{2,1,0:T(1,128)S(1)} all-to-all(f32[16,1,128]{2,1,0:T(1,128)S(1)} %broadcast_in_dim.9), channel_id=1, replica_groups={{30,28,26,24,22,20,18,16,14,12,10,8,6,4,2,0},{31,29,27,25,23,21,19,17,1..., dimensions={0} | all-to-all | bytes 16384 | tf_op jit(solution)/shard_map/all_to_all | solution.py:286
  27.8 0.7 %shard_map.88 = (f32[8]{0:T(128)}, f32[8]{0:T(128)}, f32[4]{0:T(128)}) custom-call(f32[16,128]{1,0:T(8,128)S(1)} %bitcast.4, f32[8,128]{1,0:T(8,128)S(1)} %get-tuple-element.12.meta_ref), custom_call_target="tpu_custom_call" | custom-call | tf_op jit(solution)/shard_map/pallas_call | solution.py:287
  (2 shorter events, 0.0 us)
Async XLA Ops:
  0.6 9.6 %collective-permute-start = (bf16[4096,256]{1,0:T(8,128)(2,1)}, bf16[4096,256]{1,0:T(8,128)(2,1)}, u32[]{:S(2)}, u32[]{:S(2)}) collective-permute-start(bf16[4096,256]{1,0:T(8,128)(2,1)} %own_ref.1), channel_id=1, source_target_pairs={{0,1},{1,0},{2,3},{3,2},{4,5},{5,4},{6,7},{7,6},{8,9},{9,8},{10,11... | collective-permute-start | bytes 6291464 | tf_op jit(solution)/shard_map/ppermute | solution.py:238
  2.8 12.9 %all-to-all-start = ((bf16[8,8,1152]{2,1,0:T(8,128)(2,1)}), bf16[8,8,1152]{2,1,0:T(8,128)(2,1)S(1)}, u32[]{:S(2)}, u32[]{:S(2)}) async-start(bf16[8,8,1152]{2,1,0:T(8,128)(2,1)} %shard_map.85), calls=%async_computation | async-start | bytes 294912 | tf_op jit(solution)/shard_map/all_to_all | solution.py:250
  17.5 1.2 %collective-permute-start.1 = (f32[1,128]{1,0:T(1,128)S(1)}, f32[1,128]{1,0:T(1,128)S(1)}, u32[]{:S(2)}, u32[]{:S(2)}) collective-permute-start(f32[1,128]{1,0:T(1,128)S(1)} %get-tuple-element.11), channel_id=1, source_target_pairs={{0,1},{1,0},{2,3},{3,2},{4,5},{5,4},{6,7},{7,6},{8,9},{9,8},{10,11... | collective-permute-start | bytes 1544 | tf_op jit(solution)/shard_map/ppermute | solution.py:281

commit v29 on v24

--- a/solution.py
+++ b/solution.py
@@ -208,16 +208,25 @@
     logprob = jnp.where(in_use, picked - log_norm, 0.0)
     entropy = jnp.where(in_use, log_norm - row_weighted / row_total, 0.0)
     segment, place = meta_ref[3:4, :].astype(jnp.int32), meta_ref[5:6, :].astype(jnp.int32)
-    mine = jnp.logical_and(place == sub, lane % share // MINE == own_slot(share // MINE))
-
-    def placed(values, wanted):
-        sums = jnp.sum(jnp.where(wanted, values, 0.0), axis=1, keepdims=True)
-        diagonal = iota((SUBS, LANES), 0) == iota((SUBS, LANES), 1)
-        return jnp.sum(jnp.where(diagonal, sums, 0.0), axis=0)
-
-    logprob_ref[...] = placed(logprob, mine)[:row_count]
-    entropy_ref[...] = placed(entropy, mine)[:row_count]
-    seq_ref[...] = placed(logprob, segment == sub)[:SEQS]
+    power = share.bit_length() - 1 if share & (share - 1) == 0 else None
+    in_share = lane % share if power is None else lane & (share - 1)
+    mine = jnp.logical_and(place == sub, in_share >> (MINE.bit_length() - 1) == own_slot(share // MINE))
+    stacked = jnp.concatenate(
+        [
+            jnp.where(mine, logprob, 0.0),
+            jnp.where(mine, entropy, 0.0),
+            jnp.where(segment == sub, logprob, 0.0),
+        ],
+        axis=0,
+    )
+    sums = jnp.sum(stacked, axis=1, keepdims=True)
+    diagonal = iota((SUBS, LANES), 0) == iota((SUBS, LANES), 1)
+    lines = [
+        jnp.sum(jnp.where(diagonal, sums[at * SUBS : (at + 1) * SUBS], 0.0), axis=0) for at in range(3)
+    ]
+    logprob_ref[...] = lines[0][:row_count]
+    entropy_ref[...] = lines[1][:row_count]
+    seq_ref[...] = lines[2][:SEQS]
 
 
 def grant(mebibytes):

time: 28.7 us -> 28.7 us (level)
  no operation moved by 1% of the time
where the time goes in v29:
time: 28.7 us; the launch traced here: 28.4 us
  blocking collectives  9.1 us (32%)
  starting transfers between devices  8.44 us (29%)
  Pallas kernels  6.04 us (21%)
  waiting for transfers between devices  4.11 us (14%)
  between operations  0.66 us (2%)
    all_to_all x1, blocking collectives, local(): lax.all_to_all(copies, ('req', 'tp'), 0, 0, axis_index_groups=listed)  9.1 us
    all_to_all x1, starting transfers between devices, local(): lax.all_to_all(packed, 'req', 0, 0, axis_index_groups=[members(groups)])  7.85 us
    all_to_all x1, waiting for transfers between devices, local(): lax.all_to_all(packed, 'req', 0, 0, axis_index_groups=[members(groups)])  3 us
    pallas_call x1, Pallas kernels, local(): pl.pallas_call(functools.partial(stage_kernel, share), out_shape=(VMEM(lm...  1.89 us
    pallas_call x1, Pallas kernels, local(): pl.pallas_call(score_kernel, out_shape=(jax.ShapeDtypeStruct((1, STATS *...  1.78 us
    pallas_call x1, Pallas kernels, local(): pl.pallas_call(functools.partial(pack_kernel, share), out_shape=VMEM((gro...  1.68 us
    ppermute x1, waiting for transfers between devices, local(): swapped = lax.ppermute(stats, 'tp', swap)  1.11 us
    pallas_call x1, Pallas kernels, local(): pl.pallas_call(functools.partial(finish_kernel, share), out_shape=(jax.Sh...  0.69 us
  transfers between devices with their start and end apart: 3, of which 2 were waited for; matrix products, arithmetic and copies ran while one was open for 0% of the time, Pallas kernels for 13%

profile of v29, /device:TPU:0, one launch (start us, length us, event | category | flops | bytes accessed | tf_op | source)
XLA Modules:
  0.0 28.4 jit_solution(8034520407458747524)
XLA Ops:
  0.6 0.5 %collective-permute-start = (bf16[4096,256]{1,0:T(8,128)(2,1)}, bf16[4096,256]{1,0:T(8,128)(2,1)}, u32[]{:S(2)}, u32[]{:S(2)}) collective-permute-start(bf16[4096,256]{1,0:T(8,128)(2,1)} %own_ref.1), channel_id=1, source_target_pairs={{0,1},{1,0},{2,3},{3,2},{4,5},{5,4},{6,7},{7,6},{8,9},{9,8},{10,11... | collective-permute-start | bytes 6291464 | tf_op jit(solution)/shard_map/ppermute | solution.py:247
  1.1 1.7 %shard_map.85 = bf16[8,8,1152]{2,1,0:T(8,128)(2,1)} custom-call(bf16[8,4096]{1,0:T(8,128)(2,1)} %hidden_ref.1, bf16[32,128]{1,0:T(8,128)(2,1)} %bitcast.5, s32[8]{0:T(128)} %targets_ref.1, s32[8]{0:T(128)} %segments_ref.1, s32[8]{0:T(128)} %scored_ref.1), custom_call_target="tpu_custom_call" | custom-call | tf_op jit(solution)/shard_map/pallas_call | solution.py:248
  2.8 7.8 %all-to-all-start = ((bf16[8,8,1152]{2,1,0:T(8,128)(2,1)}), bf16[8,8,1152]{2,1,0:T(8,128)(2,1)S(1)}, u32[]{:S(2)}, u32[]{:S(2)}) async-start(bf16[8,8,1152]{2,1,0:T(8,128)(2,1)} %shard_map.85), calls=%async_computation | async-start | bytes 294912 | tf_op jit(solution)/shard_map/all_to_all | solution.py:259
  10.7 0.0 collective-permute-done.other_ref
  10.7 1.9 %shard_map.86 = (bf16[4096,256]{1,0:T(8,128)(2,1)S(1)}, bf16[2048,256]{1,0:T(8,128)(2,1)S(1)}, bf16[64,64]{1,0:T(8,128)(2,1)S(1)}) custom-call(bf16[4096,256]{1,0:T(8,128)(2,1)} %own_ref.1, bf16[4096,256]{1,0:T(8,128)(2,1)} %collective-permute-done.other_ref), custom_call_target="tpu_custom_call" | custom-call | bytes 6291456 | tf_op jit(solution)/shard_map/pallas_call | solution.py:262
  12.6 3.0 %all-to-all-done.rows_ref = bf16[8,8,1152]{2,1,0:T(8,128)(2,1)S(1)} async-done(((bf16[8,8,1152]{2,1,0:T(8,128)(2,1)}), bf16[8,8,1152]{2,1,0:T(8,128)(2,1)S(1)}, u32[]{:S(2)}, u32[]{:S(2)}) %all-to-all-start) | async-done | bytes 147488 | tf_op jit(solution)/shard_map/all_to_all | solution.py:259
  15.6 1.8 %shard_map.87 = (f32[1,128]{1,0:T(1,128)S(1)}, f32[8,128]{1,0:T(8,128)S(1)}) custom-call(bf16[8,8,1152]{2,1,0:T(8,128)(2,1)S(1)} %all-to-all-done.rows_ref, bf16[4096,256]{1,0:T(8,128)(2,1)S(1)} %get-tuple-element.8.own_ref, bf16[2048,256]{1,0:T(8,128)(2,1)S(1)} %get-tuple-element.9.upper_ref, bf16[64,64]{1,0:T(8,128)(2,1)S(1)} %get-tuple-element.10.order_ref, ...), custom_call_target="tpu_custom_call" | custom-call | tf_op jit(solution)/shard_map/pallas_call | solution.py:275
  17.4 0.1 collective-permute-start.1
  17.4 1.1 %collective-permute-done.1 = f32[1,128]{1,0:T(1,128)S(1)} collective-permute-done((f32[1,128]{1,0:T(1,128)S(1)}, f32[1,128]{1,0:T(1,128)S(1)}, u32[]{:S(2)}, u32[]{:S(2)}) %collective-permute-start.1) | collective-permute-done | bytes 544 | tf_op jit(solution)/shard_map/ppermute | solution.py:290
  18.6 9.1 %all_to_all.10 = f32[16,1,128]{2,1,0:T(1,128)S(1)} all-to-all(f32[16,1,128]{2,1,0:T(1,128)S(1)} %broadcast_in_dim.9), channel_id=1, replica_groups={{30,28,26,24,22,20,18,16,14,12,10,8,6,4,2,0},{31,29,27,25,23,21,19,17,1..., dimensions={0} | all-to-all | bytes 16384 | tf_op jit(solution)/shard_map/all_to_all | solution.py:295
  27.7 0.7 %shard_map.88 = (f32[8]{0:T(128)}, f32[8]{0:T(128)}, f32[4]{0:T(128)}) custom-call(f32[16,128]{1,0:T(8,128)S(1)} %bitcast.4, f32[8,128]{1,0:T(8,128)S(1)} %get-tuple-element.12.meta_ref), custom_call_target="tpu_custom_call" | custom-call | tf_op jit(solution)/shard_map/pallas_call | solution.py:296
  (2 shorter events, 0.0 us)
Async XLA Ops:
  0.6 10.0 %collective-permute-start = (bf16[4096,256]{1,0:T(8,128)(2,1)}, bf16[4096,256]{1,0:T(8,128)(2,1)}, u32[]{:S(2)}, u32[]{:S(2)}) collective-permute-start(bf16[4096,256]{1,0:T(8,128)(2,1)} %own_ref.1), channel_id=1, source_target_pairs={{0,1},{1,0},{2,3},{3,2},{4,5},{5,4},{6,7},{7,6},{8,9},{9,8},{10,11... | collective-permute-start | bytes 6291464 | tf_op jit(solution)/shard_map/ppermute | solution.py:247
  2.8 12.7 %all-to-all-start = ((bf16[8,8,1152]{2,1,0:T(8,128)(2,1)}), bf16[8,8,1152]{2,1,0:T(8,128)(2,1)S(1)}, u32[]{:S(2)}, u32[]{:S(2)}) async-start(bf16[8,8,1152]{2,1,0:T(8,128)(2,1)} %shard_map.85), calls=%async_computation | async-start | bytes 294912 | tf_op jit(solution)/shard_map/all_to_all | solution.py:259
  17.4 1.2 %collective-permute-start.1 = (f32[1,128]{1,0:T(1,128)S(1)}, f32[1,128]{1,0:T(1,128)S(1)}, u32[]{:S(2)}, u32[]{:S(2)}) collective-permute-start(f32[1,128]{1,0:T(1,128)S(1)} %get-tuple-element.11), channel_id=1, source_target_pairs={{0,1},{1,0},{2,3},{3,2},{4,5},{5,4},{6,7},{7,6},{8,9},{9,8},{10,11... | collective-permute-start | bytes 1544 | tf_op jit(solution)/shard_map/ppermute | solution.py:290

commit v30 on v24

--- a/solution.py
+++ b/solution.py
@@ -150,13 +150,14 @@
         )
 
     def fetched(at, total):
-        return total + product(lower_ref, staged, at, (width - staged) // 2)
+        pltpu.make_async_copy(
+            other_ref.at[pl.ds(staged + at * depth, depth)], lower_ref.at[pl.ds(at * depth, depth)], sems.at[at]
+        ).wait()
+        return total + product(lower_ref, staged, at, depth)
 
     zeros = jnp.zeros((share, cols), jnp.float32)
     own_logits, other_logits = lax.fori_loop(0, 2, resident, (zeros, zeros))
-    for copy in copies:
-        copy.wait()
-    logits = jnp.concatenate([own_logits, lax.fori_loop(0, 2, fetched, other_logits)], axis=1)
+    logits = jnp.concatenate([own_logits, lax.fori_loop(0, sems.shape[0], fetched, other_logits)], axis=1)
     lanes = max(share, LANES)
     sub, lane = iota((share, lanes), 0), iota((share, lanes), 1)
     ids = meta[0:1, :lanes] + 256.0 * meta[1:2, :lanes] + 65536.0 * meta[2:3, :lanes]
@@ -274,7 +275,7 @@
         scratch_shapes=[
             VMEM((share, width), jnp.bfloat16),
             VMEM((width - staged, lm_head.shape[1]), jnp.bfloat16),
-            pltpu.SemaphoreType.DMA((4,)),
+            pltpu.SemaphoreType.DMA((2,)),
         ],
         compiler_params=grant(24),
     )(rows, *(pltpu.with_memory_space_constraint(part, VMEM) for part in slices), other)

time: 28.7 us -> 28.5 us (level)
  no operation moved by 1% of the time
where the time goes in v30:
time: 28.5 us; the launch traced here: 28.2 us
  blocking collectives  9.1 us (32%)
  starting transfers between devices  8.44 us (30%)
  Pallas kernels  5.88 us (21%)
  waiting for transfers between devices  4.11 us (14%)
  between operations  0.66 us (2%)
    all_to_all x1, blocking collectives, local(): lax.all_to_all(copies, ('req', 'tp'), 0, 0, axis_index_groups=listed)  9.1 us
    all_to_all x1, starting transfers between devices, local(): lax.all_to_all(packed, 'req', 0, 0, axis_index_groups=[members(groups)])  7.85 us
    all_to_all x1, waiting for transfers between devices, local(): lax.all_to_all(packed, 'req', 0, 0, axis_index_groups=[members(groups)])  3 us
    pallas_call x1, Pallas kernels, local(): pl.pallas_call(functools.partial(stage_kernel, share), out_shape=(VMEM(lm...  1.89 us
    pallas_call x1, Pallas kernels, local(): pl.pallas_call(functools.partial(pack_kernel, share), out_shape=VMEM((gro...  1.68 us
    pallas_call x1, Pallas kernels, local(): pl.pallas_call(score_kernel, out_shape=(jax.ShapeDtypeStruct((1, STATS *...  1.62 us
    ppermute x1, waiting for transfers between devices, local(): swapped = lax.ppermute(stats, 'tp', swap)  1.11 us
    pallas_call x1, Pallas kernels, local(): pl.pallas_call(functools.partial(finish_kernel, share), out_shape=(jax.Sh...  0.69 us
  transfers between devices with their start and end apart: 3, of which 2 were waited for; matrix products, arithmetic and copies ran while one was open for 0% of the time, Pallas kernels for 13%

profile of v30, /device:TPU:0, one launch (start us, length us, event | category | flops | bytes accessed | tf_op | source)
XLA Modules:
  0.0 28.2 jit_solution(4841433105306851765)
XLA Ops:
  0.6 0.5 %collective-permute-start = (bf16[4096,256]{1,0:T(8,128)(2,1)}, bf16[4096,256]{1,0:T(8,128)(2,1)}, u32[]{:S(2)}, u32[]{:S(2)}) collective-permute-start(bf16[4096,256]{1,0:T(8,128)(2,1)} %own_ref.1), channel_id=1, source_target_pairs={{0,1},{1,0},{2,3},{3,2},{4,5},{5,4},{6,7},{7,6},{8,9},{9,8},{10,11... | collective-permute-start | bytes 6291464 | tf_op jit(solution)/shard_map/ppermute | solution.py:239
  1.1 1.7 %shard_map.85 = bf16[8,8,1152]{2,1,0:T(8,128)(2,1)} custom-call(bf16[8,4096]{1,0:T(8,128)(2,1)} %hidden_ref.1, bf16[32,128]{1,0:T(8,128)(2,1)} %bitcast.5, s32[8]{0:T(128)} %targets_ref.1, s32[8]{0:T(128)} %segments_ref.1, s32[8]{0:T(128)} %scored_ref.1), custom_call_target="tpu_custom_call" | custom-call | tf_op jit(solution)/shard_map/pallas_call | solution.py:240
  2.8 7.8 %all-to-all-start = ((bf16[8,8,1152]{2,1,0:T(8,128)(2,1)}), bf16[8,8,1152]{2,1,0:T(8,128)(2,1)S(1)}, u32[]{:S(2)}, u32[]{:S(2)}) async-start(bf16[8,8,1152]{2,1,0:T(8,128)(2,1)} %shard_map.85), calls=%async_computation | async-start | bytes 294912 | tf_op jit(solution)/shard_map/all_to_all | solution.py:251
  10.7 0.0 collective-permute-done.other_ref
  10.7 1.9 %shard_map.86 = (bf16[4096,256]{1,0:T(8,128)(2,1)S(1)}, bf16[2048,256]{1,0:T(8,128)(2,1)S(1)}, bf16[64,64]{1,0:T(8,128)(2,1)S(1)}) custom-call(bf16[4096,256]{1,0:T(8,128)(2,1)} %own_ref.1, bf16[4096,256]{1,0:T(8,128)(2,1)} %collective-permute-done.other_ref), custom_call_target="tpu_custom_call" | custom-call | bytes 6291456 | tf_op jit(solution)/shard_map/pallas_call | solution.py:254
  12.6 3.0 %all-to-all-done.rows_ref = bf16[8,8,1152]{2,1,0:T(8,128)(2,1)S(1)} async-done(((bf16[8,8,1152]{2,1,0:T(8,128)(2,1)}), bf16[8,8,1152]{2,1,0:T(8,128)(2,1)S(1)}, u32[]{:S(2)}, u32[]{:S(2)}) %all-to-all-start) | async-done | bytes 147488 | tf_op jit(solution)/shard_map/all_to_all | solution.py:251
  15.6 1.6 %shard_map.87 = (f32[1,128]{1,0:T(1,128)S(1)}, f32[8,128]{1,0:T(8,128)S(1)}) custom-call(bf16[8,8,1152]{2,1,0:T(8,128)(2,1)S(1)} %all-to-all-done.rows_ref, bf16[4096,256]{1,0:T(8,128)(2,1)S(1)} %get-tuple-element.8.own_ref, bf16[2048,256]{1,0:T(8,128)(2,1)S(1)} %get-tuple-element.9.upper_ref, bf16[64,64]{1,0:T(8,128)(2,1)S(1)} %get-tuple-element.10.order_ref, ...), custom_call_target="tpu_custom_call" | custom-call | tf_op jit(solution)/shard_map/pallas_call | solution.py:267
  17.2 0.1 collective-permute-start.1
  17.3 1.1 %collective-permute-done.1 = f32[1,128]{1,0:T(1,128)S(1)} collective-permute-done((f32[1,128]{1,0:T(1,128)S(1)}, f32[1,128]{1,0:T(1,128)S(1)}, u32[]{:S(2)}, u32[]{:S(2)}) %collective-permute-start.1) | collective-permute-done | bytes 544 | tf_op jit(solution)/shard_map/ppermute | solution.py:282
  18.4 9.1 %all_to_all.10 = f32[16,1,128]{2,1,0:T(1,128)S(1)} all-to-all(f32[16,1,128]{2,1,0:T(1,128)S(1)} %broadcast_in_dim.9), channel_id=1, replica_groups={{30,28,26,24,22,20,18,16,14,12,10,8,6,4,2,0},{31,29,27,25,23,21,19,17,1..., dimensions={0} | all-to-all | bytes 16384 | tf_op jit(solution)/shard_map/all_to_all | solution.py:287
  27.5 0.7 %shard_map.88 = (f32[8]{0:T(128)}, f32[8]{0:T(128)}, f32[4]{0:T(128)}) custom-call(f32[16,128]{1,0:T(8,128)S(1)} %bitcast.4, f32[8,128]{1,0:T(8,128)S(1)} %get-tuple-element.12.meta_ref), custom_call_target="tpu_custom_call" | custom-call | tf_op jit(solution)/shard_map/pallas_call | solution.py:288
  (2 shorter events, 0.0 us)
Async XLA Ops:
  0.6 10.0 %collective-permute-start = (bf16[4096,256]{1,0:T(8,128)(2,1)}, bf16[4096,256]{1,0:T(8,128)(2,1)}, u32[]{:S(2)}, u32[]{:S(2)}) collective-permute-start(bf16[4096,256]{1,0:T(8,128)(2,1)} %own_ref.1), channel_id=1, source_target_pairs={{0,1},{1,0},{2,3},{3,2},{4,5},{5,4},{6,7},{7,6},{8,9},{9,8},{10,11... | collective-permute-start | bytes 6291464 | tf_op jit(solution)/shard_map/ppermute | solution.py:239
  2.8 12.7 %all-to-all-start = ((bf16[8,8,1152]{2,1,0:T(8,128)(2,1)}), bf16[8,8,1152]{2,1,0:T(8,128)(2,1)S(1)}, u32[]{:S(2)}, u32[]{:S(2)}) async-start(bf16[8,8,1152]{2,1,0:T(8,128)(2,1)} %shard_map.85), calls=%async_computation | async-start | bytes 294912 | tf_op jit(solution)/shard_map/all_to_all | solution.py:251
  17.2 1.2 %collective-permute-start.1 = (f32[1,128]{1,0:T(1,128)S(1)}, f32[1,128]{1,0:T(1,128)S(1)}, u32[]{:S(2)}, u32[]{:S(2)}) collective-permute-start(f32[1,128]{1,0:T(1,128)S(1)} %get-tuple-element.11), channel_id=1, source_target_pairs={{0,1},{1,0},{2,3},{3,2},{4,5},{5,4},{6,7},{7,6},{8,9},{9,8},{10,11... | collective-permute-start | bytes 1544 | tf_op jit(solution)/shard_map/ppermute | solution.py:282

commit v31 on v30

--- a/solution.py
+++ b/solution.py
@@ -113,14 +113,20 @@
     width, cols = own_ref.shape
     staged = upper_ref.shape[0]
     depth = lower_ref.shape[0] // sems.shape[0]
-    copies = [
-        pltpu.make_async_copy(
-            other_ref.at[pl.ds(staged + i * depth, depth)], lower_ref.at[pl.ds(i * depth, depth)], sems.at[i]
-        )
-        for i in range(sems.shape[0])
-    ]
-    for copy in copies:
-        copy.start()
+    part = depth // sems.shape[1]
+
+    def reads(at):
+        firsts = [at * depth + i * part for i in range(sems.shape[1])]
+        return [
+            pltpu.make_async_copy(
+                other_ref.at[pl.ds(staged + first, part)], lower_ref.at[pl.ds(first, part)], sems.at[at, i]
+            )
+            for i, first in enumerate(firsts)
+        ]
+
+    for at in range(sems.shape[0]):
+        for read in reads(at):
+            read.start()
     groups = rows_ref.shape[0]
     parts = SUBS // MINE
     span = width // parts
@@ -150,9 +156,8 @@
         )
 
     def fetched(at, total):
-        pltpu.make_async_copy(
-            other_ref.at[pl.ds(staged + at * depth, depth)], lower_ref.at[pl.ds(at * depth, depth)], sems.at[at]
-        ).wait()
+        for read in reads(at):
+            read.wait()
         return total + product(lower_ref, staged, at, depth)
 
     zeros = jnp.zeros((share, cols), jnp.float32)
@@ -275,7 +280,7 @@
         scratch_shapes=[
             VMEM((share, width), jnp.bfloat16),
             VMEM((width - staged, lm_head.shape[1]), jnp.bfloat16),
-            pltpu.SemaphoreType.DMA((2,)),
+            pltpu.SemaphoreType.DMA((2, 2)),
         ],
         compiler_params=grant(24),
     )(rows, *(pltpu.with_memory_space_constraint(part, VMEM) for part in slices), other)

time: 28.5 us -> 28.5 us (level)
  no operation moved by 1% of the time
where the time goes in v31:
time: 28.5 us; the launch traced here: 28.2 us
  blocking collectives  9.1 us (32%)
  starting transfers between devices  8.44 us (30%)
  Pallas kernels  5.88 us (21%)
  waiting for transfers between devices  4.11 us (14%)
  between operations  0.66 us (2%)
    all_to_all x1, blocking collectives, local(): lax.all_to_all(copies, ('req', 'tp'), 0, 0, axis_index_groups=listed)  9.1 us
    all_to_all x1, starting transfers between devices, local(): lax.all_to_all(packed, 'req', 0, 0, axis_index_groups=[members(groups)])  7.85 us
    all_to_all x1, waiting for transfers between devices, local(): lax.all_to_all(packed, 'req', 0, 0, axis_index_groups=[members(groups)])  3 us
    pallas_call x1, Pallas kernels, local(): pl.pallas_call(functools.partial(stage_kernel, share), out_shape=(VMEM(lm...  1.89 us
    pallas_call x1, Pallas kernels, local(): pl.pallas_call(functools.partial(pack_kernel, share), out_shape=VMEM((gro...  1.68 us
    pallas_call x1, Pallas kernels, local(): pl.pallas_call(score_kernel, out_shape=(jax.ShapeDtypeStruct((1, STATS *...  1.63 us
    ppermute x1, waiting for transfers between devices, local(): swapped = lax.ppermute(stats, 'tp', swap)  1.11 us
    pallas_call x1, Pallas kernels, local(): pl.pallas_call(functools.partial(finish_kernel, share), out_shape=(jax.Sh...  0.69 us
  transfers between devices with their start and end apart: 3, of which 2 were waited for; matrix products, arithmetic and copies ran while one was open for 0% of the time, Pallas kernels for 13%

profile of v31, /device:TPU:0, one launch (start us, length us, event | category | flops | bytes accessed | tf_op | source)
XLA Modules:
  0.0 28.2 jit_solution(2554085872360619237)
XLA Ops:
  0.6 0.5 %collective-permute-start = (bf16[4096,256]{1,0:T(8,128)(2,1)}, bf16[4096,256]{1,0:T(8,128)(2,1)}, u32[]{:S(2)}, u32[]{:S(2)}) collective-permute-start(bf16[4096,256]{1,0:T(8,128)(2,1)} %own_ref.1), channel_id=1, source_target_pairs={{0,1},{1,0},{2,3},{3,2},{4,5},{5,4},{6,7},{7,6},{8,9},{9,8},{10,11... | collective-permute-start | bytes 6291464 | tf_op jit(solution)/shard_map/ppermute | solution.py:244
  1.1 1.7 %shard_map.85 = bf16[8,8,1152]{2,1,0:T(8,128)(2,1)} custom-call(bf16[8,4096]{1,0:T(8,128)(2,1)} %hidden_ref.1, bf16[32,128]{1,0:T(8,128)(2,1)} %bitcast.5, s32[8]{0:T(128)} %targets_ref.1, s32[8]{0:T(128)} %segments_ref.1, s32[8]{0:T(128)} %scored_ref.1), custom_call_target="tpu_custom_call" | custom-call | tf_op jit(solution)/shard_map/pallas_call | solution.py:245
  2.8 7.8 %all-to-all-start = ((bf16[8,8,1152]{2,1,0:T(8,128)(2,1)}), bf16[8,8,1152]{2,1,0:T(8,128)(2,1)S(1)}, u32[]{:S(2)}, u32[]{:S(2)}) async-start(bf16[8,8,1152]{2,1,0:T(8,128)(2,1)} %shard_map.85), calls=%async_computation | async-start | bytes 294912 | tf_op jit(solution)/shard_map/all_to_all | solution.py:256
  10.7 0.0 collective-permute-done.other_ref
  10.7 1.9 %shard_map.86 = (bf16[4096,256]{1,0:T(8,128)(2,1)S(1)}, bf16[2048,256]{1,0:T(8,128)(2,1)S(1)}, bf16[64,64]{1,0:T(8,128)(2,1)S(1)}) custom-call(bf16[4096,256]{1,0:T(8,128)(2,1)} %own_ref.1, bf16[4096,256]{1,0:T(8,128)(2,1)} %collective-permute-done.other_ref), custom_call_target="tpu_custom_call" | custom-call | bytes 6291456 | tf_op jit(solution)/shard_map/pallas_call | solution.py:259
  12.6 3.0 %all-to-all-done.rows_ref = bf16[8,8,1152]{2,1,0:T(8,128)(2,1)S(1)} async-done(((bf16[8,8,1152]{2,1,0:T(8,128)(2,1)}), bf16[8,8,1152]{2,1,0:T(8,128)(2,1)S(1)}, u32[]{:S(2)}, u32[]{:S(2)}) %all-to-all-start) | async-done | bytes 147488 | tf_op jit(solution)/shard_map/all_to_all | solution.py:256
  15.6 1.6 %shard_map.87 = (f32[1,128]{1,0:T(1,128)S(1)}, f32[8,128]{1,0:T(8,128)S(1)}) custom-call(bf16[8,8,1152]{2,1,0:T(8,128)(2,1)S(1)} %all-to-all-done.rows_ref, bf16[4096,256]{1,0:T(8,128)(2,1)S(1)} %get-tuple-element.8.own_ref, bf16[2048,256]{1,0:T(8,128)(2,1)S(1)} %get-tuple-element.9.upper_ref, bf16[64,64]{1,0:T(8,128)(2,1)S(1)} %get-tuple-element.10.order_ref, ...), custom_call_target="tpu_custom_call" | custom-call | tf_op jit(solution)/shard_map/pallas_call | solution.py:272
  17.2 0.1 collective-permute-start.1
  17.3 1.1 %collective-permute-done.1 = f32[1,128]{1,0:T(1,128)S(1)} collective-permute-done((f32[1,128]{1,0:T(1,128)S(1)}, f32[1,128]{1,0:T(1,128)S(1)}, u32[]{:S(2)}, u32[]{:S(2)}) %collective-permute-start.1) | collective-permute-done | bytes 544 | tf_op jit(solution)/shard_map/ppermute | solution.py:287
  18.4 9.1 %all_to_all.10 = f32[16,1,128]{2,1,0:T(1,128)S(1)} all-to-all(f32[16,1,128]{2,1,0:T(1,128)S(1)} %broadcast_in_dim.9), channel_id=1, replica_groups={{30,28,26,24,22,20,18,16,14,12,10,8,6,4,2,0},{31,29,27,25,23,21,19,17,1..., dimensions={0} | all-to-all | bytes 16384 | tf_op jit(solution)/shard_map/all_to_all | solution.py:292
  27.5 0.7 %shard_map.88 = (f32[8]{0:T(128)}, f32[8]{0:T(128)}, f32[4]{0:T(128)}) custom-call(f32[16,128]{1,0:T(8,128)S(1)} %bitcast.4, f32[8,128]{1,0:T(8,128)S(1)} %get-tuple-element.12.meta_ref), custom_call_target="tpu_custom_call" | custom-call | tf_op jit(solution)/shard_map/pallas_call | solution.py:293
  (2 shorter events, 0.0 us)
Async XLA Ops:
  0.6 10.0 %collective-permute-start = (bf16[4096,256]{1,0:T(8,128)(2,1)}, bf16[4096,256]{1,0:T(8,128)(2,1)}, u32[]{:S(2)}, u32[]{:S(2)}) collective-permute-start(bf16[4096,256]{1,0:T(8,128)(2,1)} %own_ref.1), channel_id=1, source_target_pairs={{0,1},{1,0},{2,3},{3,2},{4,5},{5,4},{6,7},{7,6},{8,9},{9,8},{10,11... | collective-permute-start | bytes 6291464 | tf_op jit(solution)/shard_map/ppermute | solution.py:244
  2.8 12.7 %all-to-all-start = ((bf16[8,8,1152]{2,1,0:T(8,128)(2,1)}), bf16[8,8,1152]{2,1,0:T(8,128)(2,1)S(1)}, u32[]{:S(2)}, u32[]{:S(2)}) async-start(bf16[8,8,1152]{2,1,0:T(8,128)(2,1)} %shard_map.85), calls=%async_computation | async-start | bytes 294912 | tf_op jit(solution)/shard_map/all_to_all | solution.py:256
  17.2 1.2 %collective-permute-start.1 = (f32[1,128]{1,0:T(1,128)S(1)}, f32[1,128]{1,0:T(1,128)S(1)}, u32[]{:S(2)}, u32[]{:S(2)}) collective-permute-start(f32[1,128]{1,0:T(1,128)S(1)} %get-tuple-element.11), channel_id=1, source_target_pairs={{0,1},{1,0},{2,3},{3,2},{4,5},{5,4},{6,7},{7,6},{8,9},{9,8},{10,11... | collective-permute-start | bytes 1544 | tf_op jit(solution)/shard_map/ppermute | solution.py:287
